TPU v7x, 32 devices: a whole 2x2x4 slice. The times are simulated.
32 devices in a mesh: grp: 1, gx: 32 (over z, y, x, core), gy: 1.
Axes of the slice: x: 2, y: 2, z: 4, core: 2. Of those that a mesh axis runs over, the one named last changes fastest.
Arguments:
- incident: float32 [2, 16, 128, 128], P('grp', None, 'gx', 'gy'), may hold values from -6 to 6
- material: int32 [16, 128, 128], P('grp', 'gx', 'gy'), may hold values from 0 to 7
- contrast: float32 [8, 2], P('grp'), may hold values from 0.1 to 1.2
- w_first: bfloat16 [32, 4, 3, 3, 3], replicated, may hold values from -0.625 to 0.625
- w_middle: bfloat16 [32, 32, 3, 3, 3], replicated, may hold values from -0.21875 to 0.21875
- w_last: bfloat16 [2, 32, 3, 3, 3], replicated, may hold values from -0.21875 to 0.21875
- z_kernel: float32 [2, 16, 16], P('grp'), may hold values from -1 to 1
- spectral: float32 [2, 128, 128], P('grp', 'gx'), may hold values from -3 to 3
Outputs:
- total_field: float32 [2, 16, 128, 128], P('grp', None, 'gx', 'gy')
Inputs may be any that keep to these rules, and one draw needn't show every extreme that they name: `material`: selects a row of contrast.
All inputs are finite; a program needn't handle non-finite values.
Results may differ from a plain program's by a relative error of at most 0.0013.
Values may be sent and summed in bfloat16 or wider, within the bound.
No kernel may reach another device: no remote copies, remote signals or barrier semaphores. Data moves between devices by JAX's collectives and lax.ppermute only.
A program may use at most 64 MiB of HBM per device.

v0:
```python
import math

import jax
import jax.numpy as jnp
from jax import lax
from jax.sharding import PartitionSpec as P


def padded_2(x, sides, width):
    for axis, dim in sides:
        count, length = (lax.axis_size(axis), x.shape[dim])
        up = [(i, (i + 1) % count) for i in range(count)]
        down = [(j, i) for i, j in up]
        last = lax.slice_in_dim(x, length - width, length, axis=dim)
        leading = lax.slice_in_dim(x, 0, width, axis=dim)
        before = lax.ppermute(last, axis, up)
        after = lax.ppermute(leading, axis, down)
        x = jnp.concatenate([before, x, after], axis=dim)
    return x


def conv_layer(values, weights):
    return lax.conv_general_dilated(
        values[None],
        weights,
        (1, 1, 1),
        ((1, 1), (0, 0), (0, 0)),
        dimension_numbers=("NCDHW", "OIDHW", "NCDHW"),
        preferred_element_type=jnp.float32,
    )[0]


def activate(values):
    return jax.nn.gelu(values, approximate=False).astype(jnp.bfloat16)


def dft_tables(length):
    positions = jnp.arange(length, dtype=jnp.int32)
    product = positions[:, None] * positions[None, :] % length
    angle = product.astype(jnp.float32) * (2.0 * math.pi / length)
    return (jnp.cos(angle), jnp.sin(angle))


def green_apply(source, z_kernel, spectral):
    high = lax.Precision.HIGHEST
    kr, ki = (z_kernel[0], z_kernel[1])
    lre = jnp.einsum("zw,wxy->zxy", kr, source[0], precision=high) - jnp.einsum(
        "zw,wxy->zxy", ki, source[1], precision=high
    )
    lim = jnp.einsum("zw,wxy->zxy", kr, source[1], precision=high) + jnp.einsum(
        "zw,wxy->zxy", ki, source[0], precision=high
    )
    columns = lax.all_to_all(jnp.stack([lre, lim]), "gy", split_axis=1, concat_axis=3, tiled=True)
    count_y = columns.shape[3]
    cos_y, sin_y = dft_tables(count_y)
    fwd_re = jnp.dot(columns[0], cos_y, precision=high) + jnp.dot(columns[1], sin_y, precision=high)
    fwd_im = jnp.dot(columns[1], cos_y, precision=high) - jnp.dot(columns[0], sin_y, precision=high)
    count_x = columns.shape[2] * lax.axis_size("gx")
    cos_x, sin_x = dft_tables(count_x)
    piece = lax.all_to_all(
        jnp.stack([fwd_re, fwd_im]), "gx", split_axis=3, concat_axis=2, tiled=True
    )
    ar = jnp.einsum("zxk,xq->zkq", piece[0], cos_x, precision=high) + jnp.einsum(
        "zxk,xq->zkq", piece[1], sin_x, precision=high
    )
    ai = jnp.einsum("zxk,xq->zkq", piece[1], cos_x, precision=high) - jnp.einsum(
        "zxk,xq->zkq", piece[0], sin_x, precision=high
    )
    br = spectral[0] * ar - spectral[1] * ai
    bi = spectral[0] * ai + spectral[1] * ar
    gr = jnp.einsum("zkq,qx->zxk", br, cos_x, precision=high) - jnp.einsum(
        "zkq,qx->zxk", bi, sin_x, precision=high
    )
    gi = jnp.einsum("zkq,qx->zxk", bi, cos_x, precision=high) + jnp.einsum(
        "zkq,qx->zxk", br, sin_x, precision=high
    )
    spread = jnp.stack([gr, gi]) / count_x
    rows = lax.all_to_all(spread, "gx", split_axis=2, concat_axis=3, tiled=True)
    inv_re = jnp.dot(rows[0], cos_y, precision=high) - jnp.dot(rows[1], sin_y, precision=high)
    inv_im = jnp.dot(rows[1], cos_y, precision=high) + jnp.dot(rows[0], sin_y, precision=high)
    scattered = jnp.stack([inv_re, inv_im]) / count_y
    return lax.all_to_all(scattered, "gy", split_axis=3, concat_axis=1, tiled=True)


def per_device(incident, material, contrast, w_first, w_middle, w_last, z_kernel, spectral):
    high = lax.Precision.HIGHEST
    classes = contrast.shape[0]
    selector = (material[None] == jnp.arange(classes, dtype=jnp.int32)[:, None, None, None]).astype(
        jnp.float32
    )
    chi_re = jnp.einsum("k,kzxy->zxy", contrast[:, 0], selector, precision=high)
    chi_im = jnp.einsum("k,kzxy->zxy", contrast[:, 1], selector, precision=high)
    field = incident
    pol_re = chi_re * field[0] - chi_im * field[1]
    pol_im = chi_re * field[1] + chi_im * field[0]
    features = jnp.stack([field[0], field[1], pol_re, pol_im]).astype(jnp.bfloat16)
    padded = padded_2(features, (("gx", 2), ("gy", 3)), 3)
    hidden = activate(conv_layer(padded, w_first))
    hidden = activate(conv_layer(hidden, w_middle))
    correction = conv_layer(hidden, w_last)
    source = jnp.stack([pol_re, pol_im]) + correction
    field = incident + green_apply(source, z_kernel, spectral)
    return field


def solution(mesh):
    placed = (
        P("grp", None, "gx", "gy"),
        P("grp", "gx", "gy"),
        P("grp", None),
        P(),
        P(),
        P(),
        P("grp", None, None),
        P("grp", "gx", None),
    )
    return jax.shard_map(
        per_device,
        mesh=mesh,
        in_specs=placed,
        out_specs=P("grp", None, "gx", "gy"),
        check_vma=False,
    )
```

profile of v0, /device:TPU:0, one launch (start us, length us, event | category | flops | bytes accessed | tf_op | source)
XLA Modules:
  0.0 264.7 jit_solution(12250235178235497739)
XLA Ops:
  0.0 0.9 iota_compare_fusion.3
  0.9 0.9 fusion.60
  1.8 0.9 fusion.62
  2.8 0.8 copy.97
  3.6 0.9 convert.9
  5.8 6.0 %collective-permute-start.1 = (bf16[4,16,3,128]{3,2,1,0:T(4,128)(2,1)S(1)}, bf16[4,16,3,128]{3,2,1,0:T(4,128)(2,1)S(1)}, u32[]{:S(2)}, u32[]{:S(2)}) collective-permute-start(bf16[4,16,3,128]{3,2,1,0:T(4,128)(2,1)S(1)} %get-tuple-element.18), channel_id=1, source_target_pairs={{1,0},{2,1},{3,2},{4,3},{5,4},{6,5},{7,6},{8,7},{9,8},{10,9},{11,1... | collective-permute-start | bytes 147464 | tf_op jit(solution)/shard_map/ppermute | solution.py:17
  11.7 2.0 collective-permute-done
  14.1 0.8 maximum_bitcast_fusion
  15.0 1.1 reshape.36
  16.1 5.2 %copy.78 = bf16[4,16,10,1,8,17]{4,0,5,2,1,3:T(4,128)(2,1)} copy(bf16[4,16,10,1,8,17]{5,4,2,1,0,3:T(8,128)(2,1)S(1)} %reshape.36) | data formatting | bytes 348160 | tf_op jit(solution)/shard_map/conv_general_dilated | solution.py:23
  21.3 1.2 slice.99
  22.5 39.5 %select_bitcast_fusion = bf16[16,8,1,8,17,32]{5,3,4,1,0,2:T(8,128)(2,1)S(1)} fusion(pred[8,17]{0,1:T(8,128)(4,1)S(1)} %copy-done.9, bf16[32,4,3,3,3]{0,1,4,3,2:T(4,128)(2,1)S(1)} %copy-done.6, bf16[4,16,10,1,7,2]{4,0,5,2,1,3:T(4,128)(2,1)S(1)} %slice.99, bf16[4,16,10,1,8,17]{4,0,5,2,1,3:T(4,128)(2,1)} %copy.78), kind=kOutput, calls=%fused_computation.50 | convolution fusion | flops 153217024 | bytes 1313160 | tf_op jit(solution)/shard_map/conv_general_dilated | solution.py:23
  62.3 25.2 %select_bitcast_fusion.1 = bf16[16,6,1,8,17,32]{5,3,4,1,0,2:T(8,128)(2,1)S(1)} fusion(pred[8,17]{0,1:T(8,128)(4,1)S(1)} %copy-done.8, bf16[32,32,3,3,3]{1,0,4,3,2:T(8,128)(2,1)S(1)} %copy-done, bf16[16,8,1,7,2,32]{5,3,4,1,0,2:T(8,128)(2,1)S(1)} %slice.100, bf16[16,8,1,8,17,32]{5,3,4,1,0,2:T(8,128)(2,1)S(1)} %select_bitcast_fusion), kind=kOutput, calls=%fused_computation.54 | convolution fusion | flops 723173376 | bytes 2119816 | tf_op jit(solution)/shard_map/conv_general_dilated | solution.py:23
  87.7 137.1 %fusion.36 = f32[16,4,8,17,2]{2,4,3,1,0:T(2,128)S(1)} fusion(bf16[2,32,3,3,3]{1,0,4,3,2:T(2,128)(2,1)S(1)} %copy-done.7, bf16[16,6,1,7,2,32]{5,3,4,1,0,2:T(8,128)(2,1)S(1)} %slice.101, bf16[16,6,1,8,17,32]{5,3,4,1,0,2:T(8,128)(2,1)S(1)} %select_bitcast_fusion.1), kind=kOutput, calls=%fused_computation.53 | convolution fusion | flops 31629312 | bytes 994688 | tf_op jit(solution)/shard_map/conv_general_dilated | solution.py:23
  224.7 1.0 copy.112
  228.7 1.1 reshape.37
  229.7 5.7 %all-to-all-start = ((f32[32,1,512]{2,1,0:T(1,128)}), f32[32,1,512]{2,1,0:T(1,128)S(1)}, u32[]{:S(2)}, u32[]{:S(2)}) async-start(f32[32,1,512]{2,1,0:T(1,128)} %reshape.37), calls=%async_computation | async-start | bytes 131072 | tf_op jit(solution)/shard_map/all_to_all | solution.py:60
  235.4 7.4 %all-to-all-done = f32[32,1,512]{2,1,0:T(1,128)S(1)} async-done(((f32[32,1,512]{2,1,0:T(1,128)}), f32[32,1,512]{2,1,0:T(1,128)S(1)}, u32[]{:S(2)}, u32[]{:S(2)}) %all-to-all-start) | async-done | bytes 65568 | tf_op jit(solution)/shard_map/all_to_all | solution.py:60
  243.3 0.8 reduce
  247.0 0.6 convolution_add_fusion.2
  250.2 9.1 %all_to_all.30 = f32[32,1,512]{2,1,0:T(1,128)S(1)} all-to-all(f32[32,1,512]{2,1,0:T(1,128)S(1)} %reshape.39), channel_id=1, replica_groups=mesh['grp'=1,'gx'=32,'gy'=1] {'gx'}, dimensions={0} | all-to-all | bytes 131072 | tf_op jit(solution)/shard_map/all_to_all | solution.py:78
  259.3 0.8 reduce.1
  262.3 0.6 fusion.53
  263.7 0.7 copy.98
  (74 shorter events, 13.5 us)
Async XLA Ops:
  0.0 62.2 %copy-start = (bf16[32,32,3,3,3]{1,0,4,3,2:T(8,128)(2,1)S(1)}, bf16[32,32,3,3,3]{1,0,4,3,2:T(8,128)(2,1)}, u32[]{:S(2)}) copy-start(bf16[32,32,3,3,3]{1,0,4,3,2:T(8,128)(2,1)} %param.12) | copy-start | bytes 165892
  5.3 8.5 %collective-permute-start = (bf16[4,16,3,128]{3,2,1,0:T(4,128)(2,1)S(1)}, bf16[4,16,3,128]{3,2,1,0:T(4,128)(2,1)S(1)}, u32[]{:S(2)}, u32[]{:S(2)}) collective-permute-start(bf16[4,16,3,128]{3,2,1,0:T(4,128)(2,1)S(1)} %get-tuple-element.17), channel_id=1, source_target_pairs={{0,1},{1,2},{2,3},{3,4},{4,5},{5,6},{6,7},{7,8},{8,9},{9,10},{10,1... | collective-permute-start | bytes 147464 | tf_op jit(solution)/shard_map/ppermute | solution.py:16
  5.8 8.0 %collective-permute-start.1 = (bf16[4,16,3,128]{3,2,1,0:T(4,128)(2,1)S(1)}, bf16[4,16,3,128]{3,2,1,0:T(4,128)(2,1)S(1)}, u32[]{:S(2)}, u32[]{:S(2)}) collective-permute-start(bf16[4,16,3,128]{3,2,1,0:T(4,128)(2,1)S(1)} %get-tuple-element.18), channel_id=1, source_target_pairs={{1,0},{2,1},{3,2},{4,3},{5,4},{6,5},{7,6},{8,7},{9,8},{10,9},{11,1... | collective-permute-start | bytes 147464 | tf_op jit(solution)/shard_map/ppermute | solution.py:17
  14.1 8.5 %copy-start.6 = (bf16[32,4,3,3,3]{0,1,4,3,2:T(4,128)(2,1)S(1)}, bf16[32,4,3,3,3]{0,1,4,3,2:T(4,128)(2,1)}, u32[]{:S(2)}) copy-start(bf16[32,4,3,3,3]{0,1,4,3,2:T(4,128)(2,1)} %param.11) | copy-start | bytes 20740
  14.1 8.4 %copy-start.9 = (pred[8,17]{0,1:T(8,128)(4,1)S(1)}, pred[8,17]{0,1:T(8,128)(4,1)}, u32[]{:S(2)}) copy-start(pred[8,17]{0,1:T(8,128)(4,1)} %constant.30) | copy-start | bytes 412
  14.1 0.1 collective-permute-start.2
  22.5 39.7 %copy-start.8 = (pred[8,17]{0,1:T(8,128)(4,1)S(1)}, pred[8,17]{0,1:T(8,128)(4,1)}, u32[]{:S(2)}) copy-start(pred[8,17]{0,1:T(8,128)(4,1)} %constant.29) | copy-start | bytes 412
  62.2 25.4 %copy-start.7 = (bf16[2,32,3,3,3]{1,0,4,3,2:T(2,128)(2,1)S(1)}, bf16[2,32,3,3,3]{1,0,4,3,2:T(2,128)(2,1)}, u32[]{:S(2)}) copy-start(bf16[2,32,3,3,3]{1,0,4,3,2:T(2,128)(2,1)} %param.13) | copy-start | bytes 10372
  87.6 138.3 %copy-start.2 = (f32[1,16,4,128]{3,1,2,0:T(8,128)S(1)}, f32[1,16,4,128]{3,1,2,0:T(8,128)}, u32[]{:S(2)}) copy-start(f32[1,16,4,128]{3,1,2,0:T(8,128)} %get-tuple-element.6) | copy-start | bytes 98308
  87.6 138.3 %copy-start.3 = (f32[1,16,4,128]{3,1,2,0:T(8,128)S(1)}, f32[1,16,4,128]{3,1,2,0:T(8,128)}, u32[]{:S(2)}) copy-start(f32[1,16,4,128]{3,1,2,0:T(8,128)} %get-tuple-element.16) | copy-start | bytes 98308
  87.6 138.3 %copy-start.4 = (f32[2,16,16]{2,1,0:T(8,128)S(1)}, f32[2,16,16]{2,1,0:T(8,128)}, u32[]{:S(2)}) copy-start(f32[2,16,16]{2,1,0:T(8,128)} %param.14) | copy-start | bytes 6148
  224.7 10.7 %copy-start.5 = (f32[2,4,128]{2,1,0:T(4,128)S(1)}, f32[2,4,128]{2,1,0:T(4,128)}, u32[]{:S(2)}) copy-start(f32[2,4,128]{2,1,0:T(4,128)} %param.15) | copy-start | bytes 12292
  229.7 13.1 %all-to-all-start = ((f32[32,1,512]{2,1,0:T(1,128)}), f32[32,1,512]{2,1,0:T(1,128)S(1)}, u32[]{:S(2)}, u32[]{:S(2)}) async-start(f32[32,1,512]{2,1,0:T(1,128)} %reshape.37), calls=%async_computation | async-start | bytes 131072 | tf_op jit(solution)/shard_map/all_to_all | solution.py:60
  245.7 18.0 %copy-start.1 = (f32[2,16,4,128]{3,2,1,0:T(4,128)S(1)}, f32[2,16,4,128]{3,2,1,0:T(4,128)}, u32[]{:S(2)}) copy-start(f32[2,16,4,128]{3,2,1,0:T(4,128)} %param.8) | copy-start | bytes 196612
  (1 other events, 0.0 us)
where the time goes:
time: 268 us; the launch traced here: 265 us
  matrix products  213 us (79%)
  local copies, waits for them, and re-layouts  15 us (6%)
  starting transfers between devices  12.2 us (5%)
  waiting for transfers between devices  9.39 us (4%)
  blocking collectives  9.1 us (3%)
  other arithmetic  5 us (2%)
    conv_general_dilated x3, matrix products, conv_layer(): lax.conv_general_dilated(values[None], weights, (1, 1, 1), ((1, 1), (0, 0...  202 us
    all_to_all x1, blocking collectives, green_apply(): rows = lax.all_to_all(spread, 'gx', split_axis=2, concat_axis=3, tiled=True)  9.1 us
    conv_general_dilated x5, local copies, waits for them, and re-layouts, conv_layer(): lax.conv_general_dilated(values[None], weights, (1, 1, 1), ((1, 1), (0, 0...  8.62 us
    all_to_all x1, waiting for transfers between devices, green_apply(): lax.all_to_all(jnp.stack([fwd_re, fwd_im]), 'gx', split_axis=3, concat_ax...  7.39 us
    ppermute x2, starting transfers between devices, padded_2(): after = lax.ppermute(leading, axis, down)  6 us
    all_to_all x1, starting transfers between devices, green_apply(): lax.all_to_all(jnp.stack([fwd_re, fwd_im]), 'gx', split_axis=3, concat_ax...  5.65 us
  transfers between devices with their start and end apart: 5, of which 2 were waited for; matrix products, arithmetic and copies ran while one was open for 0% of the time, Pallas kernels for 0%

commit v1 on v0

--- a/solution.py
+++ b/solution.py
@@ -1,9 +1,18 @@
+import functools
 import math
 
 import jax
 import jax.numpy as jnp
+import ml_dtypes
+import numpy as np
 from jax import lax
+from jax.experimental import pallas as pl
+from jax.experimental.pallas import tpu as pltpu
 from jax.sharding import PartitionSpec as P
+
+F32 = jnp.float32
+BF16 = jnp.bfloat16
+VMEM_LIMIT = 48 * 1024 * 1024
 
 
 def padded_2(x, sides, width):
@@ -82,7 +91,7 @@
     return lax.all_to_all(scattered, "gy", split_axis=3, concat_axis=1, tiled=True)
 
 
-def per_device(incident, material, contrast, w_first, w_middle, w_last, z_kernel, spectral):
+def general_device(incident, material, contrast, w_first, w_middle, w_last, z_kernel, spectral):
     high = lax.Precision.HIGHEST
     classes = contrast.shape[0]
     selector = (material[None] == jnp.arange(classes, dtype=jnp.int32)[:, None, None, None]).astype(
@@ -103,6 +112,330 @@
     return field
 
 
+def split(values):
+    high = values.astype(BF16)
+    low = (values - high.astype(F32)).astype(BF16)
+    return high, low
+
+
+def split_np(values):
+    high = values.astype(ml_dtypes.bfloat16)
+    low = (values - high.astype(np.float64)).astype(ml_dtypes.bfloat16)
+    return high, low
+
+
+def angles(rows, cols, length):
+    product = (np.asarray(rows)[:, None] * np.asarray(cols)[None, :]) % length
+    angle = product.astype(np.float64) * (2.0 * math.pi / length)
+    return np.cos(angle), np.sin(angle)
+
+
+def left_table(rows, cols, length, scale=1.0):
+    high, low = split_np(np.concatenate(angles(rows, cols, length), axis=1) * scale)
+    return np.concatenate([high, high, low], axis=1)
+
+
+def right_table(rows, cols, length):
+    high, low = split_np(np.concatenate(angles(rows, cols, length), axis=0))
+    return np.concatenate([high, high, low], axis=0)
+
+
+def left_split(values):
+    high, low = split(values)
+    return jnp.concatenate([high, low, high], axis=1)
+
+
+def right_split(values):
+    high, low = split(values)
+    return jnp.concatenate([high, low, high], axis=0)
+
+
+def mm(a, b):
+    return jnp.dot(a, b, preferred_element_type=F32)
+
+
+def iota(shape, dim):
+    return lax.broadcasted_iota(jnp.int32, shape, dim)
+
+
+def other_part(values, nz, sign):
+    lanes = values.shape[1]
+    real = (iota(values.shape, 1) // nz) % 2 == 0
+    ahead = pltpu.roll(values, lanes - nz, 1)
+    behind = pltpu.roll(values, nz, 1)
+    return jnp.where(real, sign * ahead, -sign * behind)
+
+
+def swap_blocks(ref, count):
+    pieces = [ref[:, q, :] for q in range(count)]
+    lanes = pieces[0].shape[1]
+    inner = lanes // count
+    block = iota(pieces[0].shape, 1) // inner
+    rows = []
+    for x in range(count):
+        total = None
+        for q in range(count):
+            shift = ((q - x) * inner) % lanes
+            moved = pltpu.roll(pieces[q], shift, 1) if shift else pieces[q]
+            total = moved if total is None else jnp.where(block == q, moved, total)
+        rows.append(total)
+    return jnp.concatenate(rows, axis=0)
+
+
+def prepare_kernel(nz, hid, w1_ref, w2_ref, w3_ref, zk_ref, sp_ref, t1_ref, t2_ref, t3_ref, z_ref, sr_ref, si_ref):
+    taps, cols = w1_ref.shape[1], t1_ref.shape[1]
+    pick = (iota((taps, cols), 0) == iota((taps, cols), 1) // nz).astype(BF16)
+    spread = [
+        lax.dot_general(w1_ref[a], pick, (((0,), (0,)), ((), ())), preferred_element_type=F32)
+        for a in range(3)
+    ]
+    place = iota((hid, cols), 1) % nz
+    for z in range(nz):
+        rows = jnp.zeros((hid, cols), F32)
+        for a in range(3):
+            rows = jnp.where(place == z + a - 1, spread[a], rows)
+        t1_ref[z * hid : (z + 1) * hid, :] = rows.astype(BF16)
+    half = nz // 2
+    wide = half * hid
+    pick = (iota((hid, wide), 0) == iota((hid, wide), 1) % hid).astype(BF16)
+    place = iota((hid, wide), 1) // hid
+    for b in range(3):
+        for d in range(3):
+            spread = [mm(w2_ref[a, b, d], pick) for a in range(3)]
+            for r in range(half + 2):
+                rows = jnp.zeros((hid, wide), F32)
+                for a in range(3):
+                    rows = jnp.where(place == r + a - 2, spread[a], rows)
+                t2_ref[d, r * hid : (r + 1) * hid, b * wide : (b + 1) * wide] = rows.astype(BF16)
+    rows3, cols3 = t3_ref.shape
+    taps = w3_ref.shape[1]
+    repeat = (iota((rows3, taps), 0) // nz == iota((rows3, taps), 1)).astype(BF16)
+    pick = (iota((hid, cols3), 0) == iota((hid, cols3), 1) % hid).astype(BF16)
+    offset = iota((rows3, cols3), 1) // hid - iota((rows3, cols3), 0) % nz
+    total = jnp.zeros((rows3, cols3), F32)
+    for a in range(3):
+        spread = mm(mm(repeat, w3_ref[a]).astype(BF16), pick)
+        total = jnp.where(offset == a - 1, spread, total)
+    t3_ref[...] = total.astype(BF16)
+    kr, ki = zk_ref[0], zk_ref[1]
+    top = jnp.concatenate([kr, -ki], axis=1)
+    bottom = jnp.concatenate([ki, kr], axis=1)
+    high, low = split(jnp.concatenate([top, bottom, bottom, -top], axis=0))
+    z_ref[...] = jnp.concatenate([high, high, low], axis=1)
+    count, lanes = sp_ref.shape[1], sr_ref.shape[1]
+    pick = (iota((count, lanes), 0) == iota((count, lanes), 1) // (lanes // count)).astype(F32)
+    for part, ref in ((0, sr_ref), (1, si_ref)):
+        ref[...] = lax.dot_general(
+            sp_ref[part],
+            pick,
+            (((0,), (0,)), ((), ())),
+            precision=lax.Precision.HIGHEST,
+            preferred_element_type=F32,
+        )
+
+
+def polarised(inc_ref, mat_ref, con_ref, x):
+    re, im, cells = inc_ref[0, :, x, :], inc_ref[1, :, x, :], mat_ref[:, x, :]
+    chi_re = jnp.zeros_like(re)
+    chi_im = jnp.zeros_like(re)
+    for k in range(con_ref.shape[0]):
+        here = cells == k
+        chi_re = jnp.where(here, con_ref[k, 0], chi_re)
+        chi_im = jnp.where(here, con_ref[k, 1], chi_im)
+    return re, im, chi_re * re - chi_im * im, chi_re * im + chi_im * re
+
+
+def gelu(values):
+    return 0.5 * values * (1.0 + lax.erf(values * math.sqrt(0.5)))
+
+
+def corrector_kernel(
+    con_ref, left_ref, inc_ref, right_ref, mleft_ref, mat_ref, mright_ref, t1_ref, t2_ref, t3_ref,
+    z_ref, dft_ref, out_ref, feat, hid1, hid2,
+):
+    xl, ny = inc_ref.shape[2], inc_ref.shape[3]
+    nz = inc_ref.shape[1]
+    columns = [(left_ref, mleft_ref, x) for x in range(xl - 3, xl)]
+    columns += [(inc_ref, mat_ref, x) for x in range(xl)]
+    columns += [(right_ref, mright_ref, x) for x in range(3)]
+    own = []
+    deep = 12 * nz
+    for place, (field, cells, x) in enumerate(columns):
+        re, im, pol_re, pol_im = polarised(field, cells, con_ref, x)
+        if field is inc_ref:
+            own.append(jnp.concatenate([pol_re, pol_im], axis=0))
+        stack = jnp.concatenate([re, im, pol_re, pol_im], axis=0)
+        rolled = [pltpu.roll(stack, 1, 1), stack, pltpu.roll(stack, ny - 1, 1)]
+        feat[place * deep : (place + 1) * deep, :] = jnp.concatenate(rolled, axis=0).astype(BF16)
+    for j in range(0, xl + 4, 2):
+        window = [feat[(j + i) * deep : (j + i + 3) * deep, :] for i in range(2)]
+        made = mm(t1_ref[...], jnp.concatenate(window, axis=1))
+        hid1[:, j * ny : (j + 2) * ny] = gelu(made).astype(BF16)
+    rows, half = hid1.shape[0], hid1.shape[0] // 2
+    hid = rows // nz
+    tall = half + hid
+    for j in range(0, xl + 2, 2):
+        sums = []
+        for part, first in ((0, hid), (1, 0)):
+            taps = jnp.concatenate([t2_ref[d, first : first + tall, :] for d in range(3)], axis=0)
+            window = [
+                hid1[part * half : (part + 1) * half, (j + b) * ny : (j + b + 2) * ny] for b in range(3)
+            ]
+            made = mm(taps, jnp.concatenate(window, axis=0))
+            sides = []
+            for i in range(2):
+                lanes = slice(i * ny, (i + 1) * ny)
+                sides.append(
+                    pltpu.roll(made[:tall, lanes], 1, 1)
+                    + made[tall : 2 * tall, lanes]
+                    + pltpu.roll(made[2 * tall :, lanes], ny - 1, 1)
+                )
+            sums.append(jnp.concatenate(sides, axis=1))
+        low, high = sums
+        middle = low[half - hid :] + high[: 2 * hid]
+        total = jnp.concatenate([low[: half - hid], middle, high[2 * hid :]], axis=0)
+        hid2[:, j * ny : (j + 2) * ny] = gelu(total).astype(BF16)
+    made = mm(t3_ref[...], hid2[...])
+    deep = 2 * nz
+    sources = []
+    for x in range(xl):
+        parts = []
+        for d in range(3):
+            total = None
+            for b in range(3):
+                first = (b * 3 + d) * deep
+                piece = made[first : first + deep, (x + b) * ny : (x + b + 1) * ny]
+                total = piece if total is None else total + piece
+            parts.append(total)
+        correction = pltpu.roll(parts[0], 1, 1) + parts[1] + pltpu.roll(parts[2], ny - 1, 1)
+        sources.append(own[x] + correction)
+    lifted = mm(z_ref[...], right_split(jnp.concatenate(sources, axis=1)))
+    plain = [lifted[:deep, x * ny : (x + 1) * ny] for x in range(xl)]
+    turned = [lifted[deep:, x * ny : (x + 1) * ny] for x in range(xl)]
+    both = jnp.concatenate([jnp.concatenate(plain, axis=0), jnp.concatenate(turned, axis=0)], axis=1)
+    spectrum = mm(left_split(both), dft_ref[...])
+    out_ref[...] = jnp.transpose(spectrum).reshape(out_ref.shape)
+
+
+def spectral_kernel(nz, in_ref, fwd_ref, inv_ref, sr_ref, si_ref, out_ref):
+    values = swap_blocks(in_ref, in_ref.shape[1])
+    both = jnp.concatenate([values, other_part(values, nz, 1.0)], axis=0)
+    spectrum = mm(fwd_ref[...], right_split(both))
+    scaled = sr_ref[...] * spectrum + si_ref[...] * other_part(spectrum, nz, -1.0)
+    both = jnp.concatenate([scaled, other_part(scaled, nz, -1.0)], axis=0)
+    out_ref[...] = mm(inv_ref[...], right_split(both)).reshape(out_ref.shape)
+
+
+def finish_kernel(nz, in_ref, tab_ref, inc_ref, out_ref):
+    values = swap_blocks(in_ref, in_ref.shape[1])
+    both = jnp.concatenate([values, other_part(values, nz, -1.0)], axis=0)
+    field = jnp.transpose(mm(tab_ref[...], right_split(both)))
+    for x in range(inc_ref.shape[2]):
+        for part in range(2):
+            first = (2 * x + part) * nz
+            out_ref[part, :, x, :] = inc_ref[part, :, x, :] + field[first : first + nz, :]
+
+
+def call(kernel, out_shapes, args, scratch=(), smem=(), flops=0):
+    vmem = pl.BlockSpec(memory_space=pltpu.VMEM)
+    specs = [pl.BlockSpec(memory_space=pltpu.SMEM) if i in smem else vmem for i in range(len(args))]
+    single = not isinstance(out_shapes, list)
+    return pl.pallas_call(
+        kernel,
+        out_shape=out_shapes,
+        in_specs=specs,
+        out_specs=vmem if single else [vmem] * len(out_shapes),
+        scratch_shapes=scratch,
+        compiler_params=pltpu.CompilerParams(vmem_limit_bytes=VMEM_LIMIT),
+        cost_estimate=pl.CostEstimate(flops=flops, bytes_accessed=4 * 1024 * 1024, transcendentals=0),
+    )(*args)
+
+
+def lane_device(incident, material, contrast, w_first, w_middle, w_last, z_kernel, spectral):
+    count = lax.axis_size("gx")
+    nz, xl, ny = material.shape
+    hid = w_middle.shape[0]
+    ql, nx = spectral.shape[1], spectral.shape[2]
+    struct = jax.ShapeDtypeStruct
+    up = [(i, (i + 1) % count) for i in range(count)]
+    down = [(j, i) for i, j in up]
+    left, right = lax.ppermute(incident, "gx", up), lax.ppermute(incident, "gx", down)
+    mleft, mright = lax.ppermute(material, "gx", up), lax.ppermute(material, "gx", down)
+    t1, t2, t3, zmat, sr, si = call(
+        functools.partial(prepare_kernel, nz, hid),
+        [
+            struct((nz * hid, 36 * nz), BF16),
+            struct((3, (nz // 2 + 2) * hid, 3 * nz // 2 * hid), BF16),
+            struct((18 * nz, nz * hid), BF16),
+            struct((4 * nz, 6 * nz), BF16),
+            struct((nx, ql * 2 * nz), F32),
+            struct((nx, ql * 2 * nz), F32),
+        ],
+        (
+            jnp.transpose(w_first, (2, 3, 4, 1, 0)).reshape(3, 36, hid),
+            jnp.transpose(w_middle, (2, 3, 4, 0, 1)),
+            jnp.transpose(w_last, (2, 3, 4, 0, 1)).reshape(3, 18, hid),
+            z_kernel,
+            spectral,
+        ),
+        flops=10**9,
+    )
+    alternate = [xl * s + x for x in range(xl) for s in range(count)]
+    natural = list(range(nx))
+    lanes = 2 * nz * xl
+    spectrum = call(
+        corrector_kernel,
+        struct((count, ql, lanes), F32),
+        (
+            contrast, left, incident, right, mleft, material, mright, t1, t2, t3, zmat,
+            right_table(range(ny), range(ny), ny),
+        ),
+        scratch=[
+            pltpu.VMEM(((xl + 6) * 12 * nz, ny), BF16),
+            pltpu.VMEM((nz * hid, (xl + 4) * ny), BF16),
+            pltpu.VMEM((nz * hid, (xl + 2) * ny), BF16),
+        ],
+        smem=(0,),
+        flops=10**9,
+    )
+    piece = lax.all_to_all(spectrum, "gx", 0, 0, tiled=True)
+    spread = call(
+        functools.partial(spectral_kernel, nz),
+        struct((count, xl, lanes), F32),
+        (
+            piece,
+            left_table(natural, alternate, nx),
+            left_table(natural, natural, nx, 1.0 / (nx * ny)),
+            sr,
+            si,
+        ),
+        flops=10**8,
+    )
+    rows = lax.all_to_all(spread, "gx", 0, 0, tiled=True)
+    return call(
+        functools.partial(finish_kernel, nz),
+        struct(incident.shape, F32),
+        (rows, left_table(natural, alternate, ny), incident),
+        flops=10**8,
+    )
+
+
+def per_device(incident, material, contrast, w_first, w_middle, w_last, z_kernel, spectral):
+    nz, xl, ny = material.shape
+    ql, nx = spectral.shape[1], spectral.shape[2]
+    lanes = (
+        lax.axis_size("gy") == 1
+        and ny == 128
+        and nx == 128
+        and xl == 4
+        and ql == 4
+        and 2 * nz * xl == 128
+        and w_middle.shape[0] == 32
+    )
+    device = lane_device if lanes else general_device
+    return device(incident, material, contrast, w_first, w_middle, w_last, z_kernel, spectral)
+
+
 def solution(mesh):
     placed = (
         P("grp", None, "gx", "gy"),

time: 268 us -> 42.5 us (0.16); the launches traced: 265 us -> 42.1 us
  matrix products: 213 us -> 0 us
  local copies, waits for them, and re-layouts: 15 us -> 3.96 us
  blocking collectives: 9.1 us -> 20.1 us
  Pallas kernels: 0 us -> 8.93 us
  waiting for transfers between devices: 9.39 us -> 1.97 us
  starting transfers between devices: 12.2 us -> 7.05 us
  other arithmetic: 5 us -> 0 us
    conv_general_dilated x3 -> x0, matrix products: 202 us -> none  [conv_layer(): lax.conv_general_dilated(values[None], weights, (1, 1, 1), ((1, 1), (0, 0...]
    dot_general x22 -> x0, matrix products: 11.2 us -> none  [the longest x1 0.94 us: per_device(): chi_im = jnp.einsum('k,kzxy->zxy', contrast[:, 1], selector, precision=high)]
    all_to_all x1 -> x2, blocking collectives: 9.1 us -> 20.1 us  [the longest x1 11 us: lane_device(): piece = lax.all_to_all(spectrum, 'gx', 0, 0, tiled=True)]
    pallas_call x0 -> x4, Pallas kernels: none -> 8.93 us  [call(): pl.pallas_call(kernel, out_shape=out_shapes, in_specs=specs, out_specs=vm...]
    conv_general_dilated x5 -> x0, local copies, waits for them, and re-layouts: 8.62 us -> none  [conv_layer(): lax.conv_general_dilated(values[None], weights, (1, 1, 1), ((1, 1), (0, 0...]
    all_to_all x1 -> x0, waiting for transfers between devices: 7.39 us -> none  [green_apply(): lax.all_to_all(jnp.stack([fwd_re, fwd_im]), 'gx', split_axis=3, concat_ax...]
    all_to_all x1 -> x0, starting transfers between devices: 5.65 us -> none  [green_apply(): lax.all_to_all(jnp.stack([fwd_re, fwd_im]), 'gx', split_axis=3, concat_ax...]
  transfers between devices with their start and end apart: 5 -> 4, of which waited for: 2 -> 1; matrix products, arithmetic and copies ran while one was open for 0% -> 4% of each run, Pallas kernels for 0% -> 4%
where the time goes in v1:
time: 42.5 us; the launch traced here: 42.1 us
  blocking collectives  20.1 us (47%)
  Pallas kernels  8.93 us (21%)
  starting transfers between devices  7.05 us (17%)
  local copies, waits for them, and re-layouts  3.96 us (9%)
  waiting for transfers between devices  1.97 us (5%)
    all_to_all x1, blocking collectives, lane_device(): piece = lax.all_to_all(spectrum, 'gx', 0, 0, tiled=True)  11 us
    all_to_all x1, blocking collectives, lane_device(): rows = lax.all_to_all(spread, 'gx', 0, 0, tiled=True)  9.1 us
    pallas_call x4, Pallas kernels, call(): pl.pallas_call(kernel, out_shape=out_shapes, in_specs=specs, out_specs=vm...  8.93 us
    ppermute x1, starting transfers between devices, lane_device(): lax.ppermute(material, 'gx', down)  5.92 us
    unnamed x19, local copies, waits for them, and re-layouts  2.44 us
    ppermute x1, waiting for transfers between devices, lane_device(): lax.ppermute(incident, 'gx', up)  1.96 us
  transfers between devices with their start and end apart: 4, of which 1 were waited for; matrix products, arithmetic and copies ran while one was open for 4% of the time, Pallas kernels for 4%

profile of v1, /device:TPU:0, one launch (start us, length us, event | category | flops | bytes accessed | tf_op | source)
XLA Modules:
  0.0 42.1 jit_solution(7094526255367501230)
XLA Ops:
  0.0 0.5 %collective-permute-start.2 = (s32[16,4,128]{2,1,0:T(4,128)}, s32[16,4,128]{2,1,0:T(4,128)S(1)}, u32[]{:S(2)}, u32[]{:S(2)}) collective-permute-start(s32[16,4,128]{2,1,0:T(4,128)} %mat_ref.1), channel_id=1, source_target_pairs={{0,1},{1,2},{2,3},{3,4},{4,5},{5,6},{6,7},{7,8},{8,9},{9,10},{10,1... | collective-permute-start | bytes 98312 | tf_op jit(solution)/shard_map/ppermute | solution.py:363
  0.5 5.9 %collective-permute-start.3 = (s32[16,4,128]{2,1,0:T(4,128)}, s32[16,4,128]{2,1,0:T(4,128)S(1)}, u32[]{:S(2)}, u32[]{:S(2)}) collective-permute-start(s32[16,4,128]{2,1,0:T(4,128)} %mat_ref.1), channel_id=1, source_target_pairs={{1,0},{2,1},{3,2},{4,3},{5,4},{6,5},{7,6},{8,7},{9,8},{10,9},{11,1... | collective-permute-start | bytes 98312 | tf_op jit(solution)/shard_map/ppermute | solution.py:363
  6.4 0.7 %collective-permute-start.1 = (f32[2,16,4,128]{3,2,1,0:T(4,128)}, f32[2,16,4,128]{3,2,1,0:T(4,128)S(1)}, u32[]{:S(2)}, u32[]{:S(2)}) collective-permute-start(f32[2,16,4,128]{3,2,1,0:T(4,128)} %inc_ref.3), channel_id=1, source_target_pairs={{1,0},{2,1},{3,2},{4,3},{5,4},{6,5},{7,6},{8,7},{9,8},{10,9},{11,1... | collective-permute-start | bytes 196616 | tf_op jit(solution)/shard_map/ppermute | solution.py:362
  7.1 0.0 collective-permute-start
  7.1 0.7 %reshape.7.w3_ref = bf16[3,18,32]{2,1,0:T(8,128)(2,1)S(1)} reshape(bf16[3,3,3,2,32]{4,3,2,1,0:T(2,128)(2,1)} %bitcast.5) | data formatting | bytes 6912 | tf_op jit(solution)/shard_map/reshape | solution.py:377
  7.8 0.8 %reshape.6.w1_ref = bf16[3,36,32]{2,1,0:T(8,128)(2,1)S(1)} reshape(bf16[3,3,3,4,32]{4,3,2,1,0:T(4,128)(2,1)} %bitcast.4) | data formatting | bytes 13824 | tf_op jit(solution)/shard_map/reshape | solution.py:375
  8.6 0.0 copy-start.3
  8.6 0.9 %copy-done.3 = bf16[32,32,3,3,3]{1,0,4,3,2:T(8,128)(2,1)S(1)} copy-done((bf16[32,32,3,3,3]{1,0,4,3,2:T(8,128)(2,1)S(1)}, bf16[32,32,3,3,3]{1,0,4,3,2:T(8,128)(2,1)}, u32[]{:S(2)}) %copy-start.3) | copy-done | bytes 55320
  9.5 0.7 %copy-done.5 = f32[2,16,16]{2,1,0:T(8,128)S(1)} copy-done((f32[2,16,16]{2,1,0:T(8,128)S(1)}, f32[2,16,16]{2,1,0:T(8,128)}, u32[]{:S(2)}) %copy-start.5) | copy-done | bytes 2072
  10.2 0.7 %copy-done.6 = f32[2,4,128]{2,1,0:T(4,128)S(1)} copy-done((f32[2,4,128]{2,1,0:T(4,128)S(1)}, f32[2,4,128]{2,1,0:T(4,128)}, u32[]{:S(2)}) %copy-start.6) | copy-done | bytes 4120
  10.9 1.6 %shard_map.118 = (bf16[512,576]{1,0:T(8,128)(2,1)S(1)}, bf16[3,320,768]{2,1,0:T(8,128)(2,1)S(1)}, bf16[288,512]{1,0:T(8,128)(2,1)S(1)}, bf16[64,96]{1,0:T(8,128)...) custom-call(bf16[3,36,32]{2,1,0:T(8,128)(2,1)S(1)} %reshape.6.w1_ref, bf16[3,3,3,32,32]{4,3,2,1,0:T(8,128)(2,1)S(1)} %bitcast.3, ...), custom_call_target="tpu_custom_call" | custom-call | flops 1000000000 | bytes 4194304 | tf_op jit(solution)/shard_map/pallas_call | solution.py:343
  12.5 0.1 copy.14.con_ref
  12.6 0.0 collective-permute-done.2.mleft_ref
  12.6 0.0 collective-permute-done.3.mright_ref
  12.6 0.0 collective-permute-done.1.right_ref
  12.6 2.0 %collective-permute-done.left_ref = f32[2,16,4,128]{3,2,1,0:T(4,128)S(1)} collective-permute-done((f32[2,16,4,128]{3,2,1,0:T(4,128)}, f32[2,16,4,128]{3,2,1,0:T(4,128)S(1)}, u32[]{:S(2)}, u32[]{:S(2)}) %collective-permute-start) | collective-permute-done | bytes 65568 | tf_op jit(solution)/shard_map/ppermute | solution.py:362
  14.6 0.0 copy-done.4
  14.6 0.0 copy-start
  14.6 0.0 copy-start.1
  14.6 5.5 %shard_map.119 = f32[32,4,128]{2,1,0:T(4,128)S(1)} custom-call(f32[8,2]{1,0:T(8,128)S(1)} %copy.14.con_ref, f32[2,16,4,128]{3,2,1,0:T(4,128)S(1)} %collective-permute-done.left_ref, f32[2,16,4,128]{3,2,1,0:T(4,128)S(1)} %copy-done.2, f32[2,16,4,128]{3,2,1,0:T(4,128)S(1)} %collective-permute-done.1.right_ref, ...), custom_call_target="tpu_custom_call" | custom-call | flops 1000000000 | bytes 4194304 | tf_op jit(solution)/shard_map/pallas_call | solution.py:343
  20.1 11.0 %all_to_all.10.in_ref = f32[32,4,128]{2,1,0:T(4,128)S(1)} all-to-all(f32[32,4,128]{2,1,0:T(4,128)S(1)} %shard_map.119), channel_id=1, replica_groups=mesh['grp'=1,'gx'=32,'gy'=1] {'gx'}, dimensions={0} | all-to-all | bytes 131072 | tf_op jit(solution)/shard_map/all_to_all | solution.py:401
  31.1 0.7 %shard_map.120 = f32[32,4,128]{2,1,0:T(4,128)S(1)} custom-call(f32[32,4,128]{2,1,0:T(4,128)S(1)} %all_to_all.10.in_ref, bf16[128,768]{1,0:T(8,128)(2,1)S(1)} %copy-done, bf16[128,768]{1,0:T(8,128)(2,1)S(1)} %copy-done.1, f32[128,128]{1,0:T(8,128)S(1)} %get-tuple-element.15.sr_ref, f32[128,128]{1,0:T(8,128)S(1)} %get-tuple-element.16.si_ref), custom_call_target="tpu_custom_call" | custom-call | flops 100000000 | bytes 4194304 | tf_op jit(solution)/shard_map/pallas_call | solution.py:343
  31.9 9.1 %all_to_all.11.in_ref = f32[32,4,128]{2,1,0:T(4,128)S(1)} all-to-all(f32[32,4,128]{2,1,0:T(4,128)S(1)} %shard_map.120), channel_id=1, replica_groups=mesh['grp'=1,'gx'=32,'gy'=1] {'gx'}, dimensions={0} | all-to-all | bytes 131072 | tf_op jit(solution)/shard_map/all_to_all | solution.py:414
  41.0 1.1 %shard_map.121 = f32[2,16,4,128]{3,2,1,0:T(4,128)} custom-call(f32[32,4,128]{2,1,0:T(4,128)S(1)} %all_to_all.11.in_ref, bf16[128,768]{1,0:T(8,128)(2,1)S(1)} %copy-done, f32[2,16,4,128]{3,2,1,0:T(4,128)S(1)} %copy-done.2), custom_call_target="tpu_custom_call" | custom-call | flops 100000000 | bytes 4194304 | tf_op jit(solution)/shard_map/pallas_call | solution.py:343
  (11 shorter events, 0.0 us)
Async XLA Ops:
  0.0 12.6 %collective-permute-start.2 = (s32[16,4,128]{2,1,0:T(4,128)}, s32[16,4,128]{2,1,0:T(4,128)S(1)}, u32[]{:S(2)}, u32[]{:S(2)}) collective-permute-start(s32[16,4,128]{2,1,0:T(4,128)} %mat_ref.1), channel_id=1, source_target_pairs={{0,1},{1,2},{2,3},{3,4},{4,5},{5,6},{6,7},{7,8},{8,9},{9,10},{10,1... | collective-permute-start | bytes 98312 | tf_op jit(solution)/shard_map/ppermute | solution.py:363
  0.5 12.1 %collective-permute-start.3 = (s32[16,4,128]{2,1,0:T(4,128)}, s32[16,4,128]{2,1,0:T(4,128)S(1)}, u32[]{:S(2)}, u32[]{:S(2)}) collective-permute-start(s32[16,4,128]{2,1,0:T(4,128)} %mat_ref.1), channel_id=1, source_target_pairs={{1,0},{2,1},{3,2},{4,3},{5,4},{6,5},{7,6},{8,7},{9,8},{10,9},{11,1... | collective-permute-start | bytes 98312 | tf_op jit(solution)/shard_map/ppermute | solution.py:363
  6.4 6.2 %collective-permute-start.1 = (f32[2,16,4,128]{3,2,1,0:T(4,128)}, f32[2,16,4,128]{3,2,1,0:T(4,128)S(1)}, u32[]{:S(2)}, u32[]{:S(2)}) collective-permute-start(f32[2,16,4,128]{3,2,1,0:T(4,128)} %inc_ref.3), channel_id=1, source_target_pairs={{1,0},{2,1},{3,2},{4,3},{5,4},{6,5},{7,6},{8,7},{9,8},{10,9},{11,1... | collective-permute-start | bytes 196616 | tf_op jit(solution)/shard_map/ppermute | solution.py:362
  7.1 7.5 %collective-permute-start = (f32[2,16,4,128]{3,2,1,0:T(4,128)}, f32[2,16,4,128]{3,2,1,0:T(4,128)S(1)}, u32[]{:S(2)}, u32[]{:S(2)}) collective-permute-start(f32[2,16,4,128]{3,2,1,0:T(4,128)} %inc_ref.3), channel_id=1, source_target_pairs={{0,1},{1,2},{2,3},{3,4},{4,5},{5,6},{6,7},{7,8},{8,9},{9,10},{10,1... | collective-permute-start | bytes 196616 | tf_op jit(solution)/shard_map/ppermute | solution.py:362
  8.6 0.9 %copy-start.3 = (bf16[32,32,3,3,3]{1,0,4,3,2:T(8,128)(2,1)S(1)}, bf16[32,32,3,3,3]{1,0,4,3,2:T(8,128)(2,1)}, u32[]{:S(2)}) copy-start(bf16[32,32,3,3,3]{1,0,4,3,2:T(8,128)(2,1)} %param.16) | copy-start | bytes 165892
  9.5 0.7 %copy-start.5 = (f32[2,16,16]{2,1,0:T(8,128)S(1)}, f32[2,16,16]{2,1,0:T(8,128)}, u32[]{:S(2)}) copy-start(f32[2,16,16]{2,1,0:T(8,128)} %zk_ref.1) | copy-start | bytes 6148
  10.2 0.7 %copy-start.6 = (f32[2,4,128]{2,1,0:T(4,128)S(1)}, f32[2,4,128]{2,1,0:T(4,128)}, u32[]{:S(2)}) copy-start(f32[2,4,128]{2,1,0:T(4,128)} %sp_ref.1) | copy-start | bytes 12292
  10.9 1.6 %copy-start.8 = (f32[8,2]{0,1:T(2,128)S(1)}, f32[8,2]{0,1:T(2,128)}, u32[]{:S(2)}) copy-start(f32[8,2]{0,1:T(2,128)} %param.14) | copy-start | bytes 196
  10.9 3.6 %copy-start.2 = (f32[2,16,4,128]{3,2,1,0:T(4,128)S(1)}, f32[2,16,4,128]{3,2,1,0:T(4,128)}, u32[]{:S(2)}) copy-start(f32[2,16,4,128]{3,2,1,0:T(4,128)} %inc_ref.3) | copy-start | bytes 196612
  10.9 3.6 %copy-start.4 = (s32[16,4,128]{2,1,0:T(4,128)S(1)}, s32[16,4,128]{2,1,0:T(4,128)}, u32[]{:S(2)}) copy-start(s32[16,4,128]{2,1,0:T(4,128)} %mat_ref.1) | copy-start | bytes 98308
  10.9 3.6 %copy-start.7 = (bf16[768,128]{1,0:T(8,128)(2,1)S(1)}, bf16[768,128]{1,0:T(8,128)(2,1)}, u32[]{:S(2)}) copy-start(bf16[768,128]{1,0:T(8,128)(2,1)} %constant.6.clone.dft_ref) | copy-start | bytes 589828
  14.6 16.6 %copy-start = (bf16[128,768]{1,0:T(8,128)(2,1)S(1)}, bf16[128,768]{1,0:T(8,128)(2,1)}, u32[]{:S(2)}) copy-start(bf16[128,768]{1,0:T(8,128)(2,1)} %constant.7.clone.fwd_ref.tab_ref) | copy-start | bytes 589828
  14.6 16.5 %copy-start.1 = (bf16[128,768]{1,0:T(8,128)(2,1)S(1)}, bf16[128,768]{1,0:T(8,128)(2,1)}, u32[]{:S(2)}) copy-start(bf16[128,768]{1,0:T(8,128)(2,1)} %constant.8.clone.inv_ref) | copy-start | bytes 589828

commit v2 on v1

--- a/solution.py
+++ b/solution.py
@@ -3,8 +3,6 @@
 
 import jax
 import jax.numpy as jnp
-import ml_dtypes
-import numpy as np
 from jax import lax
 from jax.experimental import pallas as pl
 from jax.experimental.pallas import tpu as pltpu
@@ -118,26 +116,22 @@
     return high, low
 
 
-def split_np(values):
-    high = values.astype(ml_dtypes.bfloat16)
-    low = (values - high.astype(np.float64)).astype(ml_dtypes.bfloat16)
-    return high, low
-
-
-def angles(rows, cols, length):
-    product = (np.asarray(rows)[:, None] * np.asarray(cols)[None, :]) % length
-    angle = product.astype(np.float64) * (2.0 * math.pi / length)
-    return np.cos(angle), np.sin(angle)
-
-
-def left_table(rows, cols, length, scale=1.0):
-    high, low = split_np(np.concatenate(angles(rows, cols, length), axis=1) * scale)
-    return np.concatenate([high, high, low], axis=1)
-
-
-def right_table(rows, cols, length):
-    high, low = split_np(np.concatenate(angles(rows, cols, length), axis=0))
-    return np.concatenate([high, high, low], axis=0)
+def cosine(steps, length):
+    turn = 2.0 * math.pi / length
+    angle = (length // 4 - jnp.minimum(steps, length - steps)).astype(F32) * turn
+    square = angle * angle
+    total = jnp.full_like(angle, 1.0 / math.factorial(13))
+    for power in (11, 9, 7, 5, 3, 1):
+        sign = 1.0 if power % 4 == 1 else -1.0
+        total = total * square + sign / math.factorial(power)
+    return total * angle
+
+
+def dft_parts(rows, cols, length, axis, scale=1.0):
+    steps = lax.rem(rows * cols, length)
+    later = lax.rem(steps + 3 * length // 4, length)
+    high, low = split(jnp.concatenate([cosine(steps, length), cosine(later, length)], axis=axis) * scale)
+    return jnp.concatenate([high, high, low], axis=axis)
 
 
 def left_split(values):
@@ -182,19 +176,8 @@
     return jnp.concatenate(rows, axis=0)
 
 
-def prepare_kernel(nz, hid, w1_ref, w2_ref, w3_ref, zk_ref, sp_ref, t1_ref, t2_ref, t3_ref, z_ref, sr_ref, si_ref):
-    taps, cols = w1_ref.shape[1], t1_ref.shape[1]
-    pick = (iota((taps, cols), 0) == iota((taps, cols), 1) // nz).astype(BF16)
-    spread = [
-        lax.dot_general(w1_ref[a], pick, (((0,), (0,)), ((), ())), preferred_element_type=F32)
-        for a in range(3)
-    ]
-    place = iota((hid, cols), 1) % nz
-    for z in range(nz):
-        rows = jnp.zeros((hid, cols), F32)
-        for a in range(3):
-            rows = jnp.where(place == z + a - 1, spread[a], rows)
-        t1_ref[z * hid : (z + 1) * hid, :] = rows.astype(BF16)
+def middle_kernel(nz, w2_ref, t2_ref):
+    hid = w2_ref.shape[3]
     half = nz // 2
     wide = half * hid
     pick = (iota((hid, wide), 0) == iota((hid, wide), 1) % hid).astype(BF16)
@@ -207,14 +190,40 @@
                 for a in range(3):
                     rows = jnp.where(place == r + a - 2, spread[a], rows)
                 t2_ref[d, r * hid : (r + 1) * hid, b * wide : (b + 1) * wide] = rows.astype(BF16)
+
+
+def prepare_kernel(
+    nz, xl, w1_ref, w3_ref, zk_ref, sp_ref,
+    t1_ref, t3_ref, z_ref, sr_ref, si_ref, dft_ref, fwd_ref, inv_ref,
+):
+    channels, hid = w1_ref.shape[3:]
+    taps, cols = 9 * channels, t1_ref.shape[1]
+    pick = (iota((taps, cols), 0) == iota((taps, cols), 1) // nz).astype(BF16)
+    spread = []
+    for a in range(3):
+        stack = jnp.concatenate(
+            [w1_ref[a, b, d].astype(F32) for b in range(3) for d in range(3)], axis=0
+        ).astype(BF16)
+        spread.append(
+            lax.dot_general(stack, pick, (((0,), (0,)), ((), ())), preferred_element_type=F32)
+        )
+    place = iota((hid, cols), 1) % nz
+    for z in range(nz):
+        rows = jnp.zeros((hid, cols), F32)
+        for a in range(3):
+            rows = jnp.where(place == z + a - 1, spread[a], rows)
+        t1_ref[z * hid : (z + 1) * hid, :] = rows.astype(BF16)
     rows3, cols3 = t3_ref.shape
-    taps = w3_ref.shape[1]
+    taps = 9 * w3_ref.shape[3]
     repeat = (iota((rows3, taps), 0) // nz == iota((rows3, taps), 1)).astype(BF16)
     pick = (iota((hid, cols3), 0) == iota((hid, cols3), 1) % hid).astype(BF16)
     offset = iota((rows3, cols3), 1) // hid - iota((rows3, cols3), 0) % nz
     total = jnp.zeros((rows3, cols3), F32)
     for a in range(3):
-        spread = mm(mm(repeat, w3_ref[a]).astype(BF16), pick)
+        stack = jnp.concatenate(
+            [w3_ref[a, b, d].astype(F32) for b in range(3) for d in range(3)], axis=0
+        ).astype(BF16)
+        spread = mm(mm(repeat, stack).astype(BF16), pick)
         total = jnp.where(offset == a - 1, spread, total)
     t3_ref[...] = total.astype(BF16)
     kr, ki = zk_ref[0], zk_ref[1]
@@ -232,16 +241,23 @@
             precision=lax.Precision.HIGHEST,
             preferred_element_type=F32,
         )
-
-
-def polarised(inc_ref, mat_ref, con_ref, x):
-    re, im, cells = inc_ref[0, :, x, :], inc_ref[1, :, x, :], mat_ref[:, x, :]
+    nx, ny = inv_ref.shape[0], dft_ref.shape[1]
+    dft_ref[...] = dft_parts(iota((ny, ny), 0), iota((ny, ny), 1), ny, 0)
+    first, second = iota((nx, nx), 0), iota((nx, nx), 1)
+    inv_ref[...] = dft_parts(first, second, nx, 1, 1.0 / (nx * ny))
+    count = nx // xl
+    second = lax.rem(second, count) * xl + second // count
+    fwd_ref[...] = dft_parts(first, second, nx, 1)
+
+
+def polarised(column, con_ref):
+    re, im, cells = column
     chi_re = jnp.zeros_like(re)
     chi_im = jnp.zeros_like(re)
-    for k in range(con_ref.shape[0]):
-        here = cells == k
-        chi_re = jnp.where(here, con_ref[k, 0], chi_re)
-        chi_im = jnp.where(here, con_ref[k, 1], chi_im)
+    for k in range(con_ref.shape[1]):
+        here = cells == float(k)
+        chi_re = jnp.where(here, con_ref[0, k], chi_re)
+        chi_im = jnp.where(here, con_ref[1, k], chi_im)
     return re, im, chi_re * re - chi_im * im, chi_re * im + chi_im * re
 
 
@@ -250,19 +266,26 @@
 
 
 def corrector_kernel(
-    con_ref, left_ref, inc_ref, right_ref, mleft_ref, mat_ref, mright_ref, t1_ref, t2_ref, t3_ref,
-    z_ref, dft_ref, out_ref, feat, hid1, hid2,
+    con_ref, own_ref, chip_ref, far_ref, t1_ref, t2_ref, t3_ref, z_ref, dft_ref, out_ref,
+    feat, hid1, hid2,
 ):
-    xl, ny = inc_ref.shape[2], inc_ref.shape[3]
-    nz = inc_ref.shape[1]
-    columns = [(left_ref, mleft_ref, x) for x in range(xl - 3, xl)]
-    columns += [(inc_ref, mat_ref, x) for x in range(xl)]
-    columns += [(right_ref, mright_ref, x) for x in range(3)]
+    nz, xl, ny = own_ref.shape[1:]
+    even = lax.axis_index("gx") % 2 == 0
+
+    def column(x):
+        if x < 0:
+            x += xl
+            return [jnp.where(even, far_ref[i, :, x, :], chip_ref[i, :, x, :]) for i in range(3)]
+        if x >= xl:
+            x -= xl
+            return [jnp.where(even, chip_ref[i, :, x, :], far_ref[i, :, x, :]) for i in range(3)]
+        return [own_ref[i, :, x, :] for i in range(3)]
+
     own = []
     deep = 12 * nz
-    for place, (field, cells, x) in enumerate(columns):
-        re, im, pol_re, pol_im = polarised(field, cells, con_ref, x)
-        if field is inc_ref:
+    for place in range(xl + 6):
+        re, im, pol_re, pol_im = polarised(column(place - 3), con_ref)
+        if 0 <= place - 3 < xl:
             own.append(jnp.concatenate([pol_re, pol_im], axis=0))
         stack = jnp.concatenate([re, im, pol_re, pol_im], axis=0)
         rolled = [pltpu.roll(stack, 1, 1), stack, pltpu.roll(stack, ny - 1, 1)]
@@ -338,7 +361,9 @@
 
 def call(kernel, out_shapes, args, scratch=(), smem=(), flops=0):
     vmem = pl.BlockSpec(memory_space=pltpu.VMEM)
-    specs = [pl.BlockSpec(memory_space=pltpu.SMEM) if i in smem else vmem for i in range(len(args))]
+    specs = [vmem] * len(args)
+    for i in smem:
+        specs[i] = pl.BlockSpec(memory_space=pltpu.SMEM)
     single = not isinstance(out_shapes, list)
     return pl.pallas_call(
         kernel,
@@ -357,39 +382,42 @@
     hid = w_middle.shape[0]
     ql, nx = spectral.shape[1], spectral.shape[2]
     struct = jax.ShapeDtypeStruct
-    up = [(i, (i + 1) % count) for i in range(count)]
-    down = [(j, i) for i, j in up]
-    left, right = lax.ppermute(incident, "gx", up), lax.ppermute(incident, "gx", down)
-    mleft, mright = lax.ppermute(material, "gx", up), lax.ppermute(material, "gx", down)
-    t1, t2, t3, zmat, sr, si = call(
-        functools.partial(prepare_kernel, nz, hid),
+    last = lax.broadcasted_iota(jnp.int32, (3, 1, 1, 1), 0) == 2
+    own = jnp.where(last, material.astype(F32)[None], jnp.pad(incident, ((0, 1),) + ((0, 0),) * 3))
+    chip = lax.ppermute(own, "gx", [(i, i ^ 1) for i in range(count)])
+    pairs = [(i, (i + 1) % count) for i in range(1, count, 2)]
+    far = lax.ppermute(own, "gx", pairs + [(j, i) for i, j in pairs])
+    lanes = 2 * nz * xl
+    t2 = call(
+        functools.partial(middle_kernel, nz),
+        struct((3, (nz // 2 + 2) * hid, 3 * nz // 2 * hid), BF16),
+        (jnp.transpose(w_middle, (2, 3, 4, 0, 1)),),
+        flops=10**9,
+    )
+    t1, t3, zmat, sr, si, dft, fwd, inv = call(
+        functools.partial(prepare_kernel, nz, xl),
         [
             struct((nz * hid, 36 * nz), BF16),
-            struct((3, (nz // 2 + 2) * hid, 3 * nz // 2 * hid), BF16),
             struct((18 * nz, nz * hid), BF16),
             struct((4 * nz, 6 * nz), BF16),
             struct((nx, ql * 2 * nz), F32),
             struct((nx, ql * 2 * nz), F32),
+            struct((6 * ny, ny), BF16),
+            struct((nx, 6 * nx), BF16),
+            struct((nx, 6 * nx), BF16),
         ],
         (
-            jnp.transpose(w_first, (2, 3, 4, 1, 0)).reshape(3, 36, hid),
-            jnp.transpose(w_middle, (2, 3, 4, 0, 1)),
-            jnp.transpose(w_last, (2, 3, 4, 0, 1)).reshape(3, 18, hid),
+            jnp.transpose(w_first, (2, 3, 4, 1, 0)),
+            jnp.transpose(w_last, (2, 3, 4, 0, 1)),
             z_kernel,
             spectral,
         ),
         flops=10**9,
     )
-    alternate = [xl * s + x for x in range(xl) for s in range(count)]
-    natural = list(range(nx))
-    lanes = 2 * nz * xl
     spectrum = call(
         corrector_kernel,
         struct((count, ql, lanes), F32),
-        (
-            contrast, left, incident, right, mleft, material, mright, t1, t2, t3, zmat,
-            right_table(range(ny), range(ny), ny),
-        ),
+        (jnp.transpose(contrast), own, chip, far, t1, t2, t3, zmat, dft),
         scratch=[
             pltpu.VMEM(((xl + 6) * 12 * nz, ny), BF16),
             pltpu.VMEM((nz * hid, (xl + 4) * ny), BF16),
@@ -402,20 +430,14 @@
     spread = call(
         functools.partial(spectral_kernel, nz),
         struct((count, xl, lanes), F32),
-        (
-            piece,
-            left_table(natural, alternate, nx),
-            left_table(natural, natural, nx, 1.0 / (nx * ny)),
-            sr,
-            si,
-        ),
+        (piece, fwd, inv, sr, si),
         flops=10**8,
     )
     rows = lax.all_to_all(spread, "gx", 0, 0, tiled=True)
     return call(
         functools.partial(finish_kernel, nz),
         struct(incident.shape, F32),
-        (rows, left_table(natural, alternate, ny), incident),
+        (rows, fwd, own),
         flops=10**8,
     )
 

time: 42.5 us -> 40.2 us (0.946)
  local copies, waits for them, and re-layouts: 3.96 us -> 1.27 us
  waiting for transfers between devices: 1.97 us -> 0.01 us
  other arithmetic: 0 us -> 1.69 us
  blocking collectives: 20.1 us -> 21.2 us
  starting transfers between devices: 7.05 us -> 6.44 us
    ppermute x4 -> x2, waiting for transfers between devices: 1.97 us -> 0.01 us  [the longest x1 0.01 us: lane_device(): chip = lax.ppermute(own, 'gx', [(i, i ^ 1) for i in range(count)])]
    reshape x2 -> x0, local copies, waits for them, and re-layouts: 1.51 us -> none  [the longest x1 0.77 us: lane_device(): jnp.transpose(w_first, (2, 3, 4, 1, 0)).reshape(3, 36, hid)]
    unnamed x19 -> x12, local copies, waits for them, and re-layouts: 2.44 us -> 1.27 us
    all_to_all x1, blocking collectives: 11 us -> 12.1 us  [lane_device(): piece = lax.all_to_all(spectrum, 'gx', 0, 0, tiled=True)]
    select_n x0 -> x1, other arithmetic: none -> 0.92 us  [lane_device(): jnp.where(last, material.astype(F32)[None], jnp.pad(incident, ((0, 1),) +...]
    convert_element_type x0 -> x1, other arithmetic: none -> 0.76 us  [lane_device(): material.astype(F32)[None]]
    ppermute x4 -> x2, starting transfers between devices: 7.05 us -> 6.44 us  [the longest x1 6.44 us: lane_device(): far = lax.ppermute(own, 'gx', pairs + [(j, i) for i, j in pairs])]
    pallas_call x4 -> x5, Pallas kernels: 8.93 us -> 9.09 us  [call(): pl.pallas_call(kernel, out_shape=out_shapes, in_specs=specs, out_specs=vm...]
  transfers between devices with their start and end apart: 4 -> 2, of which waited for: 1 -> 0; matrix products, arithmetic and copies ran while one was open for 4% -> 0% of each run, Pallas kernels for 4% -> 4%
where the time goes in v2:
time: 40.2 us; the launch traced here: 39.8 us
  blocking collectives  21.2 us (53%)
  Pallas kernels  9.09 us (23%)
  starting transfers between devices  6.44 us (16%)
  other arithmetic  1.69 us (4%)
  local copies, waits for them, and re-layouts  1.27 us (3%)
    all_to_all x1, blocking collectives, lane_device(): piece = lax.all_to_all(spectrum, 'gx', 0, 0, tiled=True)  12.1 us
    all_to_all x1, blocking collectives, lane_device(): rows = lax.all_to_all(spread, 'gx', 0, 0, tiled=True)  9.1 us
    pallas_call x5, Pallas kernels, call(): pl.pallas_call(kernel, out_shape=out_shapes, in_specs=specs, out_specs=vm...  9.09 us
    ppermute x1, starting transfers between devices, lane_device(): far = lax.ppermute(own, 'gx', pairs + [(j, i) for i, j in pairs])  6.44 us
    unnamed x12, local copies, waits for them, and re-layouts  1.27 us
    select_n x1, other arithmetic, lane_device(): jnp.where(last, material.astype(F32)[None], jnp.pad(incident, ((0, 1),) +...  0.92 us
  transfers between devices with their start and end apart: 2, of which 0 were waited for; matrix products, arithmetic and copies ran while one was open for 0% of the time, Pallas kernels for 4%

profile of v2, /device:TPU:0, one launch (start us, length us, event | category | flops | bytes accessed | tf_op | source)
XLA Modules:
  0.0 39.8 jit_solution(5483085940229014289)
XLA Ops:
  0.0 0.8 %convert_element_type.5 = f32[16,4,128]{2,1,0:T(4,128)S(1)} convert(s32[16,4,128]{2,1,0:T(4,128)} %param.9) | non-fusion elementwise | flops 8192 | bytes 65536 | tf_op jit(solution)/shard_map/convert_element_type | solution.py:386
  0.8 0.9 %pad_select_fusion.own_ref.inc_ref = f32[3,16,4,128]{3,2,1,0:T(4,128)S(1)} fusion(f32[2,16,4,128]{3,2,1,0:T(4,128)} %param.8, f32[16,4,128]{2,1,0:T(4,128)S(1)} %convert_element_type.5, pred[3]{0:T(512)(128)(4,1)S(1)} %iota_compare_fusion), kind=kLoop, calls=%fused_computation | loop fusion | flops 24576 | bytes 196611 | tf_op jit(solution)/shard_map/jit(_where)/select_n | solution.py:386
  1.7 6.4 %collective-permute-start.1 = (f32[3,16,4,128]{3,2,1,0:T(4,128)S(1)}, f32[3,16,4,128]{3,2,1,0:T(4,128)S(1)}, u32[]{:S(2)}, u32[]{:S(2)}) collective-permute-start(f32[3,16,4,128]{3,2,1,0:T(4,128)S(1)} %pad_select_fusion.own_ref.inc_ref), channel_id=1, source_target_pairs={{1,2},{3,4},{5,6},{7,8},{9,10},{11,12},{13,14},{15,16},{17,18},{19... | collective-permute-start | bytes 294920 | tf_op jit(solution)/shard_map/ppermute | solution.py:389
  8.1 0.0 collective-permute-start
  8.1 0.0 copy-start
  8.1 0.9 %copy-done = bf16[32,32,3,3,3]{1,0,4,3,2:T(8,128)(2,1)S(1)} copy-done((bf16[32,32,3,3,3]{1,0,4,3,2:T(8,128)(2,1)S(1)}, bf16[32,32,3,3,3]{1,0,4,3,2:T(8,128)(2,1)}, u32[]{:S(2)}) %copy-start) | copy-done | bytes 55320
  9.1 0.0 copy-start.1
  9.1 0.0 copy-start.2
  9.1 0.0 copy-start.3
  9.1 0.0 copy-start.4
  9.1 0.4 %shard_map.83.t2_ref = bf16[3,320,768]{2,1,0:T(8,128)(2,1)S(1)} custom-call(bf16[3,3,3,32,32]{4,3,2,1,0:T(8,128)(2,1)S(1)} %bitcast.4), custom_call_target="tpu_custom_call" | custom-call | flops 1000000000 | bytes 4194304 | tf_op jit(solution)/shard_map/pallas_call | solution.py:368
  9.5 0.3 copy-done.1
  9.8 0.0 copy-done.2
  9.8 0.0 copy-done.3
  9.8 0.0 copy-done.4
  9.8 1.3 %shard_map.82 = (bf16[512,576]{1,0:T(8,128)(2,1)S(1)}, bf16[288,512]{1,0:T(8,128)(2,1)S(1)}, bf16[64,96]{1,0:T(8,128)(2,1)S(1)}, f32[128,128]{1,0:T(8,128)S(1)},...) custom-call(bf16[3,3,3,4,32]{4,3,2,1,0:T(4,128)(2,1)S(1)} %bitcast.5, ...), custom_call_target="tpu_custom_call" | custom-call | flops 1000000000 | bytes 4194304 | tf_op jit(solution)/shard_map/pallas_call | solution.py:368
  11.2 0.0 collective-permute-done.1.far_ref
  11.2 0.0 collective-permute-done.chip_ref
  11.2 0.0 copy-done.5
  11.2 5.5 %shard_map.84 = f32[32,4,128]{2,1,0:T(4,128)S(1)} custom-call(f32[2,8]{1,0:T(2,128)S(1)} %bitcast.7, f32[3,16,4,128]{3,2,1,0:T(4,128)S(1)} %pad_select_fusion.own_ref.inc_ref, f32[3,16,4,128]{3,2,1,0:T(4,128)S(1)} %collective-permute-done.chip_ref, f32[3,16,4,128]{3,2,1,0:T(4,128)S(1)} %collective-permute-done.1.far_ref, ...), custom_call_target="tpu_custom_call" | custom-call | flops 1000000000 | bytes 4194304 | tf_op jit(solution)/shard_map/pallas_call | solution.py:368
  16.7 12.1 %all_to_all.10.in_ref = f32[32,4,128]{2,1,0:T(4,128)S(1)} all-to-all(f32[32,4,128]{2,1,0:T(4,128)S(1)} %shard_map.84), channel_id=1, replica_groups=mesh['grp'=1,'gx'=32,'gy'=1] {'gx'}, dimensions={0} | all-to-all | bytes 131072 | tf_op jit(solution)/shard_map/all_to_all | solution.py:429
  28.9 0.7 %shard_map.85 = f32[32,4,128]{2,1,0:T(4,128)S(1)} custom-call(f32[32,4,128]{2,1,0:T(4,128)S(1)} %all_to_all.10.in_ref, bf16[128,768]{1,0:T(8,128)(2,1)S(1)} %get-tuple-element.17.fwd_ref.tab_ref, bf16[128,768]{1,0:T(8,128)(2,1)S(1)} %get-tuple-element.18.inv_ref, f32[128,128]{1,0:T(8,128)S(1)} %get-tuple-element.19.sr_ref, ...), custom_call_target="tpu_custom_call" | custom-call | flops 100000000 | bytes 4194304 | tf_op jit(solution)/shard_map/pallas_call | solution.py:368
  29.6 9.1 %all_to_all.11.in_ref = f32[32,4,128]{2,1,0:T(4,128)S(1)} all-to-all(f32[32,4,128]{2,1,0:T(4,128)S(1)} %shard_map.85), channel_id=1, replica_groups=mesh['grp'=1,'gx'=32,'gy'=1] {'gx'}, dimensions={0} | all-to-all | bytes 131072 | tf_op jit(solution)/shard_map/all_to_all | solution.py:436
  38.7 1.1 %shard_map.86 = f32[2,16,4,128]{3,2,1,0:T(4,128)} custom-call(f32[32,4,128]{2,1,0:T(4,128)S(1)} %all_to_all.11.in_ref, bf16[128,768]{1,0:T(8,128)(2,1)S(1)} %get-tuple-element.17.fwd_ref.tab_ref, f32[3,16,4,128]{3,2,1,0:T(4,128)S(1)} %pad_select_fusion.own_ref.inc_ref), custom_call_target="tpu_custom_call" | custom-call | flops 100000000 | bytes 4194304 | tf_op jit(solution)/shard_map/pallas_call | solution.py:368
  (2 shorter events, 0.0 us)
Async XLA Ops:
  1.7 9.5 %collective-permute-start.1 = (f32[3,16,4,128]{3,2,1,0:T(4,128)S(1)}, f32[3,16,4,128]{3,2,1,0:T(4,128)S(1)}, u32[]{:S(2)}, u32[]{:S(2)}) collective-permute-start(f32[3,16,4,128]{3,2,1,0:T(4,128)S(1)} %pad_select_fusion.own_ref.inc_ref), channel_id=1, source_target_pairs={{1,2},{3,4},{5,6},{7,8},{9,10},{11,12},{13,14},{15,16},{17,18},{19... | collective-permute-start | bytes 294920 | tf_op jit(solution)/shard_map/ppermute | solution.py:389
  8.1 3.1 %collective-permute-start = (f32[3,16,4,128]{3,2,1,0:T(4,128)S(1)}, f32[3,16,4,128]{3,2,1,0:T(4,128)S(1)}, u32[]{:S(2)}, u32[]{:S(2)}) collective-permute-start(f32[3,16,4,128]{3,2,1,0:T(4,128)S(1)} %pad_select_fusion.own_ref.inc_ref), channel_id=1, source_target_pairs={{0,1},{1,0},{2,3},{3,2},{4,5},{5,4},{6,7},{7,6},{8,9},{9,8},{10,11... | collective-permute-start | bytes 294920 | tf_op jit(solution)/shard_map/ppermute | solution.py:387
  8.1 0.9 %copy-start = (bf16[32,32,3,3,3]{1,0,4,3,2:T(8,128)(2,1)S(1)}, bf16[32,32,3,3,3]{1,0,4,3,2:T(8,128)(2,1)}, u32[]{:S(2)}) copy-start(bf16[32,32,3,3,3]{1,0,4,3,2:T(8,128)(2,1)} %param.12) | copy-start | bytes 165892
  9.1 0.7 %copy-start.1 = (bf16[32,4,3,3,3]{0,1,4,3,2:T(4,128)(2,1)S(1)}, bf16[32,4,3,3,3]{0,1,4,3,2:T(4,128)(2,1)}, u32[]{:S(2)}) copy-start(bf16[32,4,3,3,3]{0,1,4,3,2:T(4,128)(2,1)} %param.11) | copy-start | bytes 20740
  9.1 0.7 %copy-start.2 = (f32[2,16,16]{2,1,0:T(8,128)S(1)}, f32[2,16,16]{2,1,0:T(8,128)}, u32[]{:S(2)}) copy-start(f32[2,16,16]{2,1,0:T(8,128)} %zk_ref.1) | copy-start | bytes 6148
  9.1 0.7 %copy-start.3 = (bf16[2,32,3,3,3]{1,0,4,3,2:T(2,128)(2,1)S(1)}, bf16[2,32,3,3,3]{1,0,4,3,2:T(2,128)(2,1)}, u32[]{:S(2)}) copy-start(bf16[2,32,3,3,3]{1,0,4,3,2:T(2,128)(2,1)} %param.13) | copy-start | bytes 10372
  9.1 0.7 %copy-start.4 = (f32[2,4,128]{2,1,0:T(4,128)S(1)}, f32[2,4,128]{2,1,0:T(4,128)}, u32[]{:S(2)}) copy-start(f32[2,4,128]{2,1,0:T(4,128)} %sp_ref.1) | copy-start | bytes 12292
  9.8 1.4 %copy-start.5 = (f32[8,2]{0,1:T(2,128)S(1)}, f32[8,2]{0,1:T(2,128)}, u32[]{:S(2)}) copy-start(f32[8,2]{0,1:T(2,128)} %param.10) | copy-start | bytes 196

commit v3 on v2

--- a/solution.py
+++ b/solution.py
@@ -176,27 +176,47 @@
     return jnp.concatenate(rows, axis=0)
 
 
-def middle_kernel(nz, w2_ref, t2_ref):
+def table_kernel(xl, shift, dft_ref, fwd_ref, inv_ref):
+    nx, ny = inv_ref.shape[0], dft_ref.shape[1]
+    dft_ref[...] = dft_parts(iota((ny, ny), 0), iota((ny, ny), 1), ny, 0)
+    first, second = iota((nx, nx), 0), iota((nx, nx), 1)
+    inv_ref[...] = dft_parts(lax.rem(first + shift, nx), second, nx, 1, 1.0 / (nx * ny))
+    count = nx // xl
+    second = lax.rem(second, count) * xl + second // count
+    fwd_ref[...] = dft_parts(first, second, nx, 1)
+
+
+def banded(spread, place, start):
+    rows = jnp.zeros_like(spread[0])
+    for a in range(3):
+        rows = jnp.where(place == start + a, spread[a], rows)
+    return rows.astype(BF16)
+
+
+def weight_kernel(
+    nz, w1_ref, w2_ref, w3_ref, zk_ref, sp_ref, dft_ref,
+    t1_ref, t2_ref, t2m_ref, t3_ref, z_ref, sr_ref, si_ref,
+):
     hid = w2_ref.shape[3]
     half = nz // 2
     wide = half * hid
     pick = (iota((hid, wide), 0) == iota((hid, wide), 1) % hid).astype(BF16)
     place = iota((hid, wide), 1) // hid
+    tall = (half - 1) * hid
     for b in range(3):
         for d in range(3):
             spread = [mm(w2_ref[a, b, d], pick) for a in range(3)]
-            for r in range(half + 2):
-                rows = jnp.zeros((hid, wide), F32)
-                for a in range(3):
-                    rows = jnp.where(place == r + a - 2, spread[a], rows)
-                t2_ref[d, r * hid : (r + 1) * hid, b * wide : (b + 1) * wide] = rows.astype(BF16)
-
-
-def prepare_kernel(
-    nz, xl, w1_ref, w3_ref, zk_ref, sp_ref,
-    t1_ref, t3_ref, z_ref, sr_ref, si_ref, dft_ref, fwd_ref, inv_ref,
-):
-    channels, hid = w1_ref.shape[3:]
+            for r in range(half):
+                block = banded(spread, place, r - 1)
+                lanes = slice(b * wide, (b + 1) * wide)
+                if r < half - 1:
+                    t2_ref[0, d * tall + r * hid : d * tall + (r + 1) * hid, lanes] = block
+                if r > 0:
+                    t2_ref[1, d * tall + (r - 1) * hid : d * tall + r * hid, lanes] = block
+                if 0 < r < 3:
+                    top = (d * 2 + r - 1) * hid
+                    t2m_ref[top : top + hid, b * 4 * hid : (b + 1) * 4 * hid] = block[:, : 4 * hid]
+    channels = w1_ref.shape[3]
     taps, cols = 9 * channels, t1_ref.shape[1]
     pick = (iota((taps, cols), 0) == iota((taps, cols), 1) // nz).astype(BF16)
     spread = []
@@ -209,23 +229,19 @@
         )
     place = iota((hid, cols), 1) % nz
     for z in range(nz):
-        rows = jnp.zeros((hid, cols), F32)
-        for a in range(3):
-            rows = jnp.where(place == z + a - 1, spread[a], rows)
-        t1_ref[z * hid : (z + 1) * hid, :] = rows.astype(BF16)
+        t1_ref[z * hid : (z + 1) * hid, :] = banded(spread, place, z - 1)
     rows3, cols3 = t3_ref.shape
     taps = 9 * w3_ref.shape[3]
     repeat = (iota((rows3, taps), 0) // nz == iota((rows3, taps), 1)).astype(BF16)
     pick = (iota((hid, cols3), 0) == iota((hid, cols3), 1) % hid).astype(BF16)
     offset = iota((rows3, cols3), 1) // hid - iota((rows3, cols3), 0) % nz
-    total = jnp.zeros((rows3, cols3), F32)
+    spread = []
     for a in range(3):
         stack = jnp.concatenate(
             [w3_ref[a, b, d].astype(F32) for b in range(3) for d in range(3)], axis=0
         ).astype(BF16)
-        spread = mm(mm(repeat, stack).astype(BF16), pick)
-        total = jnp.where(offset == a - 1, spread, total)
-    t3_ref[...] = total.astype(BF16)
+        spread.append(mm(mm(repeat, stack).astype(BF16), pick))
+    t3_ref[...] = banded(spread, offset, -1)
     kr, ki = zk_ref[0], zk_ref[1]
     top = jnp.concatenate([kr, -ki], axis=1)
     bottom = jnp.concatenate([ki, kr], axis=1)
@@ -241,13 +257,6 @@
             precision=lax.Precision.HIGHEST,
             preferred_element_type=F32,
         )
-    nx, ny = inv_ref.shape[0], dft_ref.shape[1]
-    dft_ref[...] = dft_parts(iota((ny, ny), 0), iota((ny, ny), 1), ny, 0)
-    first, second = iota((nx, nx), 0), iota((nx, nx), 1)
-    inv_ref[...] = dft_parts(first, second, nx, 1, 1.0 / (nx * ny))
-    count = nx // xl
-    second = lax.rem(second, count) * xl + second // count
-    fwd_ref[...] = dft_parts(first, second, nx, 1)
 
 
 def polarised(column, con_ref):
@@ -266,68 +275,93 @@
 
 
 def corrector_kernel(
-    con_ref, own_ref, chip_ref, far_ref, t1_ref, t2_ref, t3_ref, z_ref, dft_ref, out_ref,
+    con_ref, own_ref, first_ref, second_ref, t1_ref, t2_ref, t2m_ref, t3_ref, z_ref, dft_ref, out_ref,
     feat, hid1, hid2,
 ):
     nz, xl, ny = own_ref.shape[1:]
-    even = lax.axis_index("gx") % 2 == 0
-
-    def column(x):
-        if x < 0:
-            x += xl
-            return [jnp.where(even, far_ref[i, :, x, :], chip_ref[i, :, x, :]) for i in range(3)]
-        if x >= xl:
-            x -= xl
-            return [jnp.where(even, chip_ref[i, :, x, :], far_ref[i, :, x, :]) for i in range(3)]
-        return [own_ref[i, :, x, :] for i in range(3)]
-
+    columns = [(second_ref, x) for x in range(2)]
+    columns += [(first_ref, x) for x in range(xl)]
+    columns += [(own_ref, x) for x in range(xl)]
     own = []
-    deep = 12 * nz
-    for place in range(xl + 6):
-        re, im, pol_re, pol_im = polarised(column(place - 3), con_ref)
-        if 0 <= place - 3 < xl:
+    depth = 12 * nz
+    half = hid1.shape[0] // 2
+    hid = 2 * half // nz
+    tall = half - hid
+    deep = 2 * nz
+    last = {}
+
+    def features(place):
+        ref, x = columns[place]
+        re, im, pol_re, pol_im = polarised([ref[i, :, x, :] for i in range(3)], con_ref)
+        if 3 <= place < xl + 3:
             own.append(jnp.concatenate([pol_re, pol_im], axis=0))
         stack = jnp.concatenate([re, im, pol_re, pol_im], axis=0)
         rolled = [pltpu.roll(stack, 1, 1), stack, pltpu.roll(stack, ny - 1, 1)]
-        feat[place * deep : (place + 1) * deep, :] = jnp.concatenate(rolled, axis=0).astype(BF16)
-    for j in range(0, xl + 4, 2):
-        window = [feat[(j + i) * deep : (j + i + 3) * deep, :] for i in range(2)]
-        made = mm(t1_ref[...], jnp.concatenate(window, axis=1))
+        feat[place * depth : (place + 1) * depth, :] = jnp.concatenate(rolled, axis=0).astype(BF16)
+
+    def first_layer(j):
+        window = [feat[(j + i) * depth : (j + i + 3) * depth, :] for i in range(2)]
+        return mm(t1_ref[...], jnp.concatenate(window, axis=1))
+
+    def first_done(j, made):
         hid1[:, j * ny : (j + 2) * ny] = gelu(made).astype(BF16)
-    rows, half = hid1.shape[0], hid1.shape[0] // 2
-    hid = rows // nz
-    tall = half + hid
-    for j in range(0, xl + 2, 2):
-        sums = []
-        for part, first in ((0, hid), (1, 0)):
-            taps = jnp.concatenate([t2_ref[d, first : first + tall, :] for d in range(3)], axis=0)
-            window = [
-                hid1[part * half : (part + 1) * half, (j + b) * ny : (j + b + 2) * ny] for b in range(3)
-            ]
-            made = mm(taps, jnp.concatenate(window, axis=0))
-            sides = []
-            for i in range(2):
-                lanes = slice(i * ny, (i + 1) * ny)
-                sides.append(
-                    pltpu.roll(made[:tall, lanes], 1, 1)
-                    + made[tall : 2 * tall, lanes]
-                    + pltpu.roll(made[2 * tall :, lanes], ny - 1, 1)
-                )
-            sums.append(jnp.concatenate(sides, axis=1))
-        low, high = sums
-        middle = low[half - hid :] + high[: 2 * hid]
-        total = jnp.concatenate([low[: half - hid], middle, high[2 * hid :]], axis=0)
-        hid2[:, j * ny : (j + 2) * ny] = gelu(total).astype(BF16)
-    made = mm(t3_ref[...], hid2[...])
-    deep = 2 * nz
+
+    def tap_sum(weights, top, bottom, j):
+        window = [hid1[top:bottom, (j + b) * ny : (j + b + 2) * ny] for b in range(3)]
+        made = mm(weights, jnp.concatenate(window, axis=0))
+        rows = weights.shape[0] // 3
+        sides = []
+        for i in range(2):
+            lanes = slice(i * ny, (i + 1) * ny)
+            sides.append(
+                pltpu.roll(made[:rows, lanes], 1, 1)
+                + made[rows : 2 * rows, lanes]
+                + pltpu.roll(made[2 * rows :, lanes], ny - 1, 1)
+            )
+        return jnp.concatenate(sides, axis=1)
+
+    def second_layer(j):
+        return [
+            tap_sum(t2_ref[0], 0, half, j),
+            tap_sum(t2m_ref[...], half - 2 * hid, half + 2 * hid, j),
+            tap_sum(t2_ref[1], half, 2 * half, j),
+        ]
+
+    def second_done(j, made):
+        lanes = slice(j * ny, (j + 2) * ny)
+        for top, part in zip((0, tall, tall + 2 * hid), made):
+            hid2[top : top + part.shape[0], lanes] = gelu(part).astype(BF16)
+
+    def third_layer(j):
+        made = mm(t3_ref[...], hid2[:, j * ny : (j + 2) * ny])
+        last[j], last[j + 1] = made[:, :ny], made[:, ny:]
+
+    for place in range(4):
+        features(place)
+    pairs1, pairs2 = range(0, xl + 4, 2), range(0, xl + 2, 2)
+    made1, made2 = {}, {}
+    for j in pairs1:
+        made1[j] = first_layer(j)
+        for place in range(j + 4, min(j + 6, xl + 6)):
+            features(place)
+        if j >= 2:
+            first_done(j - 2, made1.pop(j - 2))
+    first_done(pairs1[-1], made1.pop(pairs1[-1]))
+    for j in pairs2:
+        made2[j] = second_layer(j)
+        if j >= 2:
+            second_done(j - 2, made2.pop(j - 2))
+            third_layer(j - 2)
+    second_done(pairs2[-1], made2.pop(pairs2[-1]))
+    third_layer(pairs2[-1])
     sources = []
     for x in range(xl):
         parts = []
         for d in range(3):
             total = None
             for b in range(3):
-                first = (b * 3 + d) * deep
-                piece = made[first : first + deep, (x + b) * ny : (x + b + 1) * ny]
+                top = (b * 3 + d) * deep
+                piece = last[x + b][top : top + deep]
                 total = piece if total is None else total + piece
             parts.append(total)
         correction = pltpu.roll(parts[0], 1, 1) + parts[1] + pltpu.roll(parts[2], ny - 1, 1)
@@ -382,42 +416,42 @@
     hid = w_middle.shape[0]
     ql, nx = spectral.shape[1], spectral.shape[2]
     struct = jax.ShapeDtypeStruct
-    last = lax.broadcasted_iota(jnp.int32, (3, 1, 1, 1), 0) == 2
-    own = jnp.where(last, material.astype(F32)[None], jnp.pad(incident, ((0, 1),) + ((0, 0),) * 3))
-    chip = lax.ppermute(own, "gx", [(i, i ^ 1) for i in range(count)])
-    pairs = [(i, (i + 1) % count) for i in range(1, count, 2)]
-    far = lax.ppermute(own, "gx", pairs + [(j, i) for i, j in pairs])
+    still = ((0, 0),) * 3
+    own = jnp.pad(material[None], ((2, 0),) + still).astype(F32) + jnp.pad(incident, ((0, 1),) + still)
+    second = lax.ppermute(own[:, :, xl - 2 :], "gx", [(i, (i + 2) % count) for i in range(count)])
+    first = lax.ppermute(own, "gx", [(i, (i + 1) % count) for i in range(count)])
     lanes = 2 * nz * xl
-    t2 = call(
-        functools.partial(middle_kernel, nz),
-        struct((3, (nz // 2 + 2) * hid, 3 * nz // 2 * hid), BF16),
-        (jnp.transpose(w_middle, (2, 3, 4, 0, 1)),),
+    dft, fwd, inv = call(
+        functools.partial(table_kernel, xl, 3),
+        [struct((6 * ny, ny), BF16), struct((nx, 6 * nx), BF16), struct((nx, 6 * nx), BF16)],
+        (),
         flops=10**9,
     )
-    t1, t3, zmat, sr, si, dft, fwd, inv = call(
-        functools.partial(prepare_kernel, nz, xl),
+    t1, t2, t2m, t3, zmat, sr, si = call(
+        functools.partial(weight_kernel, nz),
         [
             struct((nz * hid, 36 * nz), BF16),
+            struct((2, 3 * (nz // 2 - 1) * hid, 3 * nz // 2 * hid), BF16),
+            struct((6 * hid, 12 * hid), BF16),
             struct((18 * nz, nz * hid), BF16),
             struct((4 * nz, 6 * nz), BF16),
             struct((nx, ql * 2 * nz), F32),
             struct((nx, ql * 2 * nz), F32),
-            struct((6 * ny, ny), BF16),
-            struct((nx, 6 * nx), BF16),
-            struct((nx, 6 * nx), BF16),
         ],
         (
             jnp.transpose(w_first, (2, 3, 4, 1, 0)),
+            jnp.transpose(w_middle, (2, 3, 4, 0, 1)),
             jnp.transpose(w_last, (2, 3, 4, 0, 1)),
             z_kernel,
             spectral,
+            dft,
         ),
         flops=10**9,
     )
     spectrum = call(
         corrector_kernel,
         struct((count, ql, lanes), F32),
-        (jnp.transpose(contrast), own, chip, far, t1, t2, t3, zmat, dft),
+        (jnp.transpose(contrast), own, first, second, t1, t2, t2m, t3, zmat, dft),
         scratch=[
             pltpu.VMEM(((xl + 6) * 12 * nz, ny), BF16),
             pltpu.VMEM((nz * hid, (xl + 4) * ny), BF16),

time: 40.2 us -> 36.4 us (0.905)
  waiting for transfers between devices: 0.01 us -> 4.15 us
  starting transfers between devices: 6.44 us -> 3.09 us
  blocking collectives: 21.2 us -> 19.1 us
  local copies, waits for them, and re-layouts: 1.27 us -> 0.05 us
  other arithmetic: 1.69 us -> 0.9 us
    ppermute x2, waiting for transfers between devices: 0.01 us -> 4.15 us  [the longest x1 4.14 us: lane_device(): lax.ppermute(own[:, :, xl - 2:], 'gx', [(i, (i + 2) % count) for i in ran...]
    ppermute x2, starting transfers between devices: 6.44 us -> 3.09 us  [the longest x1 2.56 us: lane_device(): lax.ppermute(own[:, :, xl - 2:], 'gx', [(i, (i + 2) % count) for i in ran...]
    all_to_all x1, blocking collectives: 12.1 us -> 9.98 us  [lane_device(): piece = lax.all_to_all(spectrum, 'gx', 0, 0, tiled=True)]
    unnamed x12, local copies, waits for them, and re-layouts: 1.27 us -> 0.02 us
    select_n x1 -> x0, other arithmetic: 0.92 us -> none  [lane_device(): jnp.where(last, material.astype(F32)[None], jnp.pad(incident, ((0, 1),) +...]
    add x0 -> x1, other arithmetic: none -> 0.9 us  [lane_device(): jnp.pad(material[None], ((2, 0),) + still).astype(F32)]
    convert_element_type x1 -> x0, other arithmetic: 0.76 us -> none  [lane_device(): material.astype(F32)[None]]
  transfers between devices with their start and end apart: 2 -> 2, of which waited for: 0 -> 1; matrix products, arithmetic and copies ran while one was open for 0% -> 0% of each run, Pallas kernels for 4% -> 5%
where the time goes in v3:
time: 36.4 us; the launch traced here: 36.2 us
  blocking collectives  19.1 us (52%)
  Pallas kernels  8.85 us (24%)
  waiting for transfers between devices  4.15 us (11%)
  starting transfers between devices  3.09 us (8%)
  other arithmetic  0.9 us (2%)
    all_to_all x1, blocking collectives, lane_device(): piece = lax.all_to_all(spectrum, 'gx', 0, 0, tiled=True)  9.98 us
    all_to_all x1, blocking collectives, lane_device(): rows = lax.all_to_all(spread, 'gx', 0, 0, tiled=True)  9.1 us
    pallas_call x5, Pallas kernels, call(): pl.pallas_call(kernel, out_shape=out_shapes, in_specs=specs, out_specs=vm...  8.85 us
    ppermute x1, waiting for transfers between devices, lane_device(): lax.ppermute(own[:, :, xl - 2:], 'gx', [(i, (i + 2) % count) for i in ran...  4.14 us
    ppermute x1, starting transfers between devices, lane_device(): lax.ppermute(own[:, :, xl - 2:], 'gx', [(i, (i + 2) % count) for i in ran...  2.56 us
    add x1, other arithmetic, lane_device(): jnp.pad(material[None], ((2, 0),) + still).astype(F32)  0.9 us
  transfers between devices with their start and end apart: 2, of which 1 were waited for; matrix products, arithmetic and copies ran while one was open for 0% of the time, Pallas kernels for 5%

profile of v3, /device:TPU:0, one launch (start us, length us, event | category | flops | bytes accessed | tf_op | source)
XLA Modules:
  0.0 36.2 jit_solution(434857475625250501)
XLA Ops:
  0.0 0.0 copy-start.4
  0.0 0.0 copy-start.2
  0.0 0.0 copy-start.3
  0.0 0.0 copy-start
  0.0 0.0 copy-start.1
  0.0 0.9 %pad_add_fusion.own_ref.inc_ref = f32[3,16,4,128]{3,2,1,0:T(4,128)S(1)} fusion(f32[2,16,4,128]{3,2,1,0:T(4,128)} %param.8, s32[1,16,4,128]{3,2,1,0:T(4,128)} %bitcast.9), kind=kLoop, calls=%fused_computation | loop fusion | flops 49152 | bytes 196608 | tf_op jit(solution)/shard_map/add | solution.py:420
  0.9 0.5 %collective-permute-start = (f32[3,16,4,128]{3,2,1,0:T(4,128)S(1)}, f32[3,16,4,128]{3,2,1,0:T(4,128)S(1)}, u32[]{:S(2)}, u32[]{:S(2)}) collective-permute-start(f32[3,16,4,128]{3,2,1,0:T(4,128)S(1)} %pad_add_fusion.own_ref.inc_ref), channel_id=1, source_target_pairs={{0,1},{1,2},{2,3},{3,4},{4,5},{5,6},{6,7},{7,8},{8,9},{9,10},{10,1... | collective-permute-start | bytes 294920 | tf_op jit(solution)/shard_map/ppermute | solution.py:422
  1.5 2.6 %collective-permute-start.1 = (f32[3,16,2,128]{3,2,1,0:T(2,128)S(1)}, f32[3,16,2,128]{3,2,1,0:T(2,128)S(1)}, u32[]{:S(2)}, u32[]{:S(2)}) collective-permute-start(f32[3,16,2,128]{3,2,1,0:T(2,128)S(1)} %slice.4), channel_id=1, source_target_pairs={{0,2},{1,3},{2,4},{3,5},{4,6},{5,7},{6,8},{7,9},{8,10},{9,11},{10,... | collective-permute-start | bytes 147464 | tf_op jit(solution)/shard_map/ppermute | solution.py:421
  4.0 0.4 %shard_map.82 = (bf16[768,128]{1,0:T(8,128)(2,1)S(1)}, bf16[128,768]{1,0:T(8,128)(2,1)S(1)}, bf16[128,768]{1,0:T(8,128)(2,1)S(1)}) custom-call(), custom_call_target="tpu_custom_call" | custom-call | flops 1000000000 | bytes 4194304 | tf_op jit(solution)/shard_map/pallas_call | solution.py:402
  4.5 0.0 copy-start.5
  4.5 0.0 copy-done.4
  4.5 0.0 copy-done.2
  4.5 0.0 copy-done.3
  4.5 0.0 copy-done
  4.5 0.0 copy-done.1
  4.5 1.5 %shard_map.83 = (bf16[512,576]{1,0:T(8,128)(2,1)S(1)}, bf16[2,672,768]{2,1,0:T(8,128)(2,1)S(1)}, bf16[192,384]{1,0:T(8,128)(2,1)S(1)}, bf16[288,512]{1,0:T(8,128...) custom-call(bf16[3,3,3,4,32]{4,3,2,1,0:T(4,128)(2,1)S(1)} %bitcast.6, ...), custom_call_target="tpu_custom_call" | custom-call | flops 1000000000 | bytes 4194304 | tf_op jit(solution)/shard_map/pallas_call | solution.py:402
  6.1 4.1 %collective-permute-done.1.second_ref = f32[3,16,2,128]{3,2,1,0:T(2,128)S(1)} collective-permute-done((f32[3,16,2,128]{3,2,1,0:T(2,128)S(1)}, f32[3,16,2,128]{3,2,1,0:T(2,128)S(1)}, u32[]{:S(2)}, u32[]{:S(2)}) %collective-permute-start.1) | collective-permute-done | bytes 49184 | tf_op jit(solution)/shard_map/ppermute | solution.py:421
  10.2 0.0 collective-permute-done.first_ref
  10.2 0.0 copy-done.5
  10.2 5.1 %shard_map.84 = f32[32,4,128]{2,1,0:T(4,128)S(1)} custom-call(f32[2,8]{1,0:T(2,128)S(1)} %bitcast.8, f32[3,16,4,128]{3,2,1,0:T(4,128)S(1)} %pad_add_fusion.own_ref.inc_ref, f32[3,16,4,128]{3,2,1,0:T(4,128)S(1)} %collective-permute-done.first_ref, f32[3,16,2,128]{3,2,1,0:T(2,128)S(1)} %collective-permute-done.1.second_ref, ...), custom_call_target="tpu_custom_call" | custom-call | flops 1000000000 | bytes 4194304 | tf_op jit(solution)/shard_map/pallas_call | solution.py:402
  15.3 10.0 %all_to_all.10.in_ref = f32[32,4,128]{2,1,0:T(4,128)S(1)} all-to-all(f32[32,4,128]{2,1,0:T(4,128)S(1)} %shard_map.84), channel_id=1, replica_groups=mesh['grp'=1,'gx'=32,'gy'=1] {'gx'}, dimensions={0} | all-to-all | bytes 131072 | tf_op jit(solution)/shard_map/all_to_all | solution.py:463
  25.3 0.7 %shard_map.85 = f32[32,4,128]{2,1,0:T(4,128)S(1)} custom-call(f32[32,4,128]{2,1,0:T(4,128)S(1)} %all_to_all.10.in_ref, bf16[128,768]{1,0:T(8,128)(2,1)S(1)} %get-tuple-element.21.fwd_ref.tab_ref, bf16[128,768]{1,0:T(8,128)(2,1)S(1)} %get-tuple-element.22.inv_ref, f32[128,128]{1,0:T(8,128)S(1)} %get-tuple-element.23.sr_ref, ...), custom_call_target="tpu_custom_call" | custom-call | flops 100000000 | bytes 4194304 | tf_op jit(solution)/shard_map/pallas_call | solution.py:402
  26.0 9.1 %all_to_all.11.in_ref = f32[32,4,128]{2,1,0:T(4,128)S(1)} all-to-all(f32[32,4,128]{2,1,0:T(4,128)S(1)} %shard_map.85), channel_id=1, replica_groups=mesh['grp'=1,'gx'=32,'gy'=1] {'gx'}, dimensions={0} | all-to-all | bytes 131072 | tf_op jit(solution)/shard_map/all_to_all | solution.py:470
  35.1 1.1 %shard_map.86 = f32[2,16,4,128]{3,2,1,0:T(4,128)} custom-call(f32[32,4,128]{2,1,0:T(4,128)S(1)} %all_to_all.11.in_ref, bf16[128,768]{1,0:T(8,128)(2,1)S(1)} %get-tuple-element.21.fwd_ref.tab_ref, f32[3,16,4,128]{3,2,1,0:T(4,128)S(1)} %pad_add_fusion.own_ref.inc_ref), custom_call_target="tpu_custom_call" | custom-call | flops 100000000 | bytes 4194304 | tf_op jit(solution)/shard_map/pallas_call | solution.py:402
  (1 shorter events, 0.0 us)
Async XLA Ops:
  0.0 4.5 %copy-start.4 = (f32[2,4,128]{2,1,0:T(4,128)S(1)}, f32[2,4,128]{2,1,0:T(4,128)}, u32[]{:S(2)}) copy-start(f32[2,4,128]{2,1,0:T(4,128)} %sp_ref.1) | copy-start | bytes 12292
  0.0 4.5 %copy-start.2 = (f32[2,16,16]{2,1,0:T(8,128)S(1)}, f32[2,16,16]{2,1,0:T(8,128)}, u32[]{:S(2)}) copy-start(f32[2,16,16]{2,1,0:T(8,128)} %zk_ref.1) | copy-start | bytes 6148
  0.0 4.5 %copy-start.3 = (bf16[2,32,3,3,3]{1,0,4,3,2:T(2,128)(2,1)S(1)}, bf16[2,32,3,3,3]{1,0,4,3,2:T(2,128)(2,1)}, u32[]{:S(2)}) copy-start(bf16[2,32,3,3,3]{1,0,4,3,2:T(2,128)(2,1)} %param.13) | copy-start | bytes 10372
  0.0 4.5 %copy-start = (bf16[32,32,3,3,3]{1,0,4,3,2:T(8,128)(2,1)S(1)}, bf16[32,32,3,3,3]{1,0,4,3,2:T(8,128)(2,1)}, u32[]{:S(2)}) copy-start(bf16[32,32,3,3,3]{1,0,4,3,2:T(8,128)(2,1)} %param.12) | copy-start | bytes 165892
  0.0 4.5 %copy-start.1 = (bf16[32,4,3,3,3]{0,1,4,3,2:T(4,128)(2,1)S(1)}, bf16[32,4,3,3,3]{0,1,4,3,2:T(4,128)(2,1)}, u32[]{:S(2)}) copy-start(bf16[32,4,3,3,3]{0,1,4,3,2:T(4,128)(2,1)} %param.11) | copy-start | bytes 20740
  0.9 9.3 %collective-permute-start = (f32[3,16,4,128]{3,2,1,0:T(4,128)S(1)}, f32[3,16,4,128]{3,2,1,0:T(4,128)S(1)}, u32[]{:S(2)}, u32[]{:S(2)}) collective-permute-start(f32[3,16,4,128]{3,2,1,0:T(4,128)S(1)} %pad_add_fusion.own_ref.inc_ref), channel_id=1, source_target_pairs={{0,1},{1,2},{2,3},{3,4},{4,5},{5,6},{6,7},{7,8},{8,9},{9,10},{10,1... | collective-permute-start | bytes 294920 | tf_op jit(solution)/shard_map/ppermute | solution.py:422
  1.5 8.7 %collective-permute-start.1 = (f32[3,16,2,128]{3,2,1,0:T(2,128)S(1)}, f32[3,16,2,128]{3,2,1,0:T(2,128)S(1)}, u32[]{:S(2)}, u32[]{:S(2)}) collective-permute-start(f32[3,16,2,128]{3,2,1,0:T(2,128)S(1)} %slice.4), channel_id=1, source_target_pairs={{0,2},{1,3},{2,4},{3,5},{4,6},{5,7},{6,8},{7,9},{8,10},{9,11},{10,... | collective-permute-start | bytes 147464 | tf_op jit(solution)/shard_map/ppermute | solution.py:421
  4.5 5.7 %copy-start.5 = (f32[8,2]{0,1:T(2,128)S(1)}, f32[8,2]{0,1:T(2,128)}, u32[]{:S(2)}) copy-start(f32[8,2]{0,1:T(2,128)} %param.10) | copy-start | bytes 196

commit v4 on v3

--- a/solution.py
+++ b/solution.py
@@ -174,6 +174,24 @@
             total = moved if total is None else jnp.where(block == q, moved, total)
         rows.append(total)
     return jnp.concatenate(rows, axis=0)
+
+
+def pack_kernel(own_ref, planes_ref, whole_ref):
+    xl = own_ref.shape[2]
+    for x in range(xl):
+        for i in range(3):
+            values = own_ref[i, :, x, :]
+            high, low = split(values)
+            planes_ref[3 * x + i] = values
+            whole_ref[3 * x + i] = high
+            if x > 0 and i < 2:
+                whole_ref[3 * xl + 2 * (x - 1) + i] = low
+
+
+def near_kernel(whole_ref, near_ref):
+    count = near_ref.shape[0]
+    top = 3 * (whole_ref.shape[0] + 2) // 5 - count
+    near_ref[...] = whole_ref[top : top + count]
 
 
 def table_kernel(xl, shift, dft_ref, fwd_ref, inv_ref):
@@ -278,10 +296,14 @@
     con_ref, own_ref, first_ref, second_ref, t1_ref, t2_ref, t2m_ref, t3_ref, z_ref, dft_ref, out_ref,
     feat, hid1, hid2,
 ):
-    nz, xl, ny = own_ref.shape[1:]
-    columns = [(second_ref, x) for x in range(2)]
-    columns += [(first_ref, x) for x in range(xl)]
-    columns += [(own_ref, x) for x in range(xl)]
+    nz, ny = own_ref.shape[1:]
+    xl = own_ref.shape[0] // 3
+    columns = [[second_ref[3 * x + i].astype(F32) for i in range(3)] for x in range(2)]
+    columns += [[first_ref[3 * x + i].astype(F32) for i in range(3)] for x in range(xl)]
+    columns += [[own_ref[3 * x + i] for i in range(3)] for x in range(xl)]
+    for x in range(1, xl):
+        for i in range(2):
+            columns[x + 2][i] += first_ref[3 * xl + 2 * (x - 1) + i].astype(F32)
     own = []
     depth = 12 * nz
     half = hid1.shape[0] // 2
@@ -291,8 +313,7 @@
     last = {}
 
     def features(place):
-        ref, x = columns[place]
-        re, im, pol_re, pol_im = polarised([ref[i, :, x, :] for i in range(3)], con_ref)
+        re, im, pol_re, pol_im = polarised(columns[place], con_ref)
         if 3 <= place < xl + 3:
             own.append(jnp.concatenate([pol_re, pol_im], axis=0))
         stack = jnp.concatenate([re, im, pol_re, pol_im], axis=0)
@@ -418,8 +439,15 @@
     struct = jax.ShapeDtypeStruct
     still = ((0, 0),) * 3
     own = jnp.pad(material[None], ((2, 0),) + still).astype(F32) + jnp.pad(incident, ((0, 1),) + still)
-    second = lax.ppermute(own[:, :, xl - 2 :], "gx", [(i, (i + 2) % count) for i in range(count)])
-    first = lax.ppermute(own, "gx", [(i, (i + 1) % count) for i in range(count)])
+    planes, whole = call(
+        pack_kernel,
+        [struct((3 * xl, nz, ny), F32), struct((5 * xl - 2, nz, ny), BF16)],
+        (own,),
+        flops=10**6,
+    )
+    near = call(near_kernel, struct((6, nz, ny), BF16), (whole,), flops=10**6)
+    first = lax.ppermute(whole, "gx", [(i, (i + 1) % count) for i in range(count)])
+    second = lax.ppermute(near, "gx", [(i, (i + 2) % count) for i in range(count)])
     lanes = 2 * nz * xl
     dft, fwd, inv = call(
         functools.partial(table_kernel, xl, 3),
@@ -451,7 +479,7 @@
     spectrum = call(
         corrector_kernel,
         struct((count, ql, lanes), F32),
-        (jnp.transpose(contrast), own, first, second, t1, t2, t2m, t3, zmat, dft),
+        (jnp.transpose(contrast), planes, first, second, t1, t2, t2m, t3, zmat, dft),
         scratch=[
             pltpu.VMEM(((xl + 6) * 12 * nz, ny), BF16),
             pltpu.VMEM((nz * hid, (xl + 4) * ny), BF16),

time: 36.4 us -> 35.4 us (0.973)
  Pallas kernels: 8.85 us -> 8.4 us
    pallas_call x5 -> x7, Pallas kernels: 8.85 us -> 8.4 us  [call(): pl.pallas_call(kernel, out_shape=out_shapes, in_specs=specs, out_specs=vm...]
where the time goes in v4:
time: 35.4 us; the launch traced here: 35.2 us
  blocking collectives  18.9 us (53%)
  Pallas kernels  8.4 us (24%)
  waiting for transfers between devices  3.8 us (11%)
  starting transfers between devices  3.1 us (9%)
  other arithmetic  0.9 us (3%)
    all_to_all x1, blocking collectives, lane_device(): piece = lax.all_to_all(spectrum, 'gx', 0, 0, tiled=True)  9.81 us
    all_to_all x1, blocking collectives, lane_device(): rows = lax.all_to_all(spread, 'gx', 0, 0, tiled=True)  9.1 us
    pallas_call x7, Pallas kernels, call(): pl.pallas_call(kernel, out_shape=out_shapes, in_specs=specs, out_specs=vm...  8.4 us
    ppermute x1, waiting for transfers between devices, lane_device(): lax.ppermute(near, 'gx', [(i, (i + 2) % count) for i in range(count)])  3.8 us
    ppermute x1, starting transfers between devices, lane_device(): lax.ppermute(near, 'gx', [(i, (i + 2) % count) for i in range(count)])  2.56 us
    add x1, other arithmetic, lane_device(): jnp.pad(material[None], ((2, 0),) + still).astype(F32)  0.9 us
  transfers between devices with their start and end apart: 2, of which 1 were waited for; matrix products, arithmetic and copies ran while one was open for 0% of the time, Pallas kernels for 5%

profile of v4, /device:TPU:0, one launch (start us, length us, event | category | flops | bytes accessed | tf_op | source)
XLA Modules:
  0.0 35.2 jit_solution(10063555420953114607)
XLA Ops:
  0.0 0.0 copy-start.2
  0.0 0.0 copy-start.3
  0.0 0.0 copy-start
  0.0 0.0 copy-start.1
  0.0 0.9 %pad_add_fusion.own_ref.inc_ref = f32[3,16,4,128]{3,2,1,0:T(4,128)S(1)} fusion(f32[2,16,4,128]{3,2,1,0:T(4,128)} %param.8, s32[1,16,4,128]{3,2,1,0:T(4,128)} %bitcast.9), kind=kLoop, calls=%fused_computation | loop fusion | flops 49152 | bytes 196608 | tf_op jit(solution)/shard_map/add | solution.py:441
  0.9 0.2 shard_map.82
  1.2 0.5 %collective-permute-start = (bf16[18,16,128]{2,1,0:T(8,128)(2,1)S(1)}, bf16[18,16,128]{2,1,0:T(8,128)(2,1)S(1)}, u32[]{:S(2)}, u32[]{:S(2)}) collective-permute-start(bf16[18,16,128]{2,1,0:T(8,128)(2,1)S(1)} %get-tuple-element.18.whole_ref), channel_id=1, source_target_pairs={{0,1},{1,2},{2,3},{3,4},{4,5},{5,6},{6,7},{7,8},{8,9},{9,10},{10,1... | collective-permute-start | bytes 221192 | tf_op jit(solution)/shard_map/ppermute | solution.py:449
  1.7 2.6 %collective-permute-start.1 = (bf16[6,16,128]{2,1,0:T(8,128)(2,1)S(1)}, bf16[6,16,128]{2,1,0:T(8,128)(2,1)S(1)}, u32[]{:S(2)}, u32[]{:S(2)}) collective-permute-start(bf16[6,16,128]{2,1,0:T(8,128)(2,1)S(1)} %shard_map.83), channel_id=1, source_target_pairs={{0,2},{1,3},{2,4},{3,5},{4,6},{5,7},{6,8},{7,9},{8,10},{9,11},{10,... | collective-permute-start | bytes 73736 | tf_op jit(solution)/shard_map/ppermute | solution.py:450
  4.3 0.4 %shard_map.84 = (bf16[768,128]{1,0:T(8,128)(2,1)S(1)}, bf16[128,768]{1,0:T(8,128)(2,1)S(1)}, bf16[128,768]{1,0:T(8,128)(2,1)S(1)}) custom-call(), custom_call_target="tpu_custom_call" | custom-call | flops 1000000000 | bytes 4194304 | tf_op jit(solution)/shard_map/pallas_call | solution.py:423
  4.7 0.0 copy-start.5
  4.7 0.0 copy-done.4
  4.7 0.0 copy-done.2
  4.7 0.0 copy-done.3
  4.7 0.0 copy-done
  4.7 0.0 copy-done.1
  4.7 1.5 %shard_map.85 = (bf16[512,576]{1,0:T(8,128)(2,1)S(1)}, bf16[2,672,768]{2,1,0:T(8,128)(2,1)S(1)}, bf16[192,384]{1,0:T(8,128)(2,1)S(1)}, bf16[288,512]{1,0:T(8,128...) custom-call(bf16[3,3,3,4,32]{4,3,2,1,0:T(4,128)(2,1)S(1)} %bitcast.6, ...), custom_call_target="tpu_custom_call" | custom-call | flops 1000000000 | bytes 4194304 | tf_op jit(solution)/shard_map/pallas_call | solution.py:423
  6.3 3.8 %collective-permute-done.1.second_ref = bf16[6,16,128]{2,1,0:T(8,128)(2,1)S(1)} collective-permute-done((bf16[6,16,128]{2,1,0:T(8,128)(2,1)S(1)}, bf16[6,16,128]{2,1,0:T(8,128)(2,1)S(1)}, u32[]{:S(2)}, u32[]{:S(2)}) %collective-permute-start.1) | collective-permute-done | bytes 24608 | tf_op jit(solution)/shard_map/ppermute | solution.py:450
  10.1 0.0 collective-permute-done.first_ref
  10.1 0.0 copy-done.5
  10.1 4.4 %shard_map.86 = f32[32,4,128]{2,1,0:T(4,128)S(1)} custom-call(f32[2,8]{1,0:T(2,128)S(1)} %bitcast.8, f32[12,16,128]{2,1,0:T(8,128)S(1)} %get-tuple-element.17.own_ref, bf16[18,16,128]{2,1,0:T(8,128)(2,1)S(1)} %collective-permute-done.first_ref, bf16[6,16,128]{2,1,0:T(8,128)(2,1)S(1)} %collective-permute-done.1.second_ref, ...), custom_call_target="tpu_custom_call" | custom-call | flops 1000000000 | bytes 4194304 | tf_op jit(solution)/shard_map/pallas_call | solution.py:423
  14.5 9.8 %all_to_all.10.in_ref = f32[32,4,128]{2,1,0:T(4,128)S(1)} all-to-all(f32[32,4,128]{2,1,0:T(4,128)S(1)} %shard_map.86), channel_id=1, replica_groups=mesh['grp'=1,'gx'=32,'gy'=1] {'gx'}, dimensions={0} | all-to-all | bytes 131072 | tf_op jit(solution)/shard_map/all_to_all | solution.py:491
  24.3 0.7 %shard_map.87 = f32[32,4,128]{2,1,0:T(4,128)S(1)} custom-call(f32[32,4,128]{2,1,0:T(4,128)S(1)} %all_to_all.10.in_ref, bf16[128,768]{1,0:T(8,128)(2,1)S(1)} %get-tuple-element.25.fwd_ref.tab_ref, bf16[128,768]{1,0:T(8,128)(2,1)S(1)} %get-tuple-element.26.inv_ref, f32[128,128]{1,0:T(8,128)S(1)} %get-tuple-element.27.sr_ref, ...), custom_call_target="tpu_custom_call" | custom-call | flops 100000000 | bytes 4194304 | tf_op jit(solution)/shard_map/pallas_call | solution.py:423
  25.0 9.1 %all_to_all.11.in_ref = f32[32,4,128]{2,1,0:T(4,128)S(1)} all-to-all(f32[32,4,128]{2,1,0:T(4,128)S(1)} %shard_map.87), channel_id=1, replica_groups=mesh['grp'=1,'gx'=32,'gy'=1] {'gx'}, dimensions={0} | all-to-all | bytes 131072 | tf_op jit(solution)/shard_map/all_to_all | solution.py:498
  34.1 1.1 %shard_map.88 = f32[2,16,4,128]{3,2,1,0:T(4,128)} custom-call(f32[32,4,128]{2,1,0:T(4,128)S(1)} %all_to_all.11.in_ref, bf16[128,768]{1,0:T(8,128)(2,1)S(1)} %get-tuple-element.25.fwd_ref.tab_ref, f32[3,16,4,128]{3,2,1,0:T(4,128)S(1)} %pad_add_fusion.own_ref.inc_ref), custom_call_target="tpu_custom_call" | custom-call | flops 100000000 | bytes 4194304 | tf_op jit(solution)/shard_map/pallas_call | solution.py:423
  (2 shorter events, 0.0 us)
Async XLA Ops:
  0.0 4.7 %copy-start.4 = (f32[2,4,128]{2,1,0:T(4,128)S(1)}, f32[2,4,128]{2,1,0:T(4,128)}, u32[]{:S(2)}) copy-start(f32[2,4,128]{2,1,0:T(4,128)} %sp_ref.1) | copy-start | bytes 12292
  0.0 4.7 %copy-start.2 = (f32[2,16,16]{2,1,0:T(8,128)S(1)}, f32[2,16,16]{2,1,0:T(8,128)}, u32[]{:S(2)}) copy-start(f32[2,16,16]{2,1,0:T(8,128)} %zk_ref.1) | copy-start | bytes 6148
  0.0 4.7 %copy-start.3 = (bf16[2,32,3,3,3]{1,0,4,3,2:T(2,128)(2,1)S(1)}, bf16[2,32,3,3,3]{1,0,4,3,2:T(2,128)(2,1)}, u32[]{:S(2)}) copy-start(bf16[2,32,3,3,3]{1,0,4,3,2:T(2,128)(2,1)} %param.13) | copy-start | bytes 10372
  0.0 4.7 %copy-start = (bf16[32,32,3,3,3]{1,0,4,3,2:T(8,128)(2,1)S(1)}, bf16[32,32,3,3,3]{1,0,4,3,2:T(8,128)(2,1)}, u32[]{:S(2)}) copy-start(bf16[32,32,3,3,3]{1,0,4,3,2:T(8,128)(2,1)} %param.12) | copy-start | bytes 165892
  0.0 4.7 %copy-start.1 = (bf16[32,4,3,3,3]{0,1,4,3,2:T(4,128)(2,1)S(1)}, bf16[32,4,3,3,3]{0,1,4,3,2:T(4,128)(2,1)}, u32[]{:S(2)}) copy-start(bf16[32,4,3,3,3]{0,1,4,3,2:T(4,128)(2,1)} %param.11) | copy-start | bytes 20740
  1.2 8.9 %collective-permute-start = (bf16[18,16,128]{2,1,0:T(8,128)(2,1)S(1)}, bf16[18,16,128]{2,1,0:T(8,128)(2,1)S(1)}, u32[]{:S(2)}, u32[]{:S(2)}) collective-permute-start(bf16[18,16,128]{2,1,0:T(8,128)(2,1)S(1)} %get-tuple-element.18.whole_ref), channel_id=1, source_target_pairs={{0,1},{1,2},{2,3},{3,4},{4,5},{5,6},{6,7},{7,8},{8,9},{9,10},{10,1... | collective-permute-start | bytes 221192 | tf_op jit(solution)/shard_map/ppermute | solution.py:449
  1.7 8.4 %collective-permute-start.1 = (bf16[6,16,128]{2,1,0:T(8,128)(2,1)S(1)}, bf16[6,16,128]{2,1,0:T(8,128)(2,1)S(1)}, u32[]{:S(2)}, u32[]{:S(2)}) collective-permute-start(bf16[6,16,128]{2,1,0:T(8,128)(2,1)S(1)} %shard_map.83), channel_id=1, source_target_pairs={{0,2},{1,3},{2,4},{3,5},{4,6},{5,7},{6,8},{7,9},{8,10},{9,11},{10,... | collective-permute-start | bytes 73736 | tf_op jit(solution)/shard_map/ppermute | solution.py:450
  4.7 5.4 %copy-start.5 = (f32[8,2]{0,1:T(2,128)S(1)}, f32[8,2]{0,1:T(2,128)}, u32[]{:S(2)}) copy-start(f32[8,2]{0,1:T(2,128)} %param.10) | copy-start | bytes 196

commit v5 on v4

--- a/solution.py
+++ b/solution.py
@@ -176,22 +176,37 @@
     return jnp.concatenate(rows, axis=0)
 
 
+def spread_classes(con_ref, shape):
+    return [
+        [jnp.broadcast_to(con_ref[part : part + 1, k : k + 1], shape) for part in range(2)]
+        for k in range(con_ref.shape[1])
+    ]
+
+
+def polarised(column, classes):
+    re, im, cells = column
+    chi_re = jnp.zeros_like(re)
+    chi_im = jnp.zeros_like(re)
+    for k, (class_re, class_im) in enumerate(classes):
+        here = cells == float(k)
+        chi_re = jnp.where(here, class_re, chi_re)
+        chi_im = jnp.where(here, class_im, chi_im)
+    return [re, im, chi_re * re - chi_im * im, chi_re * im + chi_im * re]
+
+
 def pack_kernel(own_ref, planes_ref, whole_ref):
-    xl = own_ref.shape[2]
-    for x in range(xl):
+    for x in range(own_ref.shape[2]):
         for i in range(3):
             values = own_ref[i, :, x, :]
             high, low = split(values)
             planes_ref[3 * x + i] = values
-            whole_ref[3 * x + i] = high
-            if x > 0 and i < 2:
-                whole_ref[3 * xl + 2 * (x - 1) + i] = low
+            whole_ref[5 * x + i] = high
+            if i < 2:
+                whole_ref[5 * x + 3 + i] = low
 
 
 def near_kernel(whole_ref, near_ref):
-    count = near_ref.shape[0]
-    top = 3 * (whole_ref.shape[0] + 2) // 5 - count
-    near_ref[...] = whole_ref[top : top + count]
+    near_ref[...] = whole_ref[whole_ref.shape[0] - near_ref.shape[0] :]
 
 
 def table_kernel(xl, shift, dft_ref, fwd_ref, inv_ref):
@@ -204,6 +219,12 @@
     fwd_ref[...] = dft_parts(first, second, nx, 1)
 
 
+def features_of(column, ny):
+    stack = jnp.concatenate([plane.astype(F32) for plane in column], axis=0)
+    rolled = [pltpu.roll(stack, 1, 1), stack, pltpu.roll(stack, ny - 1, 1)]
+    return jnp.concatenate(rolled, axis=0).astype(BF16)
+
+
 def banded(spread, place, start):
     rows = jnp.zeros_like(spread[0])
     for a in range(3):
@@ -212,8 +233,8 @@
 
 
 def weight_kernel(
-    nz, w1_ref, w2_ref, w3_ref, zk_ref, sp_ref, dft_ref,
-    t1_ref, t2_ref, t2m_ref, t3_ref, z_ref, sr_ref, si_ref,
+    nz, con_ref, planes_ref, w1_ref, w2_ref, w3_ref, zk_ref, sp_ref, dft_ref,
+    t1_ref, t2_ref, t2m_ref, t3_ref, z_ref, sr_ref, si_ref, feat_ref, hid_ref, pol_ref,
 ):
     hid = w2_ref.shape[3]
     half = nz // 2
@@ -249,17 +270,18 @@
     for z in range(nz):
         t1_ref[z * hid : (z + 1) * hid, :] = banded(spread, place, z - 1)
     rows3, cols3 = t3_ref.shape
-    taps = 9 * w3_ref.shape[3]
-    repeat = (iota((rows3, taps), 0) // nz == iota((rows3, taps), 1)).astype(BF16)
+    taps = rows3 // nz
     pick = (iota((hid, cols3), 0) == iota((hid, cols3), 1) % hid).astype(BF16)
-    offset = iota((rows3, cols3), 1) // hid - iota((rows3, cols3), 0) % nz
+    offset = iota((nz, cols3), 1) // hid - iota((nz, cols3), 0)
     spread = []
     for a in range(3):
         stack = jnp.concatenate(
             [w3_ref[a, b, d].astype(F32) for b in range(3) for d in range(3)], axis=0
         ).astype(BF16)
-        spread.append(mm(mm(repeat, stack).astype(BF16), pick))
-    t3_ref[...] = banded(spread, offset, -1)
+        spread.append(mm(stack, pick))
+    for r in range(taps):
+        rows = [jnp.broadcast_to(spread[a][r : r + 1], (nz, cols3)) for a in range(3)]
+        t3_ref[r * nz : (r + 1) * nz, :] = banded(rows, offset, -1)
     kr, ki = zk_ref[0], zk_ref[1]
     top = jnp.concatenate([kr, -ki], axis=1)
     bottom = jnp.concatenate([ki, kr], axis=1)
@@ -275,17 +297,16 @@
             precision=lax.Precision.HIGHEST,
             preferred_element_type=F32,
         )
-
-
-def polarised(column, con_ref):
-    re, im, cells = column
-    chi_re = jnp.zeros_like(re)
-    chi_im = jnp.zeros_like(re)
-    for k in range(con_ref.shape[1]):
-        here = cells == float(k)
-        chi_re = jnp.where(here, con_ref[0, k], chi_re)
-        chi_im = jnp.where(here, con_ref[1, k], chi_im)
-    return re, im, chi_re * re - chi_im * im, chi_re * im + chi_im * re
+    ny = planes_ref.shape[2]
+    depth = 12 * nz
+    classes = spread_classes(con_ref, planes_ref.shape[1:])
+    for x in range(planes_ref.shape[0] // 3):
+        column = polarised([planes_ref[3 * x + i] for i in range(3)], classes)
+        if x == 0:
+            pol_ref[...] = jnp.concatenate(column[2:], axis=0)
+        feat_ref[x * depth : (x + 1) * depth, :] = features_of(column, ny)
+    window = [feat_ref[i * depth : (i + 3) * depth, :] for i in range(2)]
+    hid_ref[...] = gelu(mm(t1_ref[...], jnp.concatenate(window, axis=1))).astype(BF16)
 
 
 def gelu(values):
@@ -293,42 +314,51 @@
 
 
 def corrector_kernel(
-    con_ref, own_ref, first_ref, second_ref, t1_ref, t2_ref, t2m_ref, t3_ref, z_ref, dft_ref, out_ref,
-    feat, hid1, hid2,
+    con_ref, first_ref, second_ref, own_feat, own_hid, own_pol, t1_ref, t2_ref, t2m_ref, t3_ref,
+    z_ref, dft_ref, out_ref, feat, hid1, hid2,
 ):
-    nz, ny = own_ref.shape[1:]
-    xl = own_ref.shape[0] // 3
-    columns = [[second_ref[3 * x + i].astype(F32) for i in range(3)] for x in range(2)]
-    columns += [[first_ref[3 * x + i].astype(F32) for i in range(3)] for x in range(xl)]
-    columns += [[own_ref[3 * x + i] for i in range(3)] for x in range(xl)]
-    for x in range(1, xl):
-        for i in range(2):
-            columns[x + 2][i] += first_ref[3 * xl + 2 * (x - 1) + i].astype(F32)
-    own = []
+    nz, ny = first_ref.shape[1:]
+    xl = own_feat.shape[0] // (12 * nz)
+    ahead = xl + 2
     depth = 12 * nz
     half = hid1.shape[0] // 2
     hid = 2 * half // nz
     tall = half - hid
     deep = 2 * nz
+    classes = spread_classes(con_ref, (nz, ny))
+    own = {}
     last = {}
 
     def features(place):
-        re, im, pol_re, pol_im = polarised(columns[place], con_ref)
-        if 3 <= place < xl + 3:
-            own.append(jnp.concatenate([pol_re, pol_im], axis=0))
-        stack = jnp.concatenate([re, im, pol_re, pol_im], axis=0)
-        rolled = [pltpu.roll(stack, 1, 1), stack, pltpu.roll(stack, ny - 1, 1)]
-        feat[place * depth : (place + 1) * depth, :] = jnp.concatenate(rolled, axis=0).astype(BF16)
+        ref, top = (second_ref, 5 * place) if place < 2 else (first_ref, 5 * (place - 2))
+        high_re, high_im, cells, low_re, low_im = [ref[top + i].astype(F32) for i in range(5)]
+        column = polarised([high_re + low_re, high_im + low_im, cells], classes)
+        if place > 2:
+            own[place - 3] = jnp.concatenate(column[2:], axis=0)
+        column = [high_re, high_im] + column[2:]
+        feat[place * depth : (place + 1) * depth, :] = features_of(column, ny)
+
+    def feature_rows(place):
+        if place < ahead:
+            return feat[place * depth : (place + 1) * depth, :]
+        return own_feat[(place - ahead) * depth : (place - ahead + 1) * depth, :]
 
     def first_layer(j):
-        window = [feat[(j + i) * depth : (j + i + 3) * depth, :] for i in range(2)]
+        window = [jnp.concatenate([feature_rows(j + i + b) for b in range(3)], axis=0) for i in range(2)]
         return mm(t1_ref[...], jnp.concatenate(window, axis=1))
 
     def first_done(j, made):
         hid1[:, j * ny : (j + 2) * ny] = gelu(made).astype(BF16)
 
+    def hidden(place, top, bottom):
+        if place < ahead:
+            return hid1[top:bottom, place * ny : (place + 1) * ny]
+        return own_hid[top:bottom, (place - ahead) * ny : (place - ahead + 1) * ny]
+
     def tap_sum(weights, top, bottom, j):
-        window = [hid1[top:bottom, (j + b) * ny : (j + b + 2) * ny] for b in range(3)]
+        window = [
+            jnp.concatenate([hidden(j + b + i, top, bottom) for i in range(2)], axis=1) for b in range(3)
+        ]
         made = mm(weights, jnp.concatenate(window, axis=0))
         rows = weights.shape[0] // 3
         sides = []
@@ -357,26 +387,7 @@
         made = mm(t3_ref[...], hid2[:, j * ny : (j + 2) * ny])
         last[j], last[j + 1] = made[:, :ny], made[:, ny:]
 
-    for place in range(4):
-        features(place)
-    pairs1, pairs2 = range(0, xl + 4, 2), range(0, xl + 2, 2)
-    made1, made2 = {}, {}
-    for j in pairs1:
-        made1[j] = first_layer(j)
-        for place in range(j + 4, min(j + 6, xl + 6)):
-            features(place)
-        if j >= 2:
-            first_done(j - 2, made1.pop(j - 2))
-    first_done(pairs1[-1], made1.pop(pairs1[-1]))
-    for j in pairs2:
-        made2[j] = second_layer(j)
-        if j >= 2:
-            second_done(j - 2, made2.pop(j - 2))
-            third_layer(j - 2)
-    second_done(pairs2[-1], made2.pop(pairs2[-1]))
-    third_layer(pairs2[-1])
-    sources = []
-    for x in range(xl):
+    def source(x):
         parts = []
         for d in range(3):
             total = None
@@ -385,13 +396,42 @@
                 piece = last[x + b][top : top + deep]
                 total = piece if total is None else total + piece
             parts.append(total)
-        correction = pltpu.roll(parts[0], 1, 1) + parts[1] + pltpu.roll(parts[2], ny - 1, 1)
-        sources.append(own[x] + correction)
-    lifted = mm(z_ref[...], right_split(jnp.concatenate(sources, axis=1)))
-    plain = [lifted[:deep, x * ny : (x + 1) * ny] for x in range(xl)]
-    turned = [lifted[deep:, x * ny : (x + 1) * ny] for x in range(xl)]
-    both = jnp.concatenate([jnp.concatenate(plain, axis=0), jnp.concatenate(turned, axis=0)], axis=1)
-    spectrum = mm(left_split(both), dft_ref[...])
+        return own[x] + (pltpu.roll(parts[0], 1, 1) + parts[1] + pltpu.roll(parts[2], ny - 1, 1))
+
+    def transformed(places):
+        lifted = mm(z_ref[...], right_split(jnp.concatenate([source(x) for x in places], axis=1)))
+        plain, turned = [], []
+        for i in range(len(places)):
+            plain.append(lifted[:deep, i * ny : (i + 1) * ny])
+            turned.append(lifted[deep:, i * ny : (i + 1) * ny])
+        both = [jnp.concatenate(plain, axis=0), jnp.concatenate(turned, axis=0)]
+        return mm(left_split(jnp.concatenate(both, axis=1)), dft_ref[...])
+
+    own[xl - 1] = own_pol[...]
+    made1, made2 = {}, {}
+    features(4)
+    features(5)
+    made1[4] = first_layer(4)
+    features(2)
+    features(3)
+    made1[2] = first_layer(2)
+    first_done(4, made1[4])
+    made2[4] = second_layer(4)
+    features(0)
+    features(1)
+    made1[0] = first_layer(0)
+    first_done(2, made1[2])
+    made2[2] = second_layer(2)
+    first_done(0, made1[0])
+    second_done(4, made2[4])
+    third_layer(4)
+    made2[0] = second_layer(0)
+    second_done(2, made2[2])
+    third_layer(2)
+    later = transformed([2, 3])
+    second_done(0, made2[0])
+    third_layer(0)
+    spectrum = jnp.concatenate([transformed([0, 1]), later], axis=0)
     out_ref[...] = jnp.transpose(spectrum).reshape(out_ref.shape)
 
 
@@ -404,26 +444,23 @@
     out_ref[...] = mm(inv_ref[...], right_split(both)).reshape(out_ref.shape)
 
 
-def finish_kernel(nz, in_ref, tab_ref, inc_ref, out_ref):
+def finish_kernel(nz, in_ref, tab_ref, planes_ref, out_ref):
     values = swap_blocks(in_ref, in_ref.shape[1])
     both = jnp.concatenate([values, other_part(values, nz, -1.0)], axis=0)
     field = jnp.transpose(mm(tab_ref[...], right_split(both)))
-    for x in range(inc_ref.shape[2]):
+    for x in range(out_ref.shape[2]):
         for part in range(2):
             first = (2 * x + part) * nz
-            out_ref[part, :, x, :] = inc_ref[part, :, x, :] + field[first : first + nz, :]
-
-
-def call(kernel, out_shapes, args, scratch=(), smem=(), flops=0):
+            out_ref[part, :, x, :] = planes_ref[3 * x + part] + field[first : first + nz, :]
+
+
+def call(kernel, out_shapes, args, scratch=(), flops=0):
     vmem = pl.BlockSpec(memory_space=pltpu.VMEM)
-    specs = [vmem] * len(args)
-    for i in smem:
-        specs[i] = pl.BlockSpec(memory_space=pltpu.SMEM)
     single = not isinstance(out_shapes, list)
     return pl.pallas_call(
         kernel,
         out_shape=out_shapes,
-        in_specs=specs,
+        in_specs=[vmem] * len(args),
         out_specs=vmem if single else [vmem] * len(out_shapes),
         scratch_shapes=scratch,
         compiler_params=pltpu.CompilerParams(vmem_limit_bytes=VMEM_LIMIT),
@@ -439,13 +476,14 @@
     struct = jax.ShapeDtypeStruct
     still = ((0, 0),) * 3
     own = jnp.pad(material[None], ((2, 0),) + still).astype(F32) + jnp.pad(incident, ((0, 1),) + still)
+    classes = jnp.transpose(contrast)
     planes, whole = call(
         pack_kernel,
-        [struct((3 * xl, nz, ny), F32), struct((5 * xl - 2, nz, ny), BF16)],
+        [struct((3 * xl, nz, ny), F32), struct((5 * xl, nz, ny), BF16)],
         (own,),
         flops=10**6,
     )
-    near = call(near_kernel, struct((6, nz, ny), BF16), (whole,), flops=10**6)
+    near = call(near_kernel, struct((10, nz, ny), BF16), (whole,), flops=10**6)
     first = lax.ppermute(whole, "gx", [(i, (i + 1) % count) for i in range(count)])
     second = lax.ppermute(near, "gx", [(i, (i + 2) % count) for i in range(count)])
     lanes = 2 * nz * xl
@@ -455,7 +493,7 @@
         (),
         flops=10**9,
     )
-    t1, t2, t2m, t3, zmat, sr, si = call(
+    t1, t2, t2m, t3, zmat, sr, si, feat, hidden, pol = call(
         functools.partial(weight_kernel, nz),
         [
             struct((nz * hid, 36 * nz), BF16),
@@ -465,8 +503,13 @@
             struct((4 * nz, 6 * nz), BF16),
             struct((nx, ql * 2 * nz), F32),
             struct((nx, ql * 2 * nz), F32),
+            struct((xl * 12 * nz, ny), BF16),
+            struct((nz * hid, 2 * ny), BF16),
+            struct((2 * nz, ny), F32),
         ],
         (
+            classes,
+            planes,
             jnp.transpose(w_first, (2, 3, 4, 1, 0)),
             jnp.transpose(w_middle, (2, 3, 4, 0, 1)),
             jnp.transpose(w_last, (2, 3, 4, 0, 1)),
@@ -479,13 +522,12 @@
     spectrum = call(
         corrector_kernel,
         struct((count, ql, lanes), F32),
-        (jnp.transpose(contrast), planes, first, second, t1, t2, t2m, t3, zmat, dft),
+        (classes, first, second, feat, hidden, pol, t1, t2, t2m, t3, zmat, dft),
         scratch=[
-            pltpu.VMEM(((xl + 6) * 12 * nz, ny), BF16),
-            pltpu.VMEM((nz * hid, (xl + 4) * ny), BF16),
+            pltpu.VMEM(((xl + 2) * 12 * nz, ny), BF16),
+            pltpu.VMEM((nz * hid, (xl + 2) * ny), BF16),
             pltpu.VMEM((nz * hid, (xl + 2) * ny), BF16),
         ],
-        smem=(0,),
         flops=10**9,
     )
     piece = lax.all_to_all(spectrum, "gx", 0, 0, tiled=True)
@@ -499,7 +541,7 @@
     return call(
         functools.partial(finish_kernel, nz),
         struct(incident.shape, F32),
-        (rows, fwd, own),
+        (rows, fwd, planes),
         flops=10**8,
     )
 

time: 35.4 us -> 35.3 us (level)
  Pallas kernels: 8.4 us -> 7.69 us
  waiting for transfers between devices: 3.8 us -> 4.27 us
    pallas_call x7, Pallas kernels: 8.4 us -> 7.69 us  [call(): pl.pallas_call(kernel, out_shape=out_shapes, in_specs=[vmem] * len(args),...]
    ppermute x1, waiting for transfers between devices: 3.8 us -> 4.27 us  [lane_device(): lax.ppermute(near, 'gx', [(i, (i + 2) % count) for i in range(count)])]
where the time goes in v5:
time: 35.3 us; the launch traced here: 35.2 us
  blocking collectives  19.1 us (54%)
  Pallas kernels  7.69 us (22%)
  waiting for transfers between devices  4.27 us (12%)
  starting transfers between devices  3.1 us (9%)
  other arithmetic  0.9 us (3%)
    all_to_all x1, blocking collectives, lane_device(): piece = lax.all_to_all(spectrum, 'gx', 0, 0, tiled=True)  9.99 us
    all_to_all x1, blocking collectives, lane_device(): rows = lax.all_to_all(spread, 'gx', 0, 0, tiled=True)  9.1 us
    pallas_call x7, Pallas kernels, call(): pl.pallas_call(kernel, out_shape=out_shapes, in_specs=[vmem] * len(args),...  7.69 us
    ppermute x1, waiting for transfers between devices, lane_device(): lax.ppermute(near, 'gx', [(i, (i + 2) % count) for i in range(count)])  4.27 us
    ppermute x1, starting transfers between devices, lane_device(): lax.ppermute(near, 'gx', [(i, (i + 2) % count) for i in range(count)])  2.56 us
    add x1, other arithmetic, lane_device(): jnp.pad(material[None], ((2, 0),) + still).astype(F32)  0.9 us
  transfers between devices with their start and end apart: 2, of which 1 were waited for; matrix products, arithmetic and copies ran while one was open for 0% of the time, Pallas kernels for 5%

profile of v5, /device:TPU:0, one launch (start us, length us, event | category | flops | bytes accessed | tf_op | source)
XLA Modules:
  0.0 35.2 jit_solution(1053730654387688932)
XLA Ops:
  0.0 0.0 copy-start.1
  0.0 0.0 copy-start.2
  0.0 0.0 copy-start.3
  0.0 0.0 copy-start.4
  0.0 0.0 copy-start.5
  0.0 0.9 %pad_add_fusion.own_ref = f32[3,16,4,128]{3,2,1,0:T(4,128)S(1)} fusion(f32[2,16,4,128]{3,2,1,0:T(4,128)} %param.8, s32[1,16,4,128]{3,2,1,0:T(4,128)} %bitcast.10), kind=kLoop, calls=%fused_computation | loop fusion | flops 49152 | bytes 196608 | tf_op jit(solution)/shard_map/add | solution.py:478
  0.9 0.2 shard_map.82
  1.2 0.5 %collective-permute-start = (bf16[20,16,128]{2,1,0:T(8,128)(2,1)S(1)}, bf16[20,16,128]{2,1,0:T(8,128)(2,1)S(1)}, u32[]{:S(2)}, u32[]{:S(2)}) collective-permute-start(bf16[20,16,128]{2,1,0:T(8,128)(2,1)S(1)} %get-tuple-element.20.whole_ref), channel_id=1, source_target_pairs={{0,1},{1,2},{2,3},{3,4},{4,5},{5,6},{6,7},{7,8},{8,9},{9,10},{10,1... | collective-permute-start | bytes 245768 | tf_op jit(solution)/shard_map/ppermute | solution.py:487
  1.7 2.6 %collective-permute-start.1 = (bf16[10,16,128]{2,1,0:T(8,128)(2,1)S(1)}, bf16[10,16,128]{2,1,0:T(8,128)(2,1)S(1)}, u32[]{:S(2)}, u32[]{:S(2)}) collective-permute-start(bf16[10,16,128]{2,1,0:T(8,128)(2,1)S(1)} %shard_map.83), channel_id=1, source_target_pairs={{0,2},{1,3},{2,4},{3,5},{4,6},{5,7},{6,8},{7,9},{8,10},{9,11},{10,... | collective-permute-start | bytes 122888 | tf_op jit(solution)/shard_map/ppermute | solution.py:488
  4.3 0.4 %shard_map.84 = (bf16[768,128]{1,0:T(8,128)(2,1)S(1)}, bf16[128,768]{1,0:T(8,128)(2,1)S(1)}, bf16[128,768]{1,0:T(8,128)(2,1)S(1)}) custom-call(), custom_call_target="tpu_custom_call" | custom-call | flops 1000000000 | bytes 4194304 | tf_op jit(solution)/shard_map/pallas_call | solution.py:460
  4.7 0.0 copy-done
  4.7 0.0 copy-done.1
  4.7 0.0 copy-done.2
  4.7 0.0 copy-done.3
  4.8 0.0 copy-done.4
  4.8 0.0 copy-done.5
  4.8 1.2 %shard_map.85 = (bf16[512,576]{1,0:T(8,128)(2,1)S(1)}, bf16[2,672,768]{2,1,0:T(8,128)(2,1)S(1)}, bf16[192,384]{1,0:T(8,128)(2,1)S(1)}, bf16[288,512]{1,0:T(8,128...) custom-call(f32[2,8]{1,0:T(2,128)S(1)} %bitcast.5, ...), custom_call_target="tpu_custom_call" | custom-call | flops 1000000000 | bytes 4194304 | tf_op jit(solution)/shard_map/pallas_call | solution.py:460
  6.0 4.3 %collective-permute-done.1.second_ref = bf16[10,16,128]{2,1,0:T(8,128)(2,1)S(1)} collective-permute-done((bf16[10,16,128]{2,1,0:T(8,128)(2,1)S(1)}, bf16[10,16,128]{2,1,0:T(8,128)(2,1)S(1)}, u32[]{:S(2)}, u32[]{:S(2)}) %collective-permute-start.1) | collective-permute-done | bytes 40992 | tf_op jit(solution)/shard_map/ppermute | solution.py:488
  10.3 0.0 collective-permute-done.first_ref
  10.3 4.0 %shard_map.86 = f32[32,4,128]{2,1,0:T(4,128)S(1)} custom-call(f32[2,8]{1,0:T(2,128)S(1)} %bitcast.6, bf16[20,16,128]{2,1,0:T(8,128)(2,1)S(1)} %collective-permute-done.first_ref, bf16[10,16,128]{2,1,0:T(8,128)(2,1)S(1)} %collective-permute-done.1.second_ref, bf16[768,128]{1,0:T(8,128)(2,1)S(1)} %get-tuple-element.23.own_feat, ...), custom_call_target="tpu_custom_call" | custom-call | flops 1000000000 | bytes 4194304 | tf_op jit(solution)/shard_map/pallas_call | solution.py:460
  14.2 10.0 %all_to_all.10.in_ref = f32[32,4,128]{2,1,0:T(4,128)S(1)} all-to-all(f32[32,4,128]{2,1,0:T(4,128)S(1)} %shard_map.86), channel_id=1, replica_groups=mesh['grp'=1,'gx'=32,'gy'=1] {'gx'}, dimensions={0} | all-to-all | bytes 131072 | tf_op jit(solution)/shard_map/all_to_all | solution.py:533
  24.2 0.7 %shard_map.87 = f32[32,4,128]{2,1,0:T(4,128)S(1)} custom-call(f32[32,4,128]{2,1,0:T(4,128)S(1)} %all_to_all.10.in_ref, bf16[128,768]{1,0:T(8,128)(2,1)S(1)} %get-tuple-element.31.fwd_ref.tab_ref, bf16[128,768]{1,0:T(8,128)(2,1)S(1)} %get-tuple-element.32.inv_ref, f32[128,128]{1,0:T(8,128)S(1)} %get-tuple-element.33.sr_ref, ...), custom_call_target="tpu_custom_call" | custom-call | flops 100000000 | bytes 4194304 | tf_op jit(solution)/shard_map/pallas_call | solution.py:460
  25.0 9.1 %all_to_all.11.in_ref = f32[32,4,128]{2,1,0:T(4,128)S(1)} all-to-all(f32[32,4,128]{2,1,0:T(4,128)S(1)} %shard_map.87), channel_id=1, replica_groups=mesh['grp'=1,'gx'=32,'gy'=1] {'gx'}, dimensions={0} | all-to-all | bytes 131072 | tf_op jit(solution)/shard_map/all_to_all | solution.py:540
  34.1 1.1 %shard_map.88 = f32[2,16,4,128]{3,2,1,0:T(4,128)} custom-call(f32[32,4,128]{2,1,0:T(4,128)S(1)} %all_to_all.11.in_ref, bf16[128,768]{1,0:T(8,128)(2,1)S(1)} %get-tuple-element.31.fwd_ref.tab_ref, f32[12,16,128]{2,1,0:T(8,128)S(1)} %get-tuple-element.21.planes_ref), custom_call_target="tpu_custom_call" | custom-call | flops 100000000 | bytes 4194304 | tf_op jit(solution)/shard_map/pallas_call | solution.py:460
  (2 shorter events, 0.0 us)
Async XLA Ops:
  0.0 4.7 %copy-start = (f32[8,2]{0,1:T(2,128)S(1)}, f32[8,2]{0,1:T(2,128)}, u32[]{:S(2)}) copy-start(f32[8,2]{0,1:T(2,128)} %param.10) | copy-start | bytes 196
  0.0 4.7 %copy-start.1 = (bf16[32,32,3,3,3]{1,0,4,3,2:T(8,128)(2,1)S(1)}, bf16[32,32,3,3,3]{1,0,4,3,2:T(8,128)(2,1)}, u32[]{:S(2)}) copy-start(bf16[32,32,3,3,3]{1,0,4,3,2:T(8,128)(2,1)} %param.12) | copy-start | bytes 165892
  0.0 4.7 %copy-start.2 = (bf16[32,4,3,3,3]{0,1,4,3,2:T(4,128)(2,1)S(1)}, bf16[32,4,3,3,3]{0,1,4,3,2:T(4,128)(2,1)}, u32[]{:S(2)}) copy-start(bf16[32,4,3,3,3]{0,1,4,3,2:T(4,128)(2,1)} %param.11) | copy-start | bytes 20740
  0.0 4.7 %copy-start.3 = (f32[2,16,16]{2,1,0:T(8,128)S(1)}, f32[2,16,16]{2,1,0:T(8,128)}, u32[]{:S(2)}) copy-start(f32[2,16,16]{2,1,0:T(8,128)} %zk_ref.1) | copy-start | bytes 6148
  0.0 4.7 %copy-start.4 = (bf16[2,32,3,3,3]{1,0,4,3,2:T(2,128)(2,1)S(1)}, bf16[2,32,3,3,3]{1,0,4,3,2:T(2,128)(2,1)}, u32[]{:S(2)}) copy-start(bf16[2,32,3,3,3]{1,0,4,3,2:T(2,128)(2,1)} %param.13) | copy-start | bytes 10372
  0.0 4.7 %copy-start.5 = (f32[2,4,128]{2,1,0:T(4,128)S(1)}, f32[2,4,128]{2,1,0:T(4,128)}, u32[]{:S(2)}) copy-start(f32[2,4,128]{2,1,0:T(4,128)} %sp_ref.1) | copy-start | bytes 12292
  1.2 9.1 %collective-permute-start = (bf16[20,16,128]{2,1,0:T(8,128)(2,1)S(1)}, bf16[20,16,128]{2,1,0:T(8,128)(2,1)S(1)}, u32[]{:S(2)}, u32[]{:S(2)}) collective-permute-start(bf16[20,16,128]{2,1,0:T(8,128)(2,1)S(1)} %get-tuple-element.20.whole_ref), channel_id=1, source_target_pairs={{0,1},{1,2},{2,3},{3,4},{4,5},{5,6},{6,7},{7,8},{8,9},{9,10},{10,1... | collective-permute-start | bytes 245768 | tf_op jit(solution)/shard_map/ppermute | solution.py:487
  1.7 8.5 %collective-permute-start.1 = (bf16[10,16,128]{2,1,0:T(8,128)(2,1)S(1)}, bf16[10,16,128]{2,1,0:T(8,128)(2,1)S(1)}, u32[]{:S(2)}, u32[]{:S(2)}) collective-permute-start(bf16[10,16,128]{2,1,0:T(8,128)(2,1)S(1)} %shard_map.83), channel_id=1, source_target_pairs={{0,2},{1,3},{2,4},{3,5},{4,6},{5,7},{6,8},{7,9},{8,10},{9,11},{10,... | collective-permute-start | bytes 122888 | tf_op jit(solution)/shard_map/ppermute | solution.py:488

commit v6 on v5

--- a/solution.py
+++ b/solution.py
@@ -127,11 +127,11 @@
     return total * angle
 
 
-def dft_parts(rows, cols, length, axis, scale=1.0):
+def dft_parts(rows, cols, length, axis, along, scale=1.0):
     steps = lax.rem(rows * cols, length)
     later = lax.rem(steps + 3 * length // 4, length)
     high, low = split(jnp.concatenate([cosine(steps, length), cosine(later, length)], axis=axis) * scale)
-    return jnp.concatenate([high, high, low], axis=axis)
+    return jnp.concatenate([high, high, low], axis=along)
 
 
 def left_split(values):
@@ -152,27 +152,29 @@
     return lax.broadcasted_iota(jnp.int32, shape, dim)
 
 
-def other_part(values, nz, sign):
-    lanes = values.shape[1]
+def turned(values, nz):
     real = (iota(values.shape, 1) // nz) % 2 == 0
-    ahead = pltpu.roll(values, lanes - nz, 1)
-    behind = pltpu.roll(values, nz, 1)
-    return jnp.where(real, sign * ahead, -sign * behind)
+    ahead = pltpu.roll(values, values.shape[1] - nz, 1)
+    return jnp.where(real, -ahead, pltpu.roll(values, nz, 1))
 
 
 def swap_blocks(ref, count):
     pieces = [ref[:, q, :] for q in range(count)]
-    lanes = pieces[0].shape[1]
-    inner = lanes // count
+    inner = pieces[0].shape[1] // count
     block = iota(pieces[0].shape, 1) // inner
-    rows = []
-    for x in range(count):
-        total = None
-        for q in range(count):
-            shift = ((q - x) * inner) % lanes
-            moved = pltpu.roll(pieces[q], shift, 1) if shift else pieces[q]
-            total = moved if total is None else jnp.where(block == q, moved, total)
-        rows.append(total)
+    places = [block == q for q in range(count)]
+
+    def chosen(options):
+        total = options[0]
+        for place, option in zip(places[1:], options[1:]):
+            total = jnp.where(place, option, total)
+        return total
+
+    moved = []
+    for step in range(count):
+        total = chosen([pieces[(x + step) % count] for x in range(count)])
+        moved.append(pltpu.roll(total, step * inner, 1) if step else total)
+    rows = [chosen([moved[(q - x) % count] for q in range(count)]) for x in range(count)]
     return jnp.concatenate(rows, axis=0)
 
 
@@ -183,40 +185,35 @@
     ]
 
 
-def polarised(column, classes):
-    re, im, cells = column
+def unpacked(ref, x, classes):
+    high_re, high_im, cells, low_re, low_im = [ref[x, i].astype(F32) for i in range(5)]
+    re, im = high_re + low_re, high_im + low_im
     chi_re = jnp.zeros_like(re)
     chi_im = jnp.zeros_like(re)
     for k, (class_re, class_im) in enumerate(classes):
         here = cells == float(k)
         chi_re = jnp.where(here, class_re, chi_re)
         chi_im = jnp.where(here, class_im, chi_im)
-    return [re, im, chi_re * re - chi_im * im, chi_re * im + chi_im * re]
-
-
-def pack_kernel(own_ref, planes_ref, whole_ref):
+    return [high_re, high_im, chi_re * re - chi_im * im, chi_re * im + chi_im * re]
+
+
+def pack_kernel(own_ref, whole_ref):
     for x in range(own_ref.shape[2]):
         for i in range(3):
-            values = own_ref[i, :, x, :]
-            high, low = split(values)
-            planes_ref[3 * x + i] = values
-            whole_ref[5 * x + i] = high
+            high, low = split(own_ref[i, :, x, :])
+            whole_ref[x, i] = high
             if i < 2:
-                whole_ref[5 * x + 3 + i] = low
-
-
-def near_kernel(whole_ref, near_ref):
-    near_ref[...] = whole_ref[whole_ref.shape[0] - near_ref.shape[0] :]
+                whole_ref[x, i + 3] = low
 
 
 def table_kernel(xl, shift, dft_ref, fwd_ref, inv_ref):
     nx, ny = inv_ref.shape[0], dft_ref.shape[1]
-    dft_ref[...] = dft_parts(iota((ny, ny), 0), iota((ny, ny), 1), ny, 0)
+    dft_ref[...] = dft_parts(iota((ny, ny), 0), iota((ny, ny), 1), ny, 0, 0)
     first, second = iota((nx, nx), 0), iota((nx, nx), 1)
-    inv_ref[...] = dft_parts(lax.rem(first + shift, nx), second, nx, 1, 1.0 / (nx * ny))
+    inv_ref[...] = dft_parts(lax.rem(first + shift, nx), second, nx, 1, 1, 1.0 / (nx * ny))
     count = nx // xl
     second = lax.rem(second, count) * xl + second // count
-    fwd_ref[...] = dft_parts(first, second, nx, 1)
+    fwd_ref[...] = dft_parts(first, second, nx, 0, 1)
 
 
 def features_of(column, ny):
@@ -233,7 +230,7 @@
 
 
 def weight_kernel(
-    nz, con_ref, planes_ref, w1_ref, w2_ref, w3_ref, zk_ref, sp_ref, dft_ref,
+    nz, con_ref, whole_ref, w1_ref, w2_ref, w3_ref, zk_ref, sp_ref, dft_ref,
     t1_ref, t2_ref, t2m_ref, t3_ref, z_ref, sr_ref, si_ref, feat_ref, hid_ref, pol_ref,
 ):
     hid = w2_ref.shape[3]
@@ -297,11 +294,11 @@
             precision=lax.Precision.HIGHEST,
             preferred_element_type=F32,
         )
-    ny = planes_ref.shape[2]
+    ny = whole_ref.shape[3]
     depth = 12 * nz
-    classes = spread_classes(con_ref, planes_ref.shape[1:])
-    for x in range(planes_ref.shape[0] // 3):
-        column = polarised([planes_ref[3 * x + i] for i in range(3)], classes)
+    classes = spread_classes(con_ref, whole_ref.shape[2:])
+    for x in range(whole_ref.shape[0]):
+        column = unpacked(whole_ref, x, classes)
         if x == 0:
             pol_ref[...] = jnp.concatenate(column[2:], axis=0)
         feat_ref[x * depth : (x + 1) * depth, :] = features_of(column, ny)
@@ -317,7 +314,7 @@
     con_ref, first_ref, second_ref, own_feat, own_hid, own_pol, t1_ref, t2_ref, t2m_ref, t3_ref,
     z_ref, dft_ref, out_ref, feat, hid1, hid2,
 ):
-    nz, ny = first_ref.shape[1:]
+    nz, ny = first_ref.shape[2:]
     xl = own_feat.shape[0] // (12 * nz)
     ahead = xl + 2
     depth = 12 * nz
@@ -330,12 +327,10 @@
     last = {}
 
     def features(place):
-        ref, top = (second_ref, 5 * place) if place < 2 else (first_ref, 5 * (place - 2))
-        high_re, high_im, cells, low_re, low_im = [ref[top + i].astype(F32) for i in range(5)]
-        column = polarised([high_re + low_re, high_im + low_im, cells], classes)
+        ref, x = (second_ref, place) if place < 2 else (first_ref, place - 2)
+        column = unpacked(ref, x, classes)
         if place > 2:
             own[place - 3] = jnp.concatenate(column[2:], axis=0)
-        column = [high_re, high_im] + column[2:]
         feat[place * depth : (place + 1) * depth, :] = features_of(column, ny)
 
     def feature_rows(place):
@@ -437,21 +432,23 @@
 
 def spectral_kernel(nz, in_ref, fwd_ref, inv_ref, sr_ref, si_ref, out_ref):
     values = swap_blocks(in_ref, in_ref.shape[1])
-    both = jnp.concatenate([values, other_part(values, nz, 1.0)], axis=0)
-    spectrum = mm(fwd_ref[...], right_split(both))
-    scaled = sr_ref[...] * spectrum + si_ref[...] * other_part(spectrum, nz, -1.0)
-    both = jnp.concatenate([scaled, other_part(scaled, nz, -1.0)], axis=0)
-    out_ref[...] = mm(inv_ref[...], right_split(both)).reshape(out_ref.shape)
-
-
-def finish_kernel(nz, in_ref, tab_ref, planes_ref, out_ref):
-    values = swap_blocks(in_ref, in_ref.shape[1])
-    both = jnp.concatenate([values, other_part(values, nz, -1.0)], axis=0)
-    field = jnp.transpose(mm(tab_ref[...], right_split(both)))
+    lanes = values.shape[1]
+    made = mm(fwd_ref[...], right_split(jnp.concatenate([values, turned(values, nz)], axis=1)))
+    nx = made.shape[0] // 2
+    plain = made[:nx, :lanes] - made[nx:, lanes:]
+    other = made[:nx, lanes:] + made[nx:, :lanes]
+    scaled = [sr_ref[...] * plain + si_ref[...] * other, sr_ref[...] * other - si_ref[...] * plain]
+    out_ref[...] = mm(inv_ref[...], right_split(jnp.concatenate(scaled, axis=0))).reshape(out_ref.shape)
+
+
+def finish_kernel(nz, in_ref, tab_ref, inc_ref, out_ref):
+    made = mm(tab_ref[...], right_split(swap_blocks(in_ref, in_ref.shape[1])))
+    ny = made.shape[0] // 2
+    field = jnp.transpose(made[:ny] + turned(made[ny:], nz))
     for x in range(out_ref.shape[2]):
         for part in range(2):
             first = (2 * x + part) * nz
-            out_ref[part, :, x, :] = planes_ref[3 * x + part] + field[first : first + nz, :]
+            out_ref[part, :, x, :] = inc_ref[part, :, x, :] + field[first : first + nz, :]
 
 
 def call(kernel, out_shapes, args, scratch=(), flops=0):
@@ -474,22 +471,16 @@
     hid = w_middle.shape[0]
     ql, nx = spectral.shape[1], spectral.shape[2]
     struct = jax.ShapeDtypeStruct
+    classes = jnp.transpose(contrast)
     still = ((0, 0),) * 3
     own = jnp.pad(material[None], ((2, 0),) + still).astype(F32) + jnp.pad(incident, ((0, 1),) + still)
-    classes = jnp.transpose(contrast)
-    planes, whole = call(
-        pack_kernel,
-        [struct((3 * xl, nz, ny), F32), struct((5 * xl, nz, ny), BF16)],
-        (own,),
-        flops=10**6,
-    )
-    near = call(near_kernel, struct((10, nz, ny), BF16), (whole,), flops=10**6)
+    whole = call(pack_kernel, struct((xl, 5, nz, ny), BF16), (own,), flops=10**6)
     first = lax.ppermute(whole, "gx", [(i, (i + 1) % count) for i in range(count)])
-    second = lax.ppermute(near, "gx", [(i, (i + 2) % count) for i in range(count)])
+    second = lax.ppermute(whole[xl - 2 :], "gx", [(i, (i + 2) % count) for i in range(count)])
     lanes = 2 * nz * xl
     dft, fwd, inv = call(
         functools.partial(table_kernel, xl, 3),
-        [struct((6 * ny, ny), BF16), struct((nx, 6 * nx), BF16), struct((nx, 6 * nx), BF16)],
+        [struct((6 * ny, ny), BF16), struct((2 * nx, 3 * nx), BF16), struct((nx, 6 * nx), BF16)],
         (),
         flops=10**9,
     )
@@ -509,7 +500,7 @@
         ],
         (
             classes,
-            planes,
+            whole,
             jnp.transpose(w_first, (2, 3, 4, 1, 0)),
             jnp.transpose(w_middle, (2, 3, 4, 0, 1)),
             jnp.transpose(w_last, (2, 3, 4, 0, 1)),
@@ -541,7 +532,7 @@
     return call(
         functools.partial(finish_kernel, nz),
         struct(incident.shape, F32),
-        (rows, fwd, planes),
+        (rows, fwd, incident),
         flops=10**8,
     )
 

time: 35.3 us -> 35.3 us (level)
    pallas_call x7 -> x6, Pallas kernels: 7.69 us -> 7.61 us  [call(): pl.pallas_call(kernel, out_shape=out_shapes, in_specs=[vmem] * len(args),...]
where the time goes in v6:
time: 35.3 us; the launch traced here: 35.1 us
  blocking collectives  19.1 us (54%)
  Pallas kernels  7.61 us (22%)
  waiting for transfers between devices  4.27 us (12%)
  starting transfers between devices  3.1 us (9%)
  other arithmetic  0.9 us (3%)
    all_to_all x1, blocking collectives, lane_device(): piece = lax.all_to_all(spectrum, 'gx', 0, 0, tiled=True)  9.99 us
    all_to_all x1, blocking collectives, lane_device(): rows = lax.all_to_all(spread, 'gx', 0, 0, tiled=True)  9.1 us
    pallas_call x6, Pallas kernels, call(): pl.pallas_call(kernel, out_shape=out_shapes, in_specs=[vmem] * len(args),...  7.61 us
    ppermute x1, waiting for transfers between devices, lane_device(): lax.ppermute(whole[xl - 2:], 'gx', [(i, (i + 2) % count) for i in range(c...  4.26 us
    ppermute x1, starting transfers between devices, lane_device(): lax.ppermute(whole[xl - 2:], 'gx', [(i, (i + 2) % count) for i in range(c...  2.56 us
    add x1, other arithmetic, lane_device(): jnp.pad(material[None], ((2, 0),) + still).astype(F32)  0.9 us
  transfers between devices with their start and end apart: 2, of which 1 were waited for; matrix products, arithmetic and copies ran while one was open for 0% of the time, Pallas kernels for 5%

profile of v6, /device:TPU:0, one launch (start us, length us, event | category | flops | bytes accessed | tf_op | source)
XLA Modules:
  0.0 35.1 jit_solution(15847847116745777163)
XLA Ops:
  0.0 0.0 copy-start.2
  0.0 0.0 copy-start.3
  0.0 0.0 copy-start.4
  0.0 0.0 copy-start.6
  0.0 0.9 %pad_add_fusion.own_ref = f32[3,16,4,128]{3,2,1,0:T(4,128)S(1)} fusion(f32[2,16,4,128]{3,2,1,0:T(4,128)} %inc_ref.1, s32[1,16,4,128]{3,2,1,0:T(4,128)} %bitcast.10), kind=kLoop, calls=%fused_computation | loop fusion | flops 49152 | bytes 196608 | tf_op jit(solution)/shard_map/add | solution.py:476
  0.9 0.2 shard_map.82.whole_ref
  1.1 0.5 %collective-permute-start = (bf16[4,5,16,128]{3,2,1,0:T(8,128)(2,1)S(1)}, bf16[4,5,16,128]{3,2,1,0:T(8,128)(2,1)S(1)}, u32[]{:S(2)}, u32[]{:S(2)}) collective-permute-start(bf16[4,5,16,128]{3,2,1,0:T(8,128)(2,1)S(1)} %shard_map.82.whole_ref), channel_id=1, source_target_pairs={{0,1},{1,2},{2,3},{3,4},{4,5},{5,6},{6,7},{7,8},{8,9},{9,10},{10,1... | collective-permute-start | bytes 245768 | tf_op jit(solution)/shard_map/ppermute | solution.py:478
  1.7 2.6 %collective-permute-start.1 = (bf16[2,5,16,128]{3,2,1,0:T(8,128)(2,1)S(1)}, bf16[2,5,16,128]{3,2,1,0:T(8,128)(2,1)S(1)}, u32[]{:S(2)}, u32[]{:S(2)}) collective-permute-start(bf16[2,5,16,128]{3,2,1,0:T(8,128)(2,1)S(1)} %slice.4), channel_id=1, source_target_pairs={{0,2},{1,3},{2,4},{3,5},{4,6},{5,7},{6,8},{7,9},{8,10},{9,11},{10,... | collective-permute-start | bytes 122888 | tf_op jit(solution)/shard_map/ppermute | solution.py:479
  4.2 0.4 %shard_map.83 = (bf16[768,128]{1,0:T(8,128)(2,1)S(1)}, bf16[256,384]{1,0:T(8,128)(2,1)S(1)}, bf16[128,768]{1,0:T(8,128)(2,1)S(1)}) custom-call(), custom_call_target="tpu_custom_call" | custom-call | flops 1000000000 | bytes 4194304 | tf_op jit(solution)/shard_map/pallas_call | solution.py:457
  4.7 0.0 copy-done.1
  4.7 0.0 copy-done.2
  4.7 0.0 copy-done.3
  4.7 0.0 copy-done.4
  4.7 0.0 copy-done.5
  4.7 0.0 copy-done.6
  4.7 1.2 %shard_map.84 = (bf16[512,576]{1,0:T(8,128)(2,1)S(1)}, bf16[2,672,768]{2,1,0:T(8,128)(2,1)S(1)}, bf16[192,384]{1,0:T(8,128)(2,1)S(1)}, bf16[288,512]{1,0:T(8,128...) custom-call(f32[2,8]{1,0:T(2,128)S(1)} %bitcast.5, ...), custom_call_target="tpu_custom_call" | custom-call | flops 1000000000 | bytes 4194304 | tf_op jit(solution)/shard_map/pallas_call | solution.py:457
  6.0 4.3 %collective-permute-done.1.second_ref = bf16[2,5,16,128]{3,2,1,0:T(8,128)(2,1)S(1)} collective-permute-done((bf16[2,5,16,128]{3,2,1,0:T(8,128)(2,1)S(1)}, bf16[2,5,16,128]{3,2,1,0:T(8,128)(2,1)S(1)}, u32[]{:S(2)}, u32[]{:S(2)}) %collective-permute-start.1) | collective-permute-done | bytes 40992 | tf_op jit(solution)/shard_map/ppermute | solution.py:479
  10.2 0.0 collective-permute-done.first_ref
  10.2 3.9 %shard_map.85 = f32[32,4,128]{2,1,0:T(4,128)S(1)} custom-call(f32[2,8]{1,0:T(2,128)S(1)} %bitcast.6, bf16[4,5,16,128]{3,2,1,0:T(8,128)(2,1)S(1)} %collective-permute-done.first_ref, bf16[2,5,16,128]{3,2,1,0:T(8,128)(2,1)S(1)} %collective-permute-done.1.second_ref, bf16[768,128]{1,0:T(8,128)(2,1)S(1)} %get-tuple-element.19.own_feat, ...), custom_call_target="tpu_custom_call" | custom-call | flops 1000000000 | bytes 4194304 | tf_op jit(solution)/shard_map/pallas_call | solution.py:457
  14.2 10.0 %all_to_all.10.in_ref = f32[32,4,128]{2,1,0:T(4,128)S(1)} all-to-all(f32[32,4,128]{2,1,0:T(4,128)S(1)} %shard_map.85), channel_id=1, replica_groups=mesh['grp'=1,'gx'=32,'gy'=1] {'gx'}, dimensions={0} | all-to-all | bytes 131072 | tf_op jit(solution)/shard_map/all_to_all | solution.py:524
  24.2 0.7 %shard_map.86 = f32[32,4,128]{2,1,0:T(4,128)S(1)} custom-call(f32[32,4,128]{2,1,0:T(4,128)S(1)} %all_to_all.10.in_ref, bf16[256,384]{1,0:T(8,128)(2,1)S(1)} %get-tuple-element.27.fwd_ref.tab_ref, bf16[128,768]{1,0:T(8,128)(2,1)S(1)} %get-tuple-element.28.inv_ref, f32[128,128]{1,0:T(8,128)S(1)} %get-tuple-element.29.sr_ref, ...), custom_call_target="tpu_custom_call" | custom-call | flops 100000000 | bytes 4194304 | tf_op jit(solution)/shard_map/pallas_call | solution.py:457
  24.9 9.1 %all_to_all.11.in_ref = f32[32,4,128]{2,1,0:T(4,128)S(1)} all-to-all(f32[32,4,128]{2,1,0:T(4,128)S(1)} %shard_map.86), channel_id=1, replica_groups=mesh['grp'=1,'gx'=32,'gy'=1] {'gx'}, dimensions={0} | all-to-all | bytes 131072 | tf_op jit(solution)/shard_map/all_to_all | solution.py:531
  34.0 0.0 copy-done
  34.0 1.1 %shard_map.87 = f32[2,16,4,128]{3,2,1,0:T(4,128)} custom-call(f32[32,4,128]{2,1,0:T(4,128)S(1)} %all_to_all.11.in_ref, bf16[256,384]{1,0:T(8,128)(2,1)S(1)} %get-tuple-element.27.fwd_ref.tab_ref, f32[2,16,4,128]{3,2,1,0:T(4,128)S(1)} %copy-done), custom_call_target="tpu_custom_call" | custom-call | flops 100000000 | bytes 4194304 | tf_op jit(solution)/shard_map/pallas_call | solution.py:457
  (4 shorter events, 0.0 us)
Async XLA Ops:
  0.0 4.7 %copy-start.1 = (f32[8,2]{0,1:T(2,128)S(1)}, f32[8,2]{0,1:T(2,128)}, u32[]{:S(2)}) copy-start(f32[8,2]{0,1:T(2,128)} %param.10) | copy-start | bytes 196
  0.0 4.7 %copy-start.2 = (bf16[32,32,3,3,3]{1,0,4,3,2:T(8,128)(2,1)S(1)}, bf16[32,32,3,3,3]{1,0,4,3,2:T(8,128)(2,1)}, u32[]{:S(2)}) copy-start(bf16[32,32,3,3,3]{1,0,4,3,2:T(8,128)(2,1)} %param.12) | copy-start | bytes 165892
  0.0 4.7 %copy-start.3 = (bf16[32,4,3,3,3]{0,1,4,3,2:T(4,128)(2,1)S(1)}, bf16[32,4,3,3,3]{0,1,4,3,2:T(4,128)(2,1)}, u32[]{:S(2)}) copy-start(bf16[32,4,3,3,3]{0,1,4,3,2:T(4,128)(2,1)} %param.11) | copy-start | bytes 20740
  0.0 4.7 %copy-start.4 = (f32[2,16,16]{2,1,0:T(8,128)S(1)}, f32[2,16,16]{2,1,0:T(8,128)}, u32[]{:S(2)}) copy-start(f32[2,16,16]{2,1,0:T(8,128)} %zk_ref.1) | copy-start | bytes 6148
  0.0 4.7 %copy-start.5 = (bf16[2,32,3,3,3]{1,0,4,3,2:T(2,128)(2,1)S(1)}, bf16[2,32,3,3,3]{1,0,4,3,2:T(2,128)(2,1)}, u32[]{:S(2)}) copy-start(bf16[2,32,3,3,3]{1,0,4,3,2:T(2,128)(2,1)} %param.13) | copy-start | bytes 10372
  0.0 4.7 %copy-start.6 = (f32[2,4,128]{2,1,0:T(4,128)S(1)}, f32[2,4,128]{2,1,0:T(4,128)}, u32[]{:S(2)}) copy-start(f32[2,4,128]{2,1,0:T(4,128)} %sp_ref.1) | copy-start | bytes 12292
  1.1 9.1 %collective-permute-start = (bf16[4,5,16,128]{3,2,1,0:T(8,128)(2,1)S(1)}, bf16[4,5,16,128]{3,2,1,0:T(8,128)(2,1)S(1)}, u32[]{:S(2)}, u32[]{:S(2)}) collective-permute-start(bf16[4,5,16,128]{3,2,1,0:T(8,128)(2,1)S(1)} %shard_map.82.whole_ref), channel_id=1, source_target_pairs={{0,1},{1,2},{2,3},{3,4},{4,5},{5,6},{6,7},{7,8},{8,9},{9,10},{10,1... | collective-permute-start | bytes 245768 | tf_op jit(solution)/shard_map/ppermute | solution.py:478
  1.7 8.5 %collective-permute-start.1 = (bf16[2,5,16,128]{3,2,1,0:T(8,128)(2,1)S(1)}, bf16[2,5,16,128]{3,2,1,0:T(8,128)(2,1)S(1)}, u32[]{:S(2)}, u32[]{:S(2)}) collective-permute-start(bf16[2,5,16,128]{3,2,1,0:T(8,128)(2,1)S(1)} %slice.4), channel_id=1, source_target_pairs={{0,2},{1,3},{2,4},{3,5},{4,6},{5,7},{6,8},{7,9},{8,10},{9,11},{10,... | collective-permute-start | bytes 122888 | tf_op jit(solution)/shard_map/ppermute | solution.py:479
  10.2 23.7 %copy-start = (f32[2,16,4,128]{3,2,1,0:T(4,128)S(1)}, f32[2,16,4,128]{3,2,1,0:T(4,128)}, u32[]{:S(2)}) copy-start(f32[2,16,4,128]{3,2,1,0:T(4,128)} %inc_ref.1) | copy-start | bytes 196612

commit v7 on v6

--- a/solution.py
+++ b/solution.py
@@ -217,9 +217,33 @@
 
 
 def features_of(column, ny):
-    stack = jnp.concatenate([plane.astype(F32) for plane in column], axis=0)
-    rolled = [pltpu.roll(stack, 1, 1), stack, pltpu.roll(stack, ny - 1, 1)]
-    return jnp.concatenate(rolled, axis=0).astype(BF16)
+    planes = [plane.astype(F32) for plane in column]
+    half = planes[0].shape[0] // 2
+    lower = jnp.concatenate([plane[:half] for plane in planes], axis=0)
+    upper = jnp.concatenate([plane[half:] for plane in planes], axis=0)
+    rows = [plane[half : half + 1] for plane in planes] + [plane[half - 1 : half] for plane in planes]
+    edge = jnp.concatenate(rows, axis=0)
+    made = []
+    for part in (lower, upper, edge):
+        made += [pltpu.roll(part, 1, 1), part, pltpu.roll(part, ny - 1, 1)]
+    return jnp.concatenate(made + [jnp.zeros_like(edge)], axis=0).astype(BF16)
+
+
+def first_product(t1_ref, rows_of, places):
+    made = []
+    depth = t1_ref.shape[2] // 3
+    for part in range(2):
+        pieces = []
+        for place in places:
+            taps = []
+            for b in range(3):
+                rows = rows_of(place + b)
+                edge = 2 * depth - rows.shape[0]
+                main = depth - edge
+                taps += [rows[part * main : (part + 1) * main], rows[2 * main :]]
+            pieces.append(jnp.concatenate(taps, axis=0))
+        made.append(mm(t1_ref[part], jnp.concatenate(pieces, axis=1)))
+    return jnp.concatenate(made, axis=0)
 
 
 def banded(spread, place, start):
@@ -253,8 +277,14 @@
                     top = (d * 2 + r - 1) * hid
                     t2m_ref[top : top + hid, b * 4 * hid : (b + 1) * 4 * hid] = block[:, : 4 * hid]
     channels = w1_ref.shape[3]
-    taps, cols = 9 * channels, t1_ref.shape[1]
-    pick = (iota((taps, cols), 0) == iota((taps, cols), 1) // nz).astype(BF16)
+    taps, cols = 9 * channels, t1_ref.shape[2]
+    depth = cols // 3
+    main = 3 * channels * half
+    row = iota((1, cols), 1) % depth
+    beyond = row - main
+    spot = jnp.where(beyond < 0, row // half, beyond // (2 * channels) * channels + beyond % channels)
+    tap = iota((1, cols), 1) // depth * 3 * channels + spot
+    pick = (iota((taps, cols), 0) == tap).astype(BF16)
     spread = []
     for a in range(3):
         stack = jnp.concatenate(
@@ -263,9 +293,12 @@
         spread.append(
             lax.dot_general(stack, pick, (((0,), (0,)), ((), ())), preferred_element_type=F32)
         )
-    place = iota((hid, cols), 1) % nz
-    for z in range(nz):
-        t1_ref[z * hid : (z + 1) * hid, :] = banded(spread, place, z - 1)
+    outer = beyond % (2 * channels) // channels
+    for part, cell in ((0, half), (1, -1)):
+        place = jnp.where((outer == part) & (spot < 3 * channels), cell, -9)
+        place = jnp.broadcast_to(jnp.where(beyond < 0, row % half, place), (hid, cols))
+        for z in range(half):
+            t1_ref[part, z * hid : (z + 1) * hid, :] = banded(spread, place, z - 1)
     rows3, cols3 = t3_ref.shape
     taps = rows3 // nz
     pick = (iota((hid, cols3), 0) == iota((hid, cols3), 1) % hid).astype(BF16)
@@ -295,15 +328,15 @@
             preferred_element_type=F32,
         )
     ny = whole_ref.shape[3]
-    depth = 12 * nz
+    deep = feat_ref.shape[0] // whole_ref.shape[0]
     classes = spread_classes(con_ref, whole_ref.shape[2:])
     for x in range(whole_ref.shape[0]):
         column = unpacked(whole_ref, x, classes)
         if x == 0:
             pol_ref[...] = jnp.concatenate(column[2:], axis=0)
-        feat_ref[x * depth : (x + 1) * depth, :] = features_of(column, ny)
-    window = [feat_ref[i * depth : (i + 3) * depth, :] for i in range(2)]
-    hid_ref[...] = gelu(mm(t1_ref[...], jnp.concatenate(window, axis=1))).astype(BF16)
+        feat_ref[x * deep : (x + 1) * deep, :] = features_of(column, ny)
+    made = first_product(t1_ref, lambda x: feat_ref[x * deep : (x + 1) * deep, :], (0, 1))
+    hid_ref[...] = gelu(made).astype(BF16)
 
 
 def gelu(values):
@@ -315,9 +348,9 @@
     z_ref, dft_ref, out_ref, feat, hid1, hid2,
 ):
     nz, ny = first_ref.shape[2:]
-    xl = own_feat.shape[0] // (12 * nz)
-    ahead = xl + 2
-    depth = 12 * nz
+    ahead = first_ref.shape[0] + second_ref.shape[0]
+    xl = first_ref.shape[0]
+    depth = feat.shape[0] // ahead
     half = hid1.shape[0] // 2
     hid = 2 * half // nz
     tall = half - hid
@@ -339,8 +372,7 @@
         return own_feat[(place - ahead) * depth : (place - ahead + 1) * depth, :]
 
     def first_layer(j):
-        window = [jnp.concatenate([feature_rows(j + i + b) for b in range(3)], axis=0) for i in range(2)]
-        return mm(t1_ref[...], jnp.concatenate(window, axis=1))
+        return first_product(t1_ref, feature_rows, (j, j + 1))
 
     def first_done(j, made):
         hid1[:, j * ny : (j + 2) * ny] = gelu(made).astype(BF16)
@@ -478,6 +510,7 @@
     first = lax.ppermute(whole, "gx", [(i, (i + 1) % count) for i in range(count)])
     second = lax.ppermute(whole[xl - 2 :], "gx", [(i, (i + 2) % count) for i in range(count)])
     lanes = 2 * nz * xl
+    depth, deep = 6 * nz + 32, 12 * nz + 32
     dft, fwd, inv = call(
         functools.partial(table_kernel, xl, 3),
         [struct((6 * ny, ny), BF16), struct((2 * nx, 3 * nx), BF16), struct((nx, 6 * nx), BF16)],
@@ -487,14 +520,14 @@
     t1, t2, t2m, t3, zmat, sr, si, feat, hidden, pol = call(
         functools.partial(weight_kernel, nz),
         [
-            struct((nz * hid, 36 * nz), BF16),
+            struct((2, nz // 2 * hid, 3 * depth), BF16),
             struct((2, 3 * (nz // 2 - 1) * hid, 3 * nz // 2 * hid), BF16),
             struct((6 * hid, 12 * hid), BF16),
             struct((18 * nz, nz * hid), BF16),
             struct((4 * nz, 6 * nz), BF16),
             struct((nx, ql * 2 * nz), F32),
             struct((nx, ql * 2 * nz), F32),
-            struct((xl * 12 * nz, ny), BF16),
+            struct((xl * deep, ny), BF16),
             struct((nz * hid, 2 * ny), BF16),
             struct((2 * nz, ny), F32),
         ],
@@ -515,7 +548,7 @@
         struct((count, ql, lanes), F32),
         (classes, first, second, feat, hidden, pol, t1, t2, t2m, t3, zmat, dft),
         scratch=[
-            pltpu.VMEM(((xl + 2) * 12 * nz, ny), BF16),
+            pltpu.VMEM(((xl + 2) * deep, ny), BF16),
             pltpu.VMEM((nz * hid, (xl + 2) * ny), BF16),
             pltpu.VMEM((nz * hid, (xl + 2) * ny), BF16),
         ],

time: 35.3 us -> 35 us (level)
  no operation moved by 1% of the time
where the time goes in v7:
time: 35 us; the launch traced here: 34.8 us
  blocking collectives  19.1 us (55%)
  Pallas kernels  7.31 us (21%)
  waiting for transfers between devices  4.31 us (12%)
  starting transfers between devices  3.1 us (9%)
  other arithmetic  0.9 us (3%)
    all_to_all x1, blocking collectives, lane_device(): piece = lax.all_to_all(spectrum, 'gx', 0, 0, tiled=True)  9.99 us
    all_to_all x1, blocking collectives, lane_device(): rows = lax.all_to_all(spread, 'gx', 0, 0, tiled=True)  9.1 us
    pallas_call x6, Pallas kernels, call(): pl.pallas_call(kernel, out_shape=out_shapes, in_specs=[vmem] * len(args),...  7.31 us
    ppermute x1, waiting for transfers between devices, lane_device(): lax.ppermute(whole[xl - 2:], 'gx', [(i, (i + 2) % count) for i in range(c...  4.31 us
    ppermute x1, starting transfers between devices, lane_device(): lax.ppermute(whole[xl - 2:], 'gx', [(i, (i + 2) % count) for i in range(c...  2.56 us
    add x1, other arithmetic, lane_device(): jnp.pad(material[None], ((2, 0),) + still).astype(F32)  0.9 us
  transfers between devices with their start and end apart: 2, of which 1 were waited for; matrix products, arithmetic and copies ran while one was open for 0% of the time, Pallas kernels for 5%

profile of v7, /device:TPU:0, one launch (start us, length us, event | category | flops | bytes accessed | tf_op | source)
XLA Modules:
  0.0 34.8 jit_solution(531545641216969433)
XLA Ops:
  0.0 0.0 copy-start.2
  0.0 0.0 copy-start.3
  0.0 0.0 copy-start.4
  0.0 0.0 copy-start.6
  0.0 0.9 %pad_add_fusion.own_ref = f32[3,16,4,128]{3,2,1,0:T(4,128)S(1)} fusion(f32[2,16,4,128]{3,2,1,0:T(4,128)} %inc_ref.1, s32[1,16,4,128]{3,2,1,0:T(4,128)} %bitcast.10), kind=kLoop, calls=%fused_computation | loop fusion | flops 49152 | bytes 196608 | tf_op jit(solution)/shard_map/add | solution.py:508
  0.9 0.2 shard_map.82.whole_ref
  1.1 0.5 %collective-permute-start = (bf16[4,5,16,128]{3,2,1,0:T(8,128)(2,1)S(1)}, bf16[4,5,16,128]{3,2,1,0:T(8,128)(2,1)S(1)}, u32[]{:S(2)}, u32[]{:S(2)}) collective-permute-start(bf16[4,5,16,128]{3,2,1,0:T(8,128)(2,1)S(1)} %shard_map.82.whole_ref), channel_id=1, source_target_pairs={{0,1},{1,2},{2,3},{3,4},{4,5},{5,6},{6,7},{7,8},{8,9},{9,10},{10,1... | collective-permute-start | bytes 245768 | tf_op jit(solution)/shard_map/ppermute | solution.py:510
  1.7 2.6 %collective-permute-start.1 = (bf16[2,5,16,128]{3,2,1,0:T(8,128)(2,1)S(1)}, bf16[2,5,16,128]{3,2,1,0:T(8,128)(2,1)S(1)}, u32[]{:S(2)}, u32[]{:S(2)}) collective-permute-start(bf16[2,5,16,128]{3,2,1,0:T(8,128)(2,1)S(1)} %slice.4), channel_id=1, source_target_pairs={{0,2},{1,3},{2,4},{3,5},{4,6},{5,7},{6,8},{7,9},{8,10},{9,11},{10,... | collective-permute-start | bytes 122888 | tf_op jit(solution)/shard_map/ppermute | solution.py:511
  4.2 0.4 %shard_map.83 = (bf16[768,128]{1,0:T(8,128)(2,1)S(1)}, bf16[256,384]{1,0:T(8,128)(2,1)S(1)}, bf16[128,768]{1,0:T(8,128)(2,1)S(1)}) custom-call(), custom_call_target="tpu_custom_call" | custom-call | flops 1000000000 | bytes 4194304 | tf_op jit(solution)/shard_map/pallas_call | solution.py:489
  4.7 0.0 copy-done.1
  4.7 0.0 copy-done.2
  4.7 0.0 copy-done.3
  4.7 0.0 copy-done.4
  4.7 0.0 copy-done.5
  4.7 0.0 copy-done.6
  4.7 1.2 %shard_map.84 = (bf16[2,256,384]{2,1,0:T(8,128)(2,1)S(1)}, bf16[2,672,768]{2,1,0:T(8,128)(2,1)S(1)}, bf16[192,384]{1,0:T(8,128)(2,1)S(1)}, bf16[288,512]{1,0:T(8...) custom-call(f32[2,8]{1,0:T(2,128)S(1)} %bitcast.5, ...), custom_call_target="tpu_custom_call" | custom-call | flops 1000000000 | bytes 4194304 | tf_op jit(solution)/shard_map/pallas_call | solution.py:489
  5.9 4.3 %collective-permute-done.1.second_ref = bf16[2,5,16,128]{3,2,1,0:T(8,128)(2,1)S(1)} collective-permute-done((bf16[2,5,16,128]{3,2,1,0:T(8,128)(2,1)S(1)}, bf16[2,5,16,128]{3,2,1,0:T(8,128)(2,1)S(1)}, u32[]{:S(2)}, u32[]{:S(2)}) %collective-permute-start.1) | collective-permute-done | bytes 40992 | tf_op jit(solution)/shard_map/ppermute | solution.py:511
  10.2 0.0 collective-permute-done.first_ref
  10.2 3.7 %shard_map.85 = f32[32,4,128]{2,1,0:T(4,128)S(1)} custom-call(f32[2,8]{1,0:T(2,128)S(1)} %bitcast.6, bf16[4,5,16,128]{3,2,1,0:T(8,128)(2,1)S(1)} %collective-permute-done.first_ref, bf16[2,5,16,128]{3,2,1,0:T(8,128)(2,1)S(1)} %collective-permute-done.1.second_ref, bf16[896,128]{1,0:T(8,128)(2,1)S(1)} %get-tuple-element.19.own_feat, ...), custom_call_target="tpu_custom_call" | custom-call | flops 1000000000 | bytes 4194304 | tf_op jit(solution)/shard_map/pallas_call | solution.py:489
  13.9 10.0 %all_to_all.10.in_ref = f32[32,4,128]{2,1,0:T(4,128)S(1)} all-to-all(f32[32,4,128]{2,1,0:T(4,128)S(1)} %shard_map.85), channel_id=1, replica_groups=mesh['grp'=1,'gx'=32,'gy'=1] {'gx'}, dimensions={0} | all-to-all | bytes 131072 | tf_op jit(solution)/shard_map/all_to_all | solution.py:557
  23.9 0.7 %shard_map.86 = f32[32,4,128]{2,1,0:T(4,128)S(1)} custom-call(f32[32,4,128]{2,1,0:T(4,128)S(1)} %all_to_all.10.in_ref, bf16[256,384]{1,0:T(8,128)(2,1)S(1)} %get-tuple-element.27.fwd_ref.tab_ref, bf16[128,768]{1,0:T(8,128)(2,1)S(1)} %get-tuple-element.28.inv_ref, f32[128,128]{1,0:T(8,128)S(1)} %get-tuple-element.29.sr_ref, ...), custom_call_target="tpu_custom_call" | custom-call | flops 100000000 | bytes 4194304 | tf_op jit(solution)/shard_map/pallas_call | solution.py:489
  24.6 9.1 %all_to_all.11.in_ref = f32[32,4,128]{2,1,0:T(4,128)S(1)} all-to-all(f32[32,4,128]{2,1,0:T(4,128)S(1)} %shard_map.86), channel_id=1, replica_groups=mesh['grp'=1,'gx'=32,'gy'=1] {'gx'}, dimensions={0} | all-to-all | bytes 131072 | tf_op jit(solution)/shard_map/all_to_all | solution.py:564
  33.7 0.0 copy-done
  33.7 1.1 %shard_map.87 = f32[2,16,4,128]{3,2,1,0:T(4,128)} custom-call(f32[32,4,128]{2,1,0:T(4,128)S(1)} %all_to_all.11.in_ref, bf16[256,384]{1,0:T(8,128)(2,1)S(1)} %get-tuple-element.27.fwd_ref.tab_ref, f32[2,16,4,128]{3,2,1,0:T(4,128)S(1)} %copy-done), custom_call_target="tpu_custom_call" | custom-call | flops 100000000 | bytes 4194304 | tf_op jit(solution)/shard_map/pallas_call | solution.py:489
  (4 shorter events, 0.0 us)
Async XLA Ops:
  0.0 4.7 %copy-start.1 = (f32[8,2]{0,1:T(2,128)S(1)}, f32[8,2]{0,1:T(2,128)}, u32[]{:S(2)}) copy-start(f32[8,2]{0,1:T(2,128)} %param.10) | copy-start | bytes 196
  0.0 4.7 %copy-start.2 = (bf16[32,32,3,3,3]{1,0,4,3,2:T(8,128)(2,1)S(1)}, bf16[32,32,3,3,3]{1,0,4,3,2:T(8,128)(2,1)}, u32[]{:S(2)}) copy-start(bf16[32,32,3,3,3]{1,0,4,3,2:T(8,128)(2,1)} %param.12) | copy-start | bytes 165892
  0.0 4.7 %copy-start.3 = (bf16[32,4,3,3,3]{0,1,4,3,2:T(4,128)(2,1)S(1)}, bf16[32,4,3,3,3]{0,1,4,3,2:T(4,128)(2,1)}, u32[]{:S(2)}) copy-start(bf16[32,4,3,3,3]{0,1,4,3,2:T(4,128)(2,1)} %param.11) | copy-start | bytes 20740
  0.0 4.7 %copy-start.4 = (f32[2,16,16]{2,1,0:T(8,128)S(1)}, f32[2,16,16]{2,1,0:T(8,128)}, u32[]{:S(2)}) copy-start(f32[2,16,16]{2,1,0:T(8,128)} %zk_ref.1) | copy-start | bytes 6148
  0.0 4.7 %copy-start.5 = (bf16[2,32,3,3,3]{1,0,4,3,2:T(2,128)(2,1)S(1)}, bf16[2,32,3,3,3]{1,0,4,3,2:T(2,128)(2,1)}, u32[]{:S(2)}) copy-start(bf16[2,32,3,3,3]{1,0,4,3,2:T(2,128)(2,1)} %param.13) | copy-start | bytes 10372
  0.0 4.7 %copy-start.6 = (f32[2,4,128]{2,1,0:T(4,128)S(1)}, f32[2,4,128]{2,1,0:T(4,128)}, u32[]{:S(2)}) copy-start(f32[2,4,128]{2,1,0:T(4,128)} %sp_ref.1) | copy-start | bytes 12292
  1.1 9.1 %collective-permute-start = (bf16[4,5,16,128]{3,2,1,0:T(8,128)(2,1)S(1)}, bf16[4,5,16,128]{3,2,1,0:T(8,128)(2,1)S(1)}, u32[]{:S(2)}, u32[]{:S(2)}) collective-permute-start(bf16[4,5,16,128]{3,2,1,0:T(8,128)(2,1)S(1)} %shard_map.82.whole_ref), channel_id=1, source_target_pairs={{0,1},{1,2},{2,3},{3,4},{4,5},{5,6},{6,7},{7,8},{8,9},{9,10},{10,1... | collective-permute-start | bytes 245768 | tf_op jit(solution)/shard_map/ppermute | solution.py:510
  1.7 8.5 %collective-permute-start.1 = (bf16[2,5,16,128]{3,2,1,0:T(8,128)(2,1)S(1)}, bf16[2,5,16,128]{3,2,1,0:T(8,128)(2,1)S(1)}, u32[]{:S(2)}, u32[]{:S(2)}) collective-permute-start(bf16[2,5,16,128]{3,2,1,0:T(8,128)(2,1)S(1)} %slice.4), channel_id=1, source_target_pairs={{0,2},{1,3},{2,4},{3,5},{4,6},{5,7},{6,8},{7,9},{8,10},{9,11},{10,... | collective-permute-start | bytes 122888 | tf_op jit(solution)/shard_map/ppermute | solution.py:511
  10.2 23.5 %copy-start = (f32[2,16,4,128]{3,2,1,0:T(4,128)S(1)}, f32[2,16,4,128]{3,2,1,0:T(4,128)}, u32[]{:S(2)}) copy-start(f32[2,16,4,128]{3,2,1,0:T(4,128)} %inc_ref.1) | copy-start | bytes 196612

commit v8 on v7

--- a/solution.py
+++ b/solution.py
@@ -340,7 +340,8 @@
 
 
 def gelu(values):
-    return 0.5 * values * (1.0 + lax.erf(values * math.sqrt(0.5)))
+    half = 0.5 * values
+    return half + half * lax.erf(values * math.sqrt(0.5))
 
 
 def corrector_kernel(
@@ -435,31 +436,17 @@
         return mm(left_split(jnp.concatenate(both, axis=1)), dft_ref[...])
 
     own[xl - 1] = own_pol[...]
-    made1, made2 = {}, {}
-    features(4)
-    features(5)
-    made1[4] = first_layer(4)
-    features(2)
-    features(3)
-    made1[2] = first_layer(2)
-    first_done(4, made1[4])
-    made2[4] = second_layer(4)
-    features(0)
-    features(1)
-    made1[0] = first_layer(0)
-    first_done(2, made1[2])
-    made2[2] = second_layer(2)
-    first_done(0, made1[0])
-    second_done(4, made2[4])
-    third_layer(4)
-    made2[0] = second_layer(0)
-    second_done(2, made2[2])
-    third_layer(2)
-    later = transformed([2, 3])
-    second_done(0, made2[0])
-    third_layer(0)
-    spectrum = jnp.concatenate([transformed([0, 1]), later], axis=0)
-    out_ref[...] = jnp.transpose(spectrum).reshape(out_ref.shape)
+    pairs = range(ahead - 2, -1, -2)
+    for j in pairs:
+        features(j)
+        features(j + 1)
+    for j in pairs:
+        first_done(j, first_layer(j))
+    for j in pairs:
+        second_done(j, second_layer(j))
+    for j in pairs:
+        third_layer(j)
+    out_ref[...] = jnp.transpose(transformed(range(xl))).reshape(out_ref.shape)
 
 
 def spectral_kernel(nz, in_ref, fwd_ref, inv_ref, sr_ref, si_ref, out_ref):

time: 35 us -> 34.9 us (level)
  no operation moved by 1% of the time
where the time goes in v8:
time: 34.9 us; the launch traced here: 34.7 us
  blocking collectives  19.1 us (55%)
  Pallas kernels  7.18 us (21%)
  waiting for transfers between devices  4.31 us (12%)
  starting transfers between devices  3.1 us (9%)
  other arithmetic  0.9 us (3%)
    all_to_all x1, blocking collectives, lane_device(): piece = lax.all_to_all(spectrum, 'gx', 0, 0, tiled=True)  9.99 us
    all_to_all x1, blocking collectives, lane_device(): rows = lax.all_to_all(spread, 'gx', 0, 0, tiled=True)  9.1 us
    pallas_call x6, Pallas kernels, call(): pl.pallas_call(kernel, out_shape=out_shapes, in_specs=[vmem] * len(args),...  7.18 us
    ppermute x1, waiting for transfers between devices, lane_device(): lax.ppermute(whole[xl - 2:], 'gx', [(i, (i + 2) % count) for i in range(c...  4.31 us
    ppermute x1, starting transfers between devices, lane_device(): lax.ppermute(whole[xl - 2:], 'gx', [(i, (i + 2) % count) for i in range(c...  2.56 us
    add x1, other arithmetic, lane_device(): jnp.pad(material[None], ((2, 0),) + still).astype(F32)  0.9 us
  transfers between devices with their start and end apart: 2, of which 1 were waited for; matrix products, arithmetic and copies ran while one was open for 0% of the time, Pallas kernels for 5%

profile of v8, /device:TPU:0, one launch (start us, length us, event | category | flops | bytes accessed | tf_op | source)
XLA Modules:
  0.0 34.7 jit_solution(18217773404681448364)
XLA Ops:
  0.0 0.0 copy-start.2
  0.0 0.0 copy-start.3
  0.0 0.0 copy-start.4
  0.0 0.0 copy-start.6
  0.0 0.9 %pad_add_fusion.own_ref = f32[3,16,4,128]{3,2,1,0:T(4,128)S(1)} fusion(f32[2,16,4,128]{3,2,1,0:T(4,128)} %inc_ref.1, s32[1,16,4,128]{3,2,1,0:T(4,128)} %bitcast.10), kind=kLoop, calls=%fused_computation | loop fusion | flops 49152 | bytes 196608 | tf_op jit(solution)/shard_map/add | solution.py:495
  0.9 0.2 shard_map.82.whole_ref
  1.1 0.5 %collective-permute-start = (bf16[4,5,16,128]{3,2,1,0:T(8,128)(2,1)S(1)}, bf16[4,5,16,128]{3,2,1,0:T(8,128)(2,1)S(1)}, u32[]{:S(2)}, u32[]{:S(2)}) collective-permute-start(bf16[4,5,16,128]{3,2,1,0:T(8,128)(2,1)S(1)} %shard_map.82.whole_ref), channel_id=1, source_target_pairs={{0,1},{1,2},{2,3},{3,4},{4,5},{5,6},{6,7},{7,8},{8,9},{9,10},{10,1... | collective-permute-start | bytes 245768 | tf_op jit(solution)/shard_map/ppermute | solution.py:497
  1.7 2.6 %collective-permute-start.1 = (bf16[2,5,16,128]{3,2,1,0:T(8,128)(2,1)S(1)}, bf16[2,5,16,128]{3,2,1,0:T(8,128)(2,1)S(1)}, u32[]{:S(2)}, u32[]{:S(2)}) collective-permute-start(bf16[2,5,16,128]{3,2,1,0:T(8,128)(2,1)S(1)} %slice.4), channel_id=1, source_target_pairs={{0,2},{1,3},{2,4},{3,5},{4,6},{5,7},{6,8},{7,9},{8,10},{9,11},{10,... | collective-permute-start | bytes 122888 | tf_op jit(solution)/shard_map/ppermute | solution.py:498
  4.2 0.4 %shard_map.83 = (bf16[768,128]{1,0:T(8,128)(2,1)S(1)}, bf16[256,384]{1,0:T(8,128)(2,1)S(1)}, bf16[128,768]{1,0:T(8,128)(2,1)S(1)}) custom-call(), custom_call_target="tpu_custom_call" | custom-call | flops 1000000000 | bytes 4194304 | tf_op jit(solution)/shard_map/pallas_call | solution.py:476
  4.7 0.0 copy-done.1
  4.7 0.0 copy-done.2
  4.7 0.0 copy-done.3
  4.7 0.0 copy-done.4
  4.7 0.0 copy-done.5
  4.7 0.0 copy-done.6
  4.7 1.2 %shard_map.84 = (bf16[2,256,384]{2,1,0:T(8,128)(2,1)S(1)}, bf16[2,672,768]{2,1,0:T(8,128)(2,1)S(1)}, bf16[192,384]{1,0:T(8,128)(2,1)S(1)}, bf16[288,512]{1,0:T(8...) custom-call(f32[2,8]{1,0:T(2,128)S(1)} %bitcast.5, ...), custom_call_target="tpu_custom_call" | custom-call | flops 1000000000 | bytes 4194304 | tf_op jit(solution)/shard_map/pallas_call | solution.py:476
  5.9 4.3 %collective-permute-done.1.second_ref = bf16[2,5,16,128]{3,2,1,0:T(8,128)(2,1)S(1)} collective-permute-done((bf16[2,5,16,128]{3,2,1,0:T(8,128)(2,1)S(1)}, bf16[2,5,16,128]{3,2,1,0:T(8,128)(2,1)S(1)}, u32[]{:S(2)}, u32[]{:S(2)}) %collective-permute-start.1) | collective-permute-done | bytes 40992 | tf_op jit(solution)/shard_map/ppermute | solution.py:498
  10.2 0.0 collective-permute-done.first_ref
  10.2 3.6 %shard_map.85 = f32[32,4,128]{2,1,0:T(4,128)S(1)} custom-call(f32[2,8]{1,0:T(2,128)S(1)} %bitcast.6, bf16[4,5,16,128]{3,2,1,0:T(8,128)(2,1)S(1)} %collective-permute-done.first_ref, bf16[2,5,16,128]{3,2,1,0:T(8,128)(2,1)S(1)} %collective-permute-done.1.second_ref, bf16[896,128]{1,0:T(8,128)(2,1)S(1)} %get-tuple-element.19.own_feat, ...), custom_call_target="tpu_custom_call" | custom-call | flops 1000000000 | bytes 4194304 | tf_op jit(solution)/shard_map/pallas_call | solution.py:476
  13.8 10.0 %all_to_all.10.in_ref = f32[32,4,128]{2,1,0:T(4,128)S(1)} all-to-all(f32[32,4,128]{2,1,0:T(4,128)S(1)} %shard_map.85), channel_id=1, replica_groups=mesh['grp'=1,'gx'=32,'gy'=1] {'gx'}, dimensions={0} | all-to-all | bytes 131072 | tf_op jit(solution)/shard_map/all_to_all | solution.py:544
  23.8 0.7 %shard_map.86 = f32[32,4,128]{2,1,0:T(4,128)S(1)} custom-call(f32[32,4,128]{2,1,0:T(4,128)S(1)} %all_to_all.10.in_ref, bf16[256,384]{1,0:T(8,128)(2,1)S(1)} %get-tuple-element.27.fwd_ref.tab_ref, bf16[128,768]{1,0:T(8,128)(2,1)S(1)} %get-tuple-element.28.inv_ref, f32[128,128]{1,0:T(8,128)S(1)} %get-tuple-element.29.sr_ref, ...), custom_call_target="tpu_custom_call" | custom-call | flops 100000000 | bytes 4194304 | tf_op jit(solution)/shard_map/pallas_call | solution.py:476
  24.5 9.1 %all_to_all.11.in_ref = f32[32,4,128]{2,1,0:T(4,128)S(1)} all-to-all(f32[32,4,128]{2,1,0:T(4,128)S(1)} %shard_map.86), channel_id=1, replica_groups=mesh['grp'=1,'gx'=32,'gy'=1] {'gx'}, dimensions={0} | all-to-all | bytes 131072 | tf_op jit(solution)/shard_map/all_to_all | solution.py:551
  33.6 0.0 copy-done
  33.6 1.1 %shard_map.87 = f32[2,16,4,128]{3,2,1,0:T(4,128)} custom-call(f32[32,4,128]{2,1,0:T(4,128)S(1)} %all_to_all.11.in_ref, bf16[256,384]{1,0:T(8,128)(2,1)S(1)} %get-tuple-element.27.fwd_ref.tab_ref, f32[2,16,4,128]{3,2,1,0:T(4,128)S(1)} %copy-done), custom_call_target="tpu_custom_call" | custom-call | flops 100000000 | bytes 4194304 | tf_op jit(solution)/shard_map/pallas_call | solution.py:476
  (4 shorter events, 0.0 us)
Async XLA Ops:
  0.0 4.7 %copy-start.1 = (f32[8,2]{0,1:T(2,128)S(1)}, f32[8,2]{0,1:T(2,128)}, u32[]{:S(2)}) copy-start(f32[8,2]{0,1:T(2,128)} %param.10) | copy-start | bytes 196
  0.0 4.7 %copy-start.2 = (bf16[32,32,3,3,3]{1,0,4,3,2:T(8,128)(2,1)S(1)}, bf16[32,32,3,3,3]{1,0,4,3,2:T(8,128)(2,1)}, u32[]{:S(2)}) copy-start(bf16[32,32,3,3,3]{1,0,4,3,2:T(8,128)(2,1)} %param.12) | copy-start | bytes 165892
  0.0 4.7 %copy-start.3 = (bf16[32,4,3,3,3]{0,1,4,3,2:T(4,128)(2,1)S(1)}, bf16[32,4,3,3,3]{0,1,4,3,2:T(4,128)(2,1)}, u32[]{:S(2)}) copy-start(bf16[32,4,3,3,3]{0,1,4,3,2:T(4,128)(2,1)} %param.11) | copy-start | bytes 20740
  0.0 4.7 %copy-start.4 = (f32[2,16,16]{2,1,0:T(8,128)S(1)}, f32[2,16,16]{2,1,0:T(8,128)}, u32[]{:S(2)}) copy-start(f32[2,16,16]{2,1,0:T(8,128)} %zk_ref.1) | copy-start | bytes 6148
  0.0 4.7 %copy-start.5 = (bf16[2,32,3,3,3]{1,0,4,3,2:T(2,128)(2,1)S(1)}, bf16[2,32,3,3,3]{1,0,4,3,2:T(2,128)(2,1)}, u32[]{:S(2)}) copy-start(bf16[2,32,3,3,3]{1,0,4,3,2:T(2,128)(2,1)} %param.13) | copy-start | bytes 10372
  0.0 4.7 %copy-start.6 = (f32[2,4,128]{2,1,0:T(4,128)S(1)}, f32[2,4,128]{2,1,0:T(4,128)}, u32[]{:S(2)}) copy-start(f32[2,4,128]{2,1,0:T(4,128)} %sp_ref.1) | copy-start | bytes 12292
  1.1 9.1 %collective-permute-start = (bf16[4,5,16,128]{3,2,1,0:T(8,128)(2,1)S(1)}, bf16[4,5,16,128]{3,2,1,0:T(8,128)(2,1)S(1)}, u32[]{:S(2)}, u32[]{:S(2)}) collective-permute-start(bf16[4,5,16,128]{3,2,1,0:T(8,128)(2,1)S(1)} %shard_map.82.whole_ref), channel_id=1, source_target_pairs={{0,1},{1,2},{2,3},{3,4},{4,5},{5,6},{6,7},{7,8},{8,9},{9,10},{10,1... | collective-permute-start | bytes 245768 | tf_op jit(solution)/shard_map/ppermute | solution.py:497
  1.7 8.5 %collective-permute-start.1 = (bf16[2,5,16,128]{3,2,1,0:T(8,128)(2,1)S(1)}, bf16[2,5,16,128]{3,2,1,0:T(8,128)(2,1)S(1)}, u32[]{:S(2)}, u32[]{:S(2)}) collective-permute-start(bf16[2,5,16,128]{3,2,1,0:T(8,128)(2,1)S(1)} %slice.4), channel_id=1, source_target_pairs={{0,2},{1,3},{2,4},{3,5},{4,6},{5,7},{6,8},{7,9},{8,10},{9,11},{10,... | collective-permute-start | bytes 122888 | tf_op jit(solution)/shard_map/ppermute | solution.py:498
  10.2 23.4 %copy-start = (f32[2,16,4,128]{3,2,1,0:T(4,128)S(1)}, f32[2,16,4,128]{3,2,1,0:T(4,128)}, u32[]{:S(2)}) copy-start(f32[2,16,4,128]{3,2,1,0:T(4,128)} %inc_ref.1) | copy-start | bytes 196612

commit v9 on v8

--- a/solution.py
+++ b/solution.py
@@ -204,6 +204,17 @@
             whole_ref[x, i] = high
             if i < 2:
                 whole_ref[x, i + 3] = low
+
+
+def near_kernel(class_count, own_ref, whole_ref, near_ref):
+    xl, _, nz, ny = whole_ref.shape
+    classes = [
+        [jnp.broadcast_to(own_ref[3, 0, part : part + 1, k : k + 1], (nz, ny)) for part in range(2)]
+        for k in range(class_count)
+    ]
+    for x in range(2):
+        for i, plane in enumerate(unpacked(whole_ref, xl - 2 + x, classes)):
+            near_ref[x, i] = plane.astype(BF16)
 
 
 def table_kernel(xl, shift, dft_ref, fwd_ref, inv_ref):
@@ -346,7 +357,7 @@
 
 def corrector_kernel(
     con_ref, first_ref, second_ref, own_feat, own_hid, own_pol, t1_ref, t2_ref, t2m_ref, t3_ref,
-    z_ref, dft_ref, out_ref, feat, hid1, hid2,
+    z_ref, dft_ref, green_ref, out_ref, feat, hid1, hid2,
 ):
     nz, ny = first_ref.shape[2:]
     ahead = first_ref.shape[0] + second_ref.shape[0]
@@ -361,8 +372,10 @@
     last = {}
 
     def features(place):
-        ref, x = (second_ref, place) if place < 2 else (first_ref, place - 2)
-        column = unpacked(ref, x, classes)
+        if place < 2:
+            column = [second_ref[place, i] for i in range(4)]
+        else:
+            column = unpacked(first_ref, place - 2, classes)
         if place > 2:
             own[place - 3] = jnp.concatenate(column[2:], axis=0)
         feat[place * depth : (place + 1) * depth, :] = features_of(column, ny)
@@ -449,15 +462,32 @@
     out_ref[...] = jnp.transpose(transformed(range(xl))).reshape(out_ref.shape)
 
 
-def spectral_kernel(nz, in_ref, fwd_ref, inv_ref, sr_ref, si_ref, out_ref):
+def green_kernel(fwd_ref, inv_ref, sr_ref, si_ref, green_ref):
+    nx = inv_ref.shape[0]
+    table = fwd_ref[:, :nx].astype(F32) + fwd_ref[:, 2 * nx :].astype(F32)
+    cos, sin = table[:nx], table[nx:]
+    count = green_ref.shape[0] // nx
+    inner = sr_ref.shape[1] // count
+    for q in range(count):
+        re, im = sr_ref[:, q * inner : q * inner + 1], si_ref[:, q * inner : q * inner + 1]
+        same, cross = re * cos + im * sin, re * sin - im * cos
+        top = jnp.concatenate([same, -cross], axis=1)
+        bottom = jnp.concatenate([cross, same], axis=1)
+        high, low = split(mm(inv_ref[...], right_split(jnp.concatenate([top, bottom], axis=0))))
+        green_ref[q * nx : (q + 1) * nx, :] = jnp.concatenate([high, high, low], axis=1)
+
+
+def spectral_kernel(nz, in_ref, green_ref, out_ref):
     values = swap_blocks(in_ref, in_ref.shape[1])
-    lanes = values.shape[1]
-    made = mm(fwd_ref[...], right_split(jnp.concatenate([values, turned(values, nz)], axis=1)))
-    nx = made.shape[0] // 2
-    plain = made[:nx, :lanes] - made[nx:, lanes:]
-    other = made[:nx, lanes:] + made[nx:, :lanes]
-    scaled = [sr_ref[...] * plain + si_ref[...] * other, sr_ref[...] * other - si_ref[...] * plain]
-    out_ref[...] = mm(inv_ref[...], right_split(jnp.concatenate(scaled, axis=0))).reshape(out_ref.shape)
+    both = jnp.concatenate([values, turned(values, nz)], axis=0)
+    made = mm(green_ref[...], right_split(both))
+    nx, lanes = values.shape
+    count = made.shape[0] // nx
+    block = iota((nx, lanes), 1) // (lanes // count)
+    total = made[:nx]
+    for q in range(1, count):
+        total = jnp.where(block == q, made[q * nx : (q + 1) * nx], total)
+    out_ref[...] = total.reshape(out_ref.shape)
 
 
 def finish_kernel(nz, in_ref, tab_ref, inc_ref, out_ref):
@@ -492,10 +522,15 @@
     struct = jax.ShapeDtypeStruct
     classes = jnp.transpose(contrast)
     still = ((0, 0),) * 3
-    own = jnp.pad(material[None], ((2, 0),) + still).astype(F32) + jnp.pad(incident, ((0, 1),) + still)
+    own = jnp.pad(material[None], ((2, 1),) + still).astype(F32) + jnp.pad(incident, ((0, 2),) + still)
+    parts, kinds = classes.shape
+    own += jnp.pad(classes[None, None], ((3, 0), (0, nz - 1), (0, xl - parts), (0, ny - kinds)))
     whole = call(pack_kernel, struct((xl, 5, nz, ny), BF16), (own,), flops=10**6)
     first = lax.ppermute(whole, "gx", [(i, (i + 1) % count) for i in range(count)])
-    second = lax.ppermute(whole[xl - 2 :], "gx", [(i, (i + 2) % count) for i in range(count)])
+    near = call(
+        functools.partial(near_kernel, kinds), struct((2, 4, nz, ny), BF16), (own, whole), flops=10**6
+    )
+    second = lax.ppermute(near, "gx", [(i, (i + 2) % count) for i in range(count)])
     lanes = 2 * nz * xl
     depth, deep = 6 * nz + 32, 12 * nz + 32
     dft, fwd, inv = call(
@@ -530,10 +565,13 @@
         ),
         flops=10**9,
     )
+    green = call(
+        green_kernel, struct((ql * nx, 6 * nx), BF16), (fwd, inv, sr, si), flops=10**9
+    )
     spectrum = call(
         corrector_kernel,
         struct((count, ql, lanes), F32),
-        (classes, first, second, feat, hidden, pol, t1, t2, t2m, t3, zmat, dft),
+        (classes, first, second, feat, hidden, pol, t1, t2, t2m, t3, zmat, dft, green),
         scratch=[
             pltpu.VMEM(((xl + 2) * deep, ny), BF16),
             pltpu.VMEM((nz * hid, (xl + 2) * ny), BF16),
@@ -545,7 +583,7 @@
     spread = call(
         functools.partial(spectral_kernel, nz),
         struct((count, xl, lanes), F32),
-        (piece, fwd, inv, sr, si),
+        (piece, green),
         flops=10**8,
     )
     rows = lax.all_to_all(spread, "gx", 0, 0, tiled=True)

time: 34.9 us -> 34.7 us (level)
  waiting for transfers between devices: 4.31 us -> 3.67 us
  Pallas kernels: 7.18 us -> 7.7 us
    ppermute x1, waiting for transfers between devices: 4.31 us -> 3.67 us  [lane_device(): lax.ppermute(near, 'gx', [(i, (i + 2) % count) for i in range(count)])]
    pallas_call x6 -> x8, Pallas kernels: 7.18 us -> 7.7 us  [call(): pl.pallas_call(kernel, out_shape=out_shapes, in_specs=[vmem] * len(args),...]
  transfers between devices with their start and end apart: 2 -> 2, of which waited for: 1 -> 1; matrix products, arithmetic and copies ran while one was open for 0% -> 0% of each run, Pallas kernels for 5% -> 7%
where the time goes in v9:
time: 34.7 us; the launch traced here: 34.5 us
  blocking collectives  19 us (55%)
  Pallas kernels  7.7 us (22%)
  waiting for transfers between devices  3.67 us (11%)
  starting transfers between devices  3.06 us (9%)
  other arithmetic  0.85 us (2%)
    all_to_all x1, blocking collectives, lane_device(): piece = lax.all_to_all(spectrum, 'gx', 0, 0, tiled=True)  9.92 us
    all_to_all x1, blocking collectives, lane_device(): rows = lax.all_to_all(spread, 'gx', 0, 0, tiled=True)  9.1 us
    pallas_call x8, Pallas kernels, call(): pl.pallas_call(kernel, out_shape=out_shapes, in_specs=[vmem] * len(args),...  7.7 us
    ppermute x1, waiting for transfers between devices, lane_device(): lax.ppermute(near, 'gx', [(i, (i + 2) % count) for i in range(count)])  3.67 us
    ppermute x1, starting transfers between devices, lane_device(): lax.ppermute(near, 'gx', [(i, (i + 2) % count) for i in range(count)])  2.55 us
    add x1, other arithmetic, lane_device(): own += jnp.pad(classes[None, None], ((3, 0), (0, nz - 1), (0, xl - parts)...  0.85 us
  transfers between devices with their start and end apart: 2, of which 1 were waited for; matrix products, arithmetic and copies ran while one was open for 0% of the time, Pallas kernels for 7%

profile of v9, /device:TPU:0, one launch (start us, length us, event | category | flops | bytes accessed | tf_op | source)
XLA Modules:
  0.0 34.5 jit_solution(15852863580815075280)
XLA Ops:
  0.0 0.9 %pad_add_fusion.own_ref = f32[4,16,4,128]{3,2,1,0:T(4,128)S(1)} fusion(f32[1,1,2,8]{3,2,1,0:T(2,128)} %bitcast.7, f32[2,16,4,128]{3,2,1,0:T(4,128)} %inc_ref.1, s32[1,16,4,128]{3,2,1,0:T(4,128)} %bitcast.13), kind=kLoop, calls=%fused_computation | loop fusion | flops 98304 | bytes 229440 | tf_op jit(solution)/shard_map/add | solution.py:527
  0.9 0.0 copy-start.1
  0.9 0.0 copy-start.2
  0.9 0.0 copy-start.3
  0.9 0.0 copy-start.4
  0.9 0.0 copy-start.5
  0.9 0.0 copy-start.6
  0.9 0.2 shard_map.82.whole_ref
  1.1 0.5 %collective-permute-start = (bf16[4,5,16,128]{3,2,1,0:T(8,128)(2,1)S(1)}, bf16[4,5,16,128]{3,2,1,0:T(8,128)(2,1)S(1)}, u32[]{:S(2)}, u32[]{:S(2)}) collective-permute-start(bf16[4,5,16,128]{3,2,1,0:T(8,128)(2,1)S(1)} %shard_map.82.whole_ref), channel_id=1, source_target_pairs={{0,1},{1,2},{2,3},{3,4},{4,5},{5,6},{6,7},{7,8},{8,9},{9,10},{10,1... | collective-permute-start | bytes 245768 | tf_op jit(solution)/shard_map/ppermute | solution.py:529
  1.6 0.1 shard_map.83
  1.8 2.6 %collective-permute-start.1 = (bf16[2,4,16,128]{3,2,1,0:T(8,128)(2,1)S(1)}, bf16[2,4,16,128]{3,2,1,0:T(8,128)(2,1)S(1)}, u32[]{:S(2)}, u32[]{:S(2)}) collective-permute-start(bf16[2,4,16,128]{3,2,1,0:T(8,128)(2,1)S(1)} %shard_map.83), channel_id=1, source_target_pairs={{0,2},{1,3},{2,4},{3,5},{4,6},{5,7},{6,8},{7,9},{8,10},{9,11},{10,... | collective-permute-start | bytes 98312 | tf_op jit(solution)/shard_map/ppermute | solution.py:533
  4.3 0.4 %shard_map.84 = (bf16[768,128]{1,0:T(8,128)(2,1)S(1)}, bf16[256,384]{1,0:T(8,128)(2,1)S(1)}, bf16[128,768]{1,0:T(8,128)(2,1)S(1)}) custom-call(), custom_call_target="tpu_custom_call" | custom-call | flops 1000000000 | bytes 4194304 | tf_op jit(solution)/shard_map/pallas_call | solution.py:506
  4.8 0.0 copy-done.1
  4.8 0.0 copy-done.2
  4.8 0.0 copy-done.3
  4.8 1.2 %shard_map.85 = (bf16[2,256,384]{2,1,0:T(8,128)(2,1)S(1)}, bf16[2,672,768]{2,1,0:T(8,128)(2,1)S(1)}, bf16[192,384]{1,0:T(8,128)(2,1)S(1)}, bf16[288,512]{1,0:T(8...) custom-call(f32[2,8]{1,0:T(2,128)S(1)} %bitcast.8, ...), custom_call_target="tpu_custom_call" | custom-call | flops 1000000000 | bytes 4194304 | tf_op jit(solution)/shard_map/pallas_call | solution.py:506
  6.0 0.5 %shard_map.86.green_ref = bf16[512,768]{1,0:T(8,128)(2,1)S(1)} custom-call(bf16[256,384]{1,0:T(8,128)(2,1)S(1)} %get-tuple-element.27.fwd_ref.tab_ref, bf16[128,768]{1,0:T(8,128)(2,1)S(1)} %get-tuple-element.28.inv_ref, f32[128,128]{1,0:T(8,128)S(1)} %get-tuple-element.29.sr_ref, f32[128,128]{1,0:T(8,128)S(1)} %get-tuple-element.30.si_ref), custom_call_target="tpu_custom_call" | custom-call | flops 1000000000 | bytes 4194304 | tf_op jit(solution)/shard_map/pallas_call | solution.py:506
  6.5 3.7 %collective-permute-done.1.second_ref = bf16[2,4,16,128]{3,2,1,0:T(8,128)(2,1)S(1)} collective-permute-done((bf16[2,4,16,128]{3,2,1,0:T(8,128)(2,1)S(1)}, bf16[2,4,16,128]{3,2,1,0:T(8,128)(2,1)S(1)}, u32[]{:S(2)}, u32[]{:S(2)}) %collective-permute-start.1) | collective-permute-done | bytes 32800 | tf_op jit(solution)/shard_map/ppermute | solution.py:533
  10.2 0.0 collective-permute-done.first_ref
  10.2 3.6 %shard_map.87 = f32[32,4,128]{2,1,0:T(4,128)S(1)} custom-call(f32[2,8]{1,0:T(2,128)S(1)} %bitcast.9, bf16[4,5,16,128]{3,2,1,0:T(8,128)(2,1)S(1)} %collective-permute-done.first_ref, bf16[2,4,16,128]{3,2,1,0:T(8,128)(2,1)S(1)} %collective-permute-done.1.second_ref, bf16[896,128]{1,0:T(8,128)(2,1)S(1)} %get-tuple-element.19.own_feat, ...), custom_call_target="tpu_custom_call" | custom-call | flops 1000000000 | bytes 4194304 | tf_op jit(solution)/shard_map/pallas_call | solution.py:506
  13.8 9.9 %all_to_all.10.in_ref = f32[32,4,128]{2,1,0:T(4,128)S(1)} all-to-all(f32[32,4,128]{2,1,0:T(4,128)S(1)} %shard_map.87), channel_id=1, replica_groups=mesh['grp'=1,'gx'=32,'gy'=1] {'gx'}, dimensions={0} | all-to-all | bytes 131072 | tf_op jit(solution)/shard_map/all_to_all | solution.py:582
  23.7 0.5 %shard_map.88 = f32[32,4,128]{2,1,0:T(4,128)S(1)} custom-call(f32[32,4,128]{2,1,0:T(4,128)S(1)} %all_to_all.10.in_ref, bf16[512,768]{1,0:T(8,128)(2,1)S(1)} %shard_map.86.green_ref), custom_call_target="tpu_custom_call" | custom-call | flops 100000000 | bytes 4194304 | tf_op jit(solution)/shard_map/pallas_call | solution.py:506
  24.3 9.1 %all_to_all.11.in_ref = f32[32,4,128]{2,1,0:T(4,128)S(1)} all-to-all(f32[32,4,128]{2,1,0:T(4,128)S(1)} %shard_map.88), channel_id=1, replica_groups=mesh['grp'=1,'gx'=32,'gy'=1] {'gx'}, dimensions={0} | all-to-all | bytes 131072 | tf_op jit(solution)/shard_map/all_to_all | solution.py:589
  33.4 1.1 %shard_map.89 = f32[2,16,4,128]{3,2,1,0:T(4,128)} custom-call(f32[32,4,128]{2,1,0:T(4,128)S(1)} %all_to_all.11.in_ref, bf16[256,384]{1,0:T(8,128)(2,1)S(1)} %get-tuple-element.27.fwd_ref.tab_ref, f32[2,16,4,128]{3,2,1,0:T(4,128)S(1)} %copy-done), custom_call_target="tpu_custom_call" | custom-call | flops 100000000 | bytes 4194304 | tf_op jit(solution)/shard_map/pallas_call | solution.py:506
  (5 shorter events, 0.0 us)
Async XLA Ops:
  0.9 3.9 %copy-start.1 = (f32[8,2]{0,1:T(2,128)S(1)}, f32[8,2]{0,1:T(2,128)}, u32[]{:S(2)}) copy-start(f32[8,2]{0,1:T(2,128)} %param.10) | copy-start | bytes 196
  0.9 3.9 %copy-start.2 = (bf16[32,32,3,3,3]{1,0,4,3,2:T(8,128)(2,1)S(1)}, bf16[32,32,3,3,3]{1,0,4,3,2:T(8,128)(2,1)}, u32[]{:S(2)}) copy-start(bf16[32,32,3,3,3]{1,0,4,3,2:T(8,128)(2,1)} %param.12) | copy-start | bytes 165892
  0.9 3.9 %copy-start.3 = (bf16[32,4,3,3,3]{0,1,4,3,2:T(4,128)(2,1)S(1)}, bf16[32,4,3,3,3]{0,1,4,3,2:T(4,128)(2,1)}, u32[]{:S(2)}) copy-start(bf16[32,4,3,3,3]{0,1,4,3,2:T(4,128)(2,1)} %param.11) | copy-start | bytes 20740
  0.9 3.9 %copy-start.4 = (f32[2,16,16]{2,1,0:T(8,128)S(1)}, f32[2,16,16]{2,1,0:T(8,128)}, u32[]{:S(2)}) copy-start(f32[2,16,16]{2,1,0:T(8,128)} %zk_ref.1) | copy-start | bytes 6148
  0.9 3.9 %copy-start.5 = (bf16[2,32,3,3,3]{1,0,4,3,2:T(2,128)(2,1)S(1)}, bf16[2,32,3,3,3]{1,0,4,3,2:T(2,128)(2,1)}, u32[]{:S(2)}) copy-start(bf16[2,32,3,3,3]{1,0,4,3,2:T(2,128)(2,1)} %param.13) | copy-start | bytes 10372
  0.9 3.9 %copy-start.6 = (f32[2,4,128]{2,1,0:T(4,128)S(1)}, f32[2,4,128]{2,1,0:T(4,128)}, u32[]{:S(2)}) copy-start(f32[2,4,128]{2,1,0:T(4,128)} %sp_ref.1) | copy-start | bytes 12292
  1.1 9.1 %collective-permute-start = (bf16[4,5,16,128]{3,2,1,0:T(8,128)(2,1)S(1)}, bf16[4,5,16,128]{3,2,1,0:T(8,128)(2,1)S(1)}, u32[]{:S(2)}, u32[]{:S(2)}) collective-permute-start(bf16[4,5,16,128]{3,2,1,0:T(8,128)(2,1)S(1)} %shard_map.82.whole_ref), channel_id=1, source_target_pairs={{0,1},{1,2},{2,3},{3,4},{4,5},{5,6},{6,7},{7,8},{8,9},{9,10},{10,1... | collective-permute-start | bytes 245768 | tf_op jit(solution)/shard_map/ppermute | solution.py:529
  1.8 8.4 %collective-permute-start.1 = (bf16[2,4,16,128]{3,2,1,0:T(8,128)(2,1)S(1)}, bf16[2,4,16,128]{3,2,1,0:T(8,128)(2,1)S(1)}, u32[]{:S(2)}, u32[]{:S(2)}) collective-permute-start(bf16[2,4,16,128]{3,2,1,0:T(8,128)(2,1)S(1)} %shard_map.83), channel_id=1, source_target_pairs={{0,2},{1,3},{2,4},{3,5},{4,6},{5,7},{6,8},{7,9},{8,10},{9,11},{10,... | collective-permute-start | bytes 98312 | tf_op jit(solution)/shard_map/ppermute | solution.py:533
  10.2 23.2 %copy-start = (f32[2,16,4,128]{3,2,1,0:T(4,128)S(1)}, f32[2,16,4,128]{3,2,1,0:T(4,128)}, u32[]{:S(2)}) copy-start(f32[2,16,4,128]{3,2,1,0:T(4,128)} %inc_ref.1) | copy-start | bytes 196612

commit v10 on v9

--- a/solution.py
+++ b/solution.py
@@ -158,6 +158,16 @@
     return jnp.where(real, -ahead, pltpu.roll(values, nz, 1))
 
 
+def mixed(made, nz, sign):
+    half = made.shape[1] // 2
+    blocks = []
+    for top in range(0, made.shape[0], 2 * nz):
+        re, im = made[top : top + nz], made[top + nz : top + 2 * nz]
+        blocks.append(re[:, :half] + sign * im[:, half:])
+        blocks.append(im[:, :half] - sign * re[:, half:])
+    return blocks
+
+
 def swap_blocks(ref, count):
     pieces = [ref[:, q, :] for q in range(count)]
     inner = pieces[0].shape[1] // count
@@ -217,14 +227,17 @@
             near_ref[x, i] = plane.astype(BF16)
 
 
-def table_kernel(xl, shift, dft_ref, fwd_ref, inv_ref):
-    nx, ny = inv_ref.shape[0], dft_ref.shape[1]
-    dft_ref[...] = dft_parts(iota((ny, ny), 0), iota((ny, ny), 1), ny, 0, 0)
+def table_kernel(xl, shift, dft_ref, fwd_ref, inv_ref, back_ref):
+    nx, ny = inv_ref.shape[0], dft_ref.shape[1] // 2
+    dft_ref[...] = dft_parts(iota((ny, ny), 0), iota((ny, ny), 1), ny, 1, 0)
     first, second = iota((nx, nx), 0), iota((nx, nx), 1)
     inv_ref[...] = dft_parts(lax.rem(first + shift, nx), second, nx, 1, 1, 1.0 / (nx * ny))
     count = nx // xl
     second = lax.rem(second, count) * xl + second // count
     fwd_ref[...] = dft_parts(first, second, nx, 0, 1)
+    first, second = iota((ny, ny), 0), iota((ny, ny), 1)
+    count = ny // xl
+    back_ref[...] = dft_parts(lax.rem(first, count) * xl + first // count, second, ny, 1, 0)
 
 
 def features_of(column, ny):
@@ -326,7 +339,7 @@
     kr, ki = zk_ref[0], zk_ref[1]
     top = jnp.concatenate([kr, -ki], axis=1)
     bottom = jnp.concatenate([ki, kr], axis=1)
-    high, low = split(jnp.concatenate([top, bottom, bottom, -top], axis=0))
+    high, low = split(jnp.concatenate([top, bottom], axis=0))
     z_ref[...] = jnp.concatenate([high, high, low], axis=1)
     count, lanes = sp_ref.shape[1], sr_ref.shape[1]
     pick = (iota((count, lanes), 0) == iota((count, lanes), 1) // (lanes // count)).astype(F32)
@@ -441,12 +454,9 @@
 
     def transformed(places):
         lifted = mm(z_ref[...], right_split(jnp.concatenate([source(x) for x in places], axis=1)))
-        plain, turned = [], []
-        for i in range(len(places)):
-            plain.append(lifted[:deep, i * ny : (i + 1) * ny])
-            turned.append(lifted[deep:, i * ny : (i + 1) * ny])
-        both = [jnp.concatenate(plain, axis=0), jnp.concatenate(turned, axis=0)]
-        return mm(left_split(jnp.concatenate(both, axis=1)), dft_ref[...])
+        rows = [lifted[:, i * ny : (i + 1) * ny] for i in range(len(places))]
+        made = mm(left_split(jnp.concatenate(rows, axis=0)), dft_ref[...])
+        return jnp.concatenate(mixed(made, nz, 1.0), axis=0)
 
     own[xl - 1] = own_pol[...]
     pairs = range(ahead - 2, -1, -2)
@@ -490,14 +500,12 @@
     out_ref[...] = total.reshape(out_ref.shape)
 
 
-def finish_kernel(nz, in_ref, tab_ref, inc_ref, out_ref):
-    made = mm(tab_ref[...], right_split(swap_blocks(in_ref, in_ref.shape[1])))
-    ny = made.shape[0] // 2
-    field = jnp.transpose(made[:ny] + turned(made[ny:], nz))
-    for x in range(out_ref.shape[2]):
+def finish_kernel(nz, in_ref, back_ref, inc_ref, out_ref):
+    values = jnp.transpose(swap_blocks(in_ref, in_ref.shape[1]))
+    blocks = mixed(mm(left_split(values), back_ref[...]), nz, -1.0)
+    for x in range(inc_ref.shape[2]):
         for part in range(2):
-            first = (2 * x + part) * nz
-            out_ref[part, :, x, :] = inc_ref[part, :, x, :] + field[first : first + nz, :]
+            out_ref[part, :, x, :] = inc_ref[part, :, x, :] + blocks[2 * x + part]
 
 
 def call(kernel, out_shapes, args, scratch=(), flops=0):
@@ -533,9 +541,14 @@
     second = lax.ppermute(near, "gx", [(i, (i + 2) % count) for i in range(count)])
     lanes = 2 * nz * xl
     depth, deep = 6 * nz + 32, 12 * nz + 32
-    dft, fwd, inv = call(
+    dft, fwd, inv, back = call(
         functools.partial(table_kernel, xl, 3),
-        [struct((6 * ny, ny), BF16), struct((2 * nx, 3 * nx), BF16), struct((nx, 6 * nx), BF16)],
+        [
+            struct((3 * ny, 2 * ny), BF16),
+            struct((2 * nx, 3 * nx), BF16),
+            struct((nx, 6 * nx), BF16),
+            struct((3 * ny, 2 * ny), BF16),
+        ],
         (),
         flops=10**9,
     )
@@ -546,7 +559,7 @@
             struct((2, 3 * (nz // 2 - 1) * hid, 3 * nz // 2 * hid), BF16),
             struct((6 * hid, 12 * hid), BF16),
             struct((18 * nz, nz * hid), BF16),
-            struct((4 * nz, 6 * nz), BF16),
+            struct((2 * nz, 6 * nz), BF16),
             struct((nx, ql * 2 * nz), F32),
             struct((nx, ql * 2 * nz), F32),
             struct((xl * deep, ny), BF16),
@@ -590,7 +603,7 @@
     return call(
         functools.partial(finish_kernel, nz),
         struct(incident.shape, F32),
-        (rows, fwd, incident),
+        (rows, back, incident),
         flops=10**8,
     )
 

time: 34.7 us -> 34.5 us (level)
  no operation moved by 1% of the time
where the time goes in v10:
time: 34.5 us; the launch traced here: 34.3 us
  blocking collectives  19 us (55%)
  Pallas kernels  7.65 us (22%)
  waiting for transfers between devices  3.56 us (10%)
  starting transfers between devices  3.06 us (9%)
  other arithmetic  0.85 us (2%)
    all_to_all x1, blocking collectives, lane_device(): piece = lax.all_to_all(spectrum, 'gx', 0, 0, tiled=True)  9.91 us
    all_to_all x1, blocking collectives, lane_device(): rows = lax.all_to_all(spread, 'gx', 0, 0, tiled=True)  9.1 us
    pallas_call x8, Pallas kernels, call(): pl.pallas_call(kernel, out_shape=out_shapes, in_specs=[vmem] * len(args),...  7.65 us
    ppermute x1, waiting for transfers between devices, lane_device(): lax.ppermute(near, 'gx', [(i, (i + 2) % count) for i in range(count)])  3.56 us
    ppermute x1, starting transfers between devices, lane_device(): lax.ppermute(near, 'gx', [(i, (i + 2) % count) for i in range(count)])  2.55 us
    add x1, other arithmetic, lane_device(): own += jnp.pad(classes[None, None], ((3, 0), (0, nz - 1), (0, xl - parts)...  0.85 us
  transfers between devices with their start and end apart: 2, of which 1 were waited for; matrix products, arithmetic and copies ran while one was open for 0% of the time, Pallas kernels for 7%

profile of v10, /device:TPU:0, one launch (start us, length us, event | category | flops | bytes accessed | tf_op | source)
XLA Modules:
  0.0 34.3 jit_solution(2075851740623045933)
XLA Ops:
  0.0 0.9 %pad_add_fusion.own_ref = f32[4,16,4,128]{3,2,1,0:T(4,128)S(1)} fusion(f32[1,1,2,8]{3,2,1,0:T(2,128)} %bitcast.7, f32[2,16,4,128]{3,2,1,0:T(4,128)} %inc_ref.1, s32[1,16,4,128]{3,2,1,0:T(4,128)} %bitcast.13), kind=kLoop, calls=%fused_computation | loop fusion | flops 98304 | bytes 229440 | tf_op jit(solution)/shard_map/add | solution.py:535
  0.9 0.0 copy-start.1
  0.9 0.0 copy-start.2
  0.9 0.0 copy-start.3
  0.9 0.0 copy-start.4
  0.9 0.0 copy-start.5
  0.9 0.0 copy-start.6
  0.9 0.2 shard_map.82.whole_ref
  1.1 0.5 %collective-permute-start = (bf16[4,5,16,128]{3,2,1,0:T(8,128)(2,1)S(1)}, bf16[4,5,16,128]{3,2,1,0:T(8,128)(2,1)S(1)}, u32[]{:S(2)}, u32[]{:S(2)}) collective-permute-start(bf16[4,5,16,128]{3,2,1,0:T(8,128)(2,1)S(1)} %shard_map.82.whole_ref), channel_id=1, source_target_pairs={{0,1},{1,2},{2,3},{3,4},{4,5},{5,6},{6,7},{7,8},{8,9},{9,10},{10,1... | collective-permute-start | bytes 245768 | tf_op jit(solution)/shard_map/ppermute | solution.py:537
  1.6 0.1 shard_map.83
  1.8 2.6 %collective-permute-start.1 = (bf16[2,4,16,128]{3,2,1,0:T(8,128)(2,1)S(1)}, bf16[2,4,16,128]{3,2,1,0:T(8,128)(2,1)S(1)}, u32[]{:S(2)}, u32[]{:S(2)}) collective-permute-start(bf16[2,4,16,128]{3,2,1,0:T(8,128)(2,1)S(1)} %shard_map.83), channel_id=1, source_target_pairs={{0,2},{1,3},{2,4},{3,5},{4,6},{5,7},{6,8},{7,9},{8,10},{9,11},{10,... | collective-permute-start | bytes 98312 | tf_op jit(solution)/shard_map/ppermute | solution.py:541
  4.3 0.6 %shard_map.84 = (bf16[384,256]{1,0:T(8,128)(2,1)S(1)}, bf16[256,384]{1,0:T(8,128)(2,1)S(1)}, bf16[128,768]{1,0:T(8,128)(2,1)S(1)}, bf16[384,256]{1,0:T(8,128)(2,1)S(1)}) custom-call(), custom_call_target="tpu_custom_call" | custom-call | flops 1000000000 | bytes 4194304 | tf_op jit(solution)/shard_map/pallas_call | solution.py:514
  4.9 0.0 copy-done.1
  4.9 0.0 copy-done.2
  4.9 0.0 copy-done.3
  4.9 1.2 %shard_map.85 = (bf16[2,256,384]{2,1,0:T(8,128)(2,1)S(1)}, bf16[2,672,768]{2,1,0:T(8,128)(2,1)S(1)}, bf16[192,384]{1,0:T(8,128)(2,1)S(1)}, bf16[288,512]{1,0:T(8...) custom-call(f32[2,8]{1,0:T(2,128)S(1)} %bitcast.8, ...), custom_call_target="tpu_custom_call" | custom-call | flops 1000000000 | bytes 4194304 | tf_op jit(solution)/shard_map/pallas_call | solution.py:514
  6.1 0.5 %shard_map.86.green_ref = bf16[512,768]{1,0:T(8,128)(2,1)S(1)} custom-call(bf16[256,384]{1,0:T(8,128)(2,1)S(1)} %get-tuple-element.28.fwd_ref, bf16[128,768]{1,0:T(8,128)(2,1)S(1)} %get-tuple-element.29.inv_ref, f32[128,128]{1,0:T(8,128)S(1)} %get-tuple-element.30.sr_ref, f32[128,128]{1,0:T(8,128)S(1)} %get-tuple-element.31.si_ref), custom_call_target="tpu_custom_call" | custom-call | flops 1000000000 | bytes 4194304 | tf_op jit(solution)/shard_map/pallas_call | solution.py:514
  6.7 3.6 %collective-permute-done.1.second_ref = bf16[2,4,16,128]{3,2,1,0:T(8,128)(2,1)S(1)} collective-permute-done((bf16[2,4,16,128]{3,2,1,0:T(8,128)(2,1)S(1)}, bf16[2,4,16,128]{3,2,1,0:T(8,128)(2,1)S(1)}, u32[]{:S(2)}, u32[]{:S(2)}) %collective-permute-start.1) | collective-permute-done | bytes 32800 | tf_op jit(solution)/shard_map/ppermute | solution.py:541
  10.2 0.0 collective-permute-done.first_ref
  10.2 3.5 %shard_map.87 = f32[32,4,128]{2,1,0:T(4,128)S(1)} custom-call(f32[2,8]{1,0:T(2,128)S(1)} %bitcast.9, bf16[4,5,16,128]{3,2,1,0:T(8,128)(2,1)S(1)} %collective-permute-done.first_ref, bf16[2,4,16,128]{3,2,1,0:T(8,128)(2,1)S(1)} %collective-permute-done.1.second_ref, bf16[896,128]{1,0:T(8,128)(2,1)S(1)} %get-tuple-element.20.own_feat, ...), custom_call_target="tpu_custom_call" | custom-call | flops 1000000000 | bytes 4194304 | tf_op jit(solution)/shard_map/pallas_call | solution.py:514
  13.8 9.9 %all_to_all.10.in_ref = f32[32,4,128]{2,1,0:T(4,128)S(1)} all-to-all(f32[32,4,128]{2,1,0:T(4,128)S(1)} %shard_map.87), channel_id=1, replica_groups=mesh['grp'=1,'gx'=32,'gy'=1] {'gx'}, dimensions={0} | all-to-all | bytes 131072 | tf_op jit(solution)/shard_map/all_to_all | solution.py:595
  23.7 0.5 %shard_map.88 = f32[32,4,128]{2,1,0:T(4,128)S(1)} custom-call(f32[32,4,128]{2,1,0:T(4,128)S(1)} %all_to_all.10.in_ref, bf16[512,768]{1,0:T(8,128)(2,1)S(1)} %shard_map.86.green_ref), custom_call_target="tpu_custom_call" | custom-call | flops 100000000 | bytes 4194304 | tf_op jit(solution)/shard_map/pallas_call | solution.py:514
  24.2 9.1 %all_to_all.11.in_ref = f32[32,4,128]{2,1,0:T(4,128)S(1)} all-to-all(f32[32,4,128]{2,1,0:T(4,128)S(1)} %shard_map.88), channel_id=1, replica_groups=mesh['grp'=1,'gx'=32,'gy'=1] {'gx'}, dimensions={0} | all-to-all | bytes 131072 | tf_op jit(solution)/shard_map/all_to_all | solution.py:602
  33.3 1.0 %shard_map.89 = f32[2,16,4,128]{3,2,1,0:T(4,128)} custom-call(f32[32,4,128]{2,1,0:T(4,128)S(1)} %all_to_all.11.in_ref, bf16[384,256]{1,0:T(8,128)(2,1)S(1)} %get-tuple-element.32.back_ref, f32[2,16,4,128]{3,2,1,0:T(4,128)S(1)} %copy-done), custom_call_target="tpu_custom_call" | custom-call | flops 100000000 | bytes 4194304 | tf_op jit(solution)/shard_map/pallas_call | solution.py:514
  (5 shorter events, 0.0 us)
Async XLA Ops:
  0.9 4.0 %copy-start.1 = (f32[8,2]{0,1:T(2,128)S(1)}, f32[8,2]{0,1:T(2,128)}, u32[]{:S(2)}) copy-start(f32[8,2]{0,1:T(2,128)} %param.10) | copy-start | bytes 196
  0.9 4.0 %copy-start.2 = (bf16[32,32,3,3,3]{1,0,4,3,2:T(8,128)(2,1)S(1)}, bf16[32,32,3,3,3]{1,0,4,3,2:T(8,128)(2,1)}, u32[]{:S(2)}) copy-start(bf16[32,32,3,3,3]{1,0,4,3,2:T(8,128)(2,1)} %param.12) | copy-start | bytes 165892
  0.9 4.0 %copy-start.3 = (bf16[32,4,3,3,3]{0,1,4,3,2:T(4,128)(2,1)S(1)}, bf16[32,4,3,3,3]{0,1,4,3,2:T(4,128)(2,1)}, u32[]{:S(2)}) copy-start(bf16[32,4,3,3,3]{0,1,4,3,2:T(4,128)(2,1)} %param.11) | copy-start | bytes 20740
  0.9 4.0 %copy-start.4 = (f32[2,16,16]{2,1,0:T(8,128)S(1)}, f32[2,16,16]{2,1,0:T(8,128)}, u32[]{:S(2)}) copy-start(f32[2,16,16]{2,1,0:T(8,128)} %zk_ref.1) | copy-start | bytes 6148
  0.9 4.0 %copy-start.5 = (bf16[2,32,3,3,3]{1,0,4,3,2:T(2,128)(2,1)S(1)}, bf16[2,32,3,3,3]{1,0,4,3,2:T(2,128)(2,1)}, u32[]{:S(2)}) copy-start(bf16[2,32,3,3,3]{1,0,4,3,2:T(2,128)(2,1)} %param.13) | copy-start | bytes 10372
  0.9 4.0 %copy-start.6 = (f32[2,4,128]{2,1,0:T(4,128)S(1)}, f32[2,4,128]{2,1,0:T(4,128)}, u32[]{:S(2)}) copy-start(f32[2,4,128]{2,1,0:T(4,128)} %sp_ref.1) | copy-start | bytes 12292
  1.1 9.1 %collective-permute-start = (bf16[4,5,16,128]{3,2,1,0:T(8,128)(2,1)S(1)}, bf16[4,5,16,128]{3,2,1,0:T(8,128)(2,1)S(1)}, u32[]{:S(2)}, u32[]{:S(2)}) collective-permute-start(bf16[4,5,16,128]{3,2,1,0:T(8,128)(2,1)S(1)} %shard_map.82.whole_ref), channel_id=1, source_target_pairs={{0,1},{1,2},{2,3},{3,4},{4,5},{5,6},{6,7},{7,8},{8,9},{9,10},{10,1... | collective-permute-start | bytes 245768 | tf_op jit(solution)/shard_map/ppermute | solution.py:537
  1.8 8.4 %collective-permute-start.1 = (bf16[2,4,16,128]{3,2,1,0:T(8,128)(2,1)S(1)}, bf16[2,4,16,128]{3,2,1,0:T(8,128)(2,1)S(1)}, u32[]{:S(2)}, u32[]{:S(2)}) collective-permute-start(bf16[2,4,16,128]{3,2,1,0:T(8,128)(2,1)S(1)} %shard_map.83), channel_id=1, source_target_pairs={{0,2},{1,3},{2,4},{3,5},{4,6},{5,7},{6,8},{7,9},{8,10},{9,11},{10,... | collective-permute-start | bytes 98312 | tf_op jit(solution)/shard_map/ppermute | solution.py:541
  10.2 23.1 %copy-start = (f32[2,16,4,128]{3,2,1,0:T(4,128)S(1)}, f32[2,16,4,128]{3,2,1,0:T(4,128)}, u32[]{:S(2)}) copy-start(f32[2,16,4,128]{3,2,1,0:T(4,128)} %inc_ref.1) | copy-start | bytes 196612

commit v11 on v10

--- a/solution.py
+++ b/solution.py
@@ -205,15 +205,6 @@
         chi_re = jnp.where(here, class_re, chi_re)
         chi_im = jnp.where(here, class_im, chi_im)
     return [high_re, high_im, chi_re * re - chi_im * im, chi_re * im + chi_im * re]
-
-
-def pack_kernel(own_ref, whole_ref):
-    for x in range(own_ref.shape[2]):
-        for i in range(3):
-            high, low = split(own_ref[i, :, x, :])
-            whole_ref[x, i] = high
-            if i < 2:
-                whole_ref[x, i + 3] = low
 
 
 def near_kernel(class_count, own_ref, whole_ref, near_ref):
@@ -503,7 +494,7 @@
 def finish_kernel(nz, in_ref, back_ref, inc_ref, out_ref):
     values = jnp.transpose(swap_blocks(in_ref, in_ref.shape[1]))
     blocks = mixed(mm(left_split(values), back_ref[...]), nz, -1.0)
-    for x in range(inc_ref.shape[2]):
+    for x in range(out_ref.shape[2]):
         for part in range(2):
             out_ref[part, :, x, :] = inc_ref[part, :, x, :] + blocks[2 * x + part]
 
@@ -533,7 +524,12 @@
     own = jnp.pad(material[None], ((2, 1),) + still).astype(F32) + jnp.pad(incident, ((0, 2),) + still)
     parts, kinds = classes.shape
     own += jnp.pad(classes[None, None], ((3, 0), (0, nz - 1), (0, xl - parts), (0, ny - kinds)))
-    whole = call(pack_kernel, struct((xl, 5, nz, ny), BF16), (own,), flops=10**6)
+    planes = jnp.transpose(own, (2, 0, 1, 3))[:, :3]
+    again = jnp.pad(planes, ((0, 0), (0, 2), (0, 0), (0, 0)))
+    again += jnp.pad(planes[:, :2], ((0, 0), (3, 0), (0, 0), (0, 0)))
+    high = lax.reduce_precision(again, 8, 7)
+    later = lax.broadcasted_iota(jnp.int32, (1, 5, 1, 1), 1) > 2
+    whole = jnp.where(later, again - high, high).astype(BF16)
     first = lax.ppermute(whole, "gx", [(i, (i + 1) % count) for i in range(count)])
     near = call(
         functools.partial(near_kernel, kinds), struct((2, 4, nz, ny), BF16), (own, whole), flops=10**6
@@ -603,7 +599,7 @@
     return call(
         functools.partial(finish_kernel, nz),
         struct(incident.shape, F32),
-        (rows, back, incident),
+        (rows, back, own),
         flops=10**8,
     )
 

time: 34.5 us -> 34.5 us (level)
    ppermute x1, waiting for transfers between devices: 3.56 us -> 0.53 us  [lane_device(): lax.ppermute(near, 'gx', [(i, (i + 2) % count) for i in range(count)])]
    ppermute x1, waiting for transfers between devices: 0.01 us -> 3.01 us  [lane_device(): lax.ppermute(whole, 'gx', [(i, (i + 1) % count) for i in range(count)])]
    pallas_call x8 -> x7, Pallas kernels: 7.65 us -> 7.45 us  [call(): pl.pallas_call(kernel, out_shape=out_shapes, in_specs=[vmem] * len(args),...]
  transfers between devices with their start and end apart: 2 -> 2, of which waited for: 1 -> 2; matrix products, arithmetic and copies ran while one was open for 0% -> 0% of each run, Pallas kernels for 7% -> 7%
where the time goes in v11:
time: 34.5 us; the launch traced here: 34.3 us
  blocking collectives  19 us (55%)
  Pallas kernels  7.45 us (22%)
  waiting for transfers between devices  3.54 us (10%)
  starting transfers between devices  3.06 us (9%)
  other arithmetic  0.98 us (3%)
    all_to_all x1, blocking collectives, lane_device(): piece = lax.all_to_all(spectrum, 'gx', 0, 0, tiled=True)  9.92 us
    all_to_all x1, blocking collectives, lane_device(): rows = lax.all_to_all(spread, 'gx', 0, 0, tiled=True)  9.1 us
    pallas_call x7, Pallas kernels, call(): pl.pallas_call(kernel, out_shape=out_shapes, in_specs=[vmem] * len(args),...  7.45 us
    ppermute x1, waiting for transfers between devices, lane_device(): lax.ppermute(whole, 'gx', [(i, (i + 1) % count) for i in range(count)])  3.01 us
    ppermute x1, starting transfers between devices, lane_device(): lax.ppermute(near, 'gx', [(i, (i + 2) % count) for i in range(count)])  2.56 us
    add x1, other arithmetic, lane_device(): own += jnp.pad(classes[None, None], ((3, 0), (0, nz - 1), (0, xl - parts)...  0.87 us
  transfers between devices with their start and end apart: 2, of which 2 were waited for; matrix products, arithmetic and copies ran while one was open for 0% of the time, Pallas kernels for 7%

profile of v11, /device:TPU:0, one launch (start us, length us, event | category | flops | bytes accessed | tf_op | source)
XLA Modules:
  0.0 34.3 jit_solution(12077173178271720402)
XLA Ops:
  0.0 0.9 %pad_add_fusion = (f32[4,16,4,128]{3,2,1,0:T(4,128)S(1)}, f32[4,4,16,128]{3,0,2,1:T(4,128)S(1)}) fusion(f32[1,1,2,8]{3,2,1,0:T(2,128)} %bitcast.9, f32[2,16,4,128]{3,2,1,0:T(4,128)} %param.8, s32[1,16,4,128]{3,2,1,0:T(4,128)} %bitcast.15), kind=kLoop, calls=%fused_computation.2 | loop fusion | flops 98304 | bytes 360512 | tf_op jit(solution)/shard_map/add | solution.py:526
  0.9 0.1 fusion
  1.0 0.0 copy-start
  1.0 0.0 copy-start.1
  1.0 0.0 copy-start.2
  1.1 0.0 copy-start.3
  1.1 0.0 copy-start.4
  1.1 0.0 copy-start.5
  1.1 0.5 %collective-permute-start = (bf16[4,5,16,128]{3,0,2,1:T(4,128)(2,1)S(1)}, bf16[4,5,16,128]{3,0,2,1:T(4,128)(2,1)S(1)}, u32[]{:S(2)}, u32[]{:S(2)}) collective-permute-start(bf16[4,5,16,128]{3,0,2,1:T(4,128)(2,1)S(1)} %fusion), channel_id=1, source_target_pairs={{0,1},{1,2},{2,3},{3,4},{4,5},{5,6},{6,7},{7,8},{8,9},{9,10},{10,1... | collective-permute-start | bytes 245768 | tf_op jit(solution)/shard_map/ppermute | solution.py:533
  1.6 0.1 shard_map.82
  1.7 2.6 %collective-permute-start.1 = (bf16[2,4,16,128]{3,2,1,0:T(8,128)(2,1)S(1)}, bf16[2,4,16,128]{3,2,1,0:T(8,128)(2,1)S(1)}, u32[]{:S(2)}, u32[]{:S(2)}) collective-permute-start(bf16[2,4,16,128]{3,2,1,0:T(8,128)(2,1)S(1)} %shard_map.82), channel_id=1, source_target_pairs={{0,2},{1,3},{2,4},{3,5},{4,6},{5,7},{6,8},{7,9},{8,10},{9,11},{10,... | collective-permute-start | bytes 98312 | tf_op jit(solution)/shard_map/ppermute | solution.py:537
  4.3 0.6 %shard_map.83 = (bf16[384,256]{1,0:T(8,128)(2,1)S(1)}, bf16[256,384]{1,0:T(8,128)(2,1)S(1)}, bf16[128,768]{1,0:T(8,128)(2,1)S(1)}, bf16[384,256]{1,0:T(8,128)(2,1)S(1)}) custom-call(), custom_call_target="tpu_custom_call" | custom-call | flops 1000000000 | bytes 4194304 | tf_op jit(solution)/shard_map/pallas_call | solution.py:505
  4.9 0.0 copy-done
  4.9 0.0 copy-done.1
  4.9 0.0 copy-done.2
  4.9 1.2 %shard_map.84 = (bf16[2,256,384]{2,1,0:T(8,128)(2,1)S(1)}, bf16[2,672,768]{2,1,0:T(8,128)(2,1)S(1)}, bf16[192,384]{1,0:T(8,128)(2,1)S(1)}, bf16[288,512]{1,0:T(8...) custom-call(f32[2,8]{1,0:T(2,128)S(1)} %bitcast.10, ...), custom_call_target="tpu_custom_call" | custom-call | flops 1000000000 | bytes 4194304 | tf_op jit(solution)/shard_map/pallas_call | solution.py:505
  6.1 0.5 %shard_map.85.green_ref = bf16[512,768]{1,0:T(8,128)(2,1)S(1)} custom-call(bf16[256,384]{1,0:T(8,128)(2,1)S(1)} %get-tuple-element.28.fwd_ref, bf16[128,768]{1,0:T(8,128)(2,1)S(1)} %get-tuple-element.29.inv_ref, f32[128,128]{1,0:T(8,128)S(1)} %get-tuple-element.30.sr_ref, f32[128,128]{1,0:T(8,128)S(1)} %get-tuple-element.31.si_ref), custom_call_target="tpu_custom_call" | custom-call | flops 1000000000 | bytes 4194304 | tf_op jit(solution)/shard_map/pallas_call | solution.py:505
  6.6 3.0 %collective-permute-done = bf16[4,5,16,128]{3,0,2,1:T(4,128)(2,1)S(1)} collective-permute-done((bf16[4,5,16,128]{3,0,2,1:T(4,128)(2,1)S(1)}, bf16[4,5,16,128]{3,0,2,1:T(4,128)(2,1)S(1)}, u32[]{:S(2)}, u32[]{:S(2)}) %collective-permute-start) | collective-permute-done | bytes 81952 | tf_op jit(solution)/shard_map/ppermute | solution.py:533
  9.7 0.5 %collective-permute-done.1.second_ref = bf16[2,4,16,128]{3,2,1,0:T(8,128)(2,1)S(1)} collective-permute-done((bf16[2,4,16,128]{3,2,1,0:T(8,128)(2,1)S(1)}, bf16[2,4,16,128]{3,2,1,0:T(8,128)(2,1)S(1)}, u32[]{:S(2)}, u32[]{:S(2)}) %collective-permute-start.1) | collective-permute-done | bytes 32800 | tf_op jit(solution)/shard_map/ppermute | solution.py:537
  10.2 3.5 %shard_map.86 = f32[32,4,128]{2,1,0:T(4,128)S(1)} custom-call(f32[2,8]{1,0:T(2,128)S(1)} %bitcast.11, bf16[4,5,16,128]{3,2,1,0:T(8,128)(2,1)S(1)} %copy.11.first_ref, bf16[2,4,16,128]{3,2,1,0:T(8,128)(2,1)S(1)} %collective-permute-done.1.second_ref, bf16[896,128]{1,0:T(8,128)(2,1)S(1)} %get-tuple-element.20.own_feat, ...), custom_call_target="tpu_custom_call" | custom-call | flops 1000000000 | bytes 4194304 | tf_op jit(solution)/shard_map/pallas_call | solution.py:505
  13.7 9.9 %all_to_all.10.in_ref = f32[32,4,128]{2,1,0:T(4,128)S(1)} all-to-all(f32[32,4,128]{2,1,0:T(4,128)S(1)} %shard_map.86), channel_id=1, replica_groups=mesh['grp'=1,'gx'=32,'gy'=1] {'gx'}, dimensions={0} | all-to-all | bytes 131072 | tf_op jit(solution)/shard_map/all_to_all | solution.py:591
  23.7 0.5 %shard_map.87 = f32[32,4,128]{2,1,0:T(4,128)S(1)} custom-call(f32[32,4,128]{2,1,0:T(4,128)S(1)} %all_to_all.10.in_ref, bf16[512,768]{1,0:T(8,128)(2,1)S(1)} %shard_map.85.green_ref), custom_call_target="tpu_custom_call" | custom-call | flops 100000000 | bytes 4194304 | tf_op jit(solution)/shard_map/pallas_call | solution.py:505
  24.2 9.1 %all_to_all.11.in_ref = f32[32,4,128]{2,1,0:T(4,128)S(1)} all-to-all(f32[32,4,128]{2,1,0:T(4,128)S(1)} %shard_map.87), channel_id=1, replica_groups=mesh['grp'=1,'gx'=32,'gy'=1] {'gx'}, dimensions={0} | all-to-all | bytes 131072 | tf_op jit(solution)/shard_map/all_to_all | solution.py:598
  33.3 1.0 %shard_map.88 = f32[2,16,4,128]{3,2,1,0:T(4,128)} custom-call(f32[32,4,128]{2,1,0:T(4,128)S(1)} %all_to_all.11.in_ref, bf16[384,256]{1,0:T(8,128)(2,1)S(1)} %get-tuple-element.32.back_ref, f32[4,16,4,128]{3,2,1,0:T(4,128)S(1)} %get-tuple-element.33.own_ref.inc_ref), custom_call_target="tpu_custom_call" | custom-call | flops 100000000 | bytes 4194304 | tf_op jit(solution)/shard_map/pallas_call | solution.py:505
  (8 shorter events, 0.1 us)
Async XLA Ops:
  1.0 3.8 %copy-start = (f32[8,2]{0,1:T(2,128)S(1)}, f32[8,2]{0,1:T(2,128)}, u32[]{:S(2)}) copy-start(f32[8,2]{0,1:T(2,128)} %param.10) | copy-start | bytes 196
  1.0 3.8 %copy-start.1 = (bf16[32,32,3,3,3]{1,0,4,3,2:T(8,128)(2,1)S(1)}, bf16[32,32,3,3,3]{1,0,4,3,2:T(8,128)(2,1)}, u32[]{:S(2)}) copy-start(bf16[32,32,3,3,3]{1,0,4,3,2:T(8,128)(2,1)} %param.12) | copy-start | bytes 165892
  1.0 3.8 %copy-start.2 = (bf16[32,4,3,3,3]{0,1,4,3,2:T(4,128)(2,1)S(1)}, bf16[32,4,3,3,3]{0,1,4,3,2:T(4,128)(2,1)}, u32[]{:S(2)}) copy-start(bf16[32,4,3,3,3]{0,1,4,3,2:T(4,128)(2,1)} %param.11) | copy-start | bytes 20740
  1.1 3.8 %copy-start.3 = (f32[2,16,16]{2,1,0:T(8,128)S(1)}, f32[2,16,16]{2,1,0:T(8,128)}, u32[]{:S(2)}) copy-start(f32[2,16,16]{2,1,0:T(8,128)} %zk_ref.1) | copy-start | bytes 6148
  1.1 3.8 %copy-start.4 = (bf16[2,32,3,3,3]{1,0,4,3,2:T(2,128)(2,1)S(1)}, bf16[2,32,3,3,3]{1,0,4,3,2:T(2,128)(2,1)}, u32[]{:S(2)}) copy-start(bf16[2,32,3,3,3]{1,0,4,3,2:T(2,128)(2,1)} %param.13) | copy-start | bytes 10372
  1.1 3.8 %copy-start.5 = (f32[2,4,128]{2,1,0:T(4,128)S(1)}, f32[2,4,128]{2,1,0:T(4,128)}, u32[]{:S(2)}) copy-start(f32[2,4,128]{2,1,0:T(4,128)} %sp_ref.1) | copy-start | bytes 12292
  1.1 8.6 %collective-permute-start = (bf16[4,5,16,128]{3,0,2,1:T(4,128)(2,1)S(1)}, bf16[4,5,16,128]{3,0,2,1:T(4,128)(2,1)S(1)}, u32[]{:S(2)}, u32[]{:S(2)}) collective-permute-start(bf16[4,5,16,128]{3,0,2,1:T(4,128)(2,1)S(1)} %fusion), channel_id=1, source_target_pairs={{0,1},{1,2},{2,3},{3,4},{4,5},{5,6},{6,7},{7,8},{8,9},{9,10},{10,1... | collective-permute-start | bytes 245768 | tf_op jit(solution)/shard_map/ppermute | solution.py:533
  1.7 8.4 %collective-permute-start.1 = (bf16[2,4,16,128]{3,2,1,0:T(8,128)(2,1)S(1)}, bf16[2,4,16,128]{3,2,1,0:T(8,128)(2,1)S(1)}, u32[]{:S(2)}, u32[]{:S(2)}) collective-permute-start(bf16[2,4,16,128]{3,2,1,0:T(8,128)(2,1)S(1)} %shard_map.82), channel_id=1, source_target_pairs={{0,2},{1,3},{2,4},{3,5},{4,6},{5,7},{6,8},{7,9},{8,10},{9,11},{10,... | collective-permute-start | bytes 98312 | tf_op jit(solution)/shard_map/ppermute | solution.py:537

commit v12 on v11

--- a/solution.py
+++ b/solution.py
@@ -402,12 +402,12 @@
 
     def tap_sum(weights, top, bottom, j):
         window = [
-            jnp.concatenate([hidden(j + b + i, top, bottom) for i in range(2)], axis=1) for b in range(3)
+            jnp.concatenate([hidden(j + b + i, top, bottom) for i in range(ahead)], axis=1) for b in range(3)
         ]
         made = mm(weights, jnp.concatenate(window, axis=0))
         rows = weights.shape[0] // 3
         sides = []
-        for i in range(2):
+        for i in range(ahead):
             lanes = slice(i * ny, (i + 1) * ny)
             sides.append(
                 pltpu.roll(made[:rows, lanes], 1, 1)
@@ -424,7 +424,7 @@
         ]
 
     def second_done(j, made):
-        lanes = slice(j * ny, (j + 2) * ny)
+        lanes = slice(j * ny, (j + ahead) * ny)
         for top, part in zip((0, tall, tall + 2 * hid), made):
             hid2[top : top + part.shape[0], lanes] = gelu(part).astype(BF16)
 
@@ -450,16 +450,13 @@
         return jnp.concatenate(mixed(made, nz, 1.0), axis=0)
 
     own[xl - 1] = own_pol[...]
-    pairs = range(ahead - 2, -1, -2)
-    for j in pairs:
-        features(j)
-        features(j + 1)
-    for j in pairs:
-        first_done(j, first_layer(j))
-    for j in pairs:
-        second_done(j, second_layer(j))
-    for j in pairs:
-        third_layer(j)
+    for place in range(ahead):
+        features(place)
+    hid1[...] = gelu(first_product(t1_ref, feature_rows, range(ahead))).astype(BF16)
+    second_done(0, second_layer(0))
+    made = mm(t3_ref[...], hid2[...])
+    for x in range(ahead):
+        last[x] = made[:, x * ny : (x + 1) * ny]
     out_ref[...] = jnp.transpose(transformed(range(xl))).reshape(out_ref.shape)
 
 

time: 34.5 us -> 34.4 us (level)
  no operation moved by 1% of the time
where the time goes in v12:
time: 34.4 us; the launch traced here: 34.2 us
  blocking collectives  19 us (55%)
  Pallas kernels  7.4 us (22%)
  waiting for transfers between devices  3.54 us (10%)
  starting transfers between devices  3.06 us (9%)
  other arithmetic  0.98 us (3%)
    all_to_all x1, blocking collectives, lane_device(): piece = lax.all_to_all(spectrum, 'gx', 0, 0, tiled=True)  9.91 us
    all_to_all x1, blocking collectives, lane_device(): rows = lax.all_to_all(spread, 'gx', 0, 0, tiled=True)  9.1 us
    pallas_call x7, Pallas kernels, call(): pl.pallas_call(kernel, out_shape=out_shapes, in_specs=[vmem] * len(args),...  7.4 us
    ppermute x1, waiting for transfers between devices, lane_device(): lax.ppermute(whole, 'gx', [(i, (i + 1) % count) for i in range(count)])  3.01 us
    ppermute x1, starting transfers between devices, lane_device(): lax.ppermute(near, 'gx', [(i, (i + 2) % count) for i in range(count)])  2.56 us
    add x1, other arithmetic, lane_device(): own += jnp.pad(classes[None, None], ((3, 0), (0, nz - 1), (0, xl - parts)...  0.87 us
  transfers between devices with their start and end apart: 2, of which 2 were waited for; matrix products, arithmetic and copies ran while one was open for 0% of the time, Pallas kernels for 7%

profile of v12, /device:TPU:0, one launch (start us, length us, event | category | flops | bytes accessed | tf_op | source)
XLA Modules:
  0.0 34.2 jit_solution(5641915712989930554)
XLA Ops:
  0.0 0.9 %pad_add_fusion = (f32[4,16,4,128]{3,2,1,0:T(4,128)S(1)}, f32[4,4,16,128]{3,0,2,1:T(4,128)S(1)}) fusion(f32[1,1,2,8]{3,2,1,0:T(2,128)} %bitcast.9, f32[2,16,4,128]{3,2,1,0:T(4,128)} %param.8, s32[1,16,4,128]{3,2,1,0:T(4,128)} %bitcast.15), kind=kLoop, calls=%fused_computation.2 | loop fusion | flops 98304 | bytes 360512 | tf_op jit(solution)/shard_map/add | solution.py:523
  0.9 0.1 fusion
  1.0 0.0 copy-start
  1.0 0.0 copy-start.1
  1.0 0.0 copy-start.2
  1.1 0.0 copy-start.3
  1.1 0.0 copy-start.4
  1.1 0.0 copy-start.5
  1.1 0.5 %collective-permute-start = (bf16[4,5,16,128]{3,0,2,1:T(4,128)(2,1)S(1)}, bf16[4,5,16,128]{3,0,2,1:T(4,128)(2,1)S(1)}, u32[]{:S(2)}, u32[]{:S(2)}) collective-permute-start(bf16[4,5,16,128]{3,0,2,1:T(4,128)(2,1)S(1)} %fusion), channel_id=1, source_target_pairs={{0,1},{1,2},{2,3},{3,4},{4,5},{5,6},{6,7},{7,8},{8,9},{9,10},{10,1... | collective-permute-start | bytes 245768 | tf_op jit(solution)/shard_map/ppermute | solution.py:530
  1.6 0.1 shard_map.82
  1.7 2.6 %collective-permute-start.1 = (bf16[2,4,16,128]{3,2,1,0:T(8,128)(2,1)S(1)}, bf16[2,4,16,128]{3,2,1,0:T(8,128)(2,1)S(1)}, u32[]{:S(2)}, u32[]{:S(2)}) collective-permute-start(bf16[2,4,16,128]{3,2,1,0:T(8,128)(2,1)S(1)} %shard_map.82), channel_id=1, source_target_pairs={{0,2},{1,3},{2,4},{3,5},{4,6},{5,7},{6,8},{7,9},{8,10},{9,11},{10,... | collective-permute-start | bytes 98312 | tf_op jit(solution)/shard_map/ppermute | solution.py:534
  4.3 0.6 %shard_map.83 = (bf16[384,256]{1,0:T(8,128)(2,1)S(1)}, bf16[256,384]{1,0:T(8,128)(2,1)S(1)}, bf16[128,768]{1,0:T(8,128)(2,1)S(1)}, bf16[384,256]{1,0:T(8,128)(2,1)S(1)}) custom-call(), custom_call_target="tpu_custom_call" | custom-call | flops 1000000000 | bytes 4194304 | tf_op jit(solution)/shard_map/pallas_call | solution.py:502
  4.9 0.0 copy-done
  4.9 0.0 copy-done.1
  4.9 0.0 copy-done.2
  4.9 1.2 %shard_map.84 = (bf16[2,256,384]{2,1,0:T(8,128)(2,1)S(1)}, bf16[2,672,768]{2,1,0:T(8,128)(2,1)S(1)}, bf16[192,384]{1,0:T(8,128)(2,1)S(1)}, bf16[288,512]{1,0:T(8...) custom-call(f32[2,8]{1,0:T(2,128)S(1)} %bitcast.10, ...), custom_call_target="tpu_custom_call" | custom-call | flops 1000000000 | bytes 4194304 | tf_op jit(solution)/shard_map/pallas_call | solution.py:502
  6.1 0.5 %shard_map.85.green_ref = bf16[512,768]{1,0:T(8,128)(2,1)S(1)} custom-call(bf16[256,384]{1,0:T(8,128)(2,1)S(1)} %get-tuple-element.28.fwd_ref, bf16[128,768]{1,0:T(8,128)(2,1)S(1)} %get-tuple-element.29.inv_ref, f32[128,128]{1,0:T(8,128)S(1)} %get-tuple-element.30.sr_ref, f32[128,128]{1,0:T(8,128)S(1)} %get-tuple-element.31.si_ref), custom_call_target="tpu_custom_call" | custom-call | flops 1000000000 | bytes 4194304 | tf_op jit(solution)/shard_map/pallas_call | solution.py:502
  6.6 3.0 %collective-permute-done = bf16[4,5,16,128]{3,0,2,1:T(4,128)(2,1)S(1)} collective-permute-done((bf16[4,5,16,128]{3,0,2,1:T(4,128)(2,1)S(1)}, bf16[4,5,16,128]{3,0,2,1:T(4,128)(2,1)S(1)}, u32[]{:S(2)}, u32[]{:S(2)}) %collective-permute-start) | collective-permute-done | bytes 81952 | tf_op jit(solution)/shard_map/ppermute | solution.py:530
  9.7 0.5 %collective-permute-done.1.second_ref = bf16[2,4,16,128]{3,2,1,0:T(8,128)(2,1)S(1)} collective-permute-done((bf16[2,4,16,128]{3,2,1,0:T(8,128)(2,1)S(1)}, bf16[2,4,16,128]{3,2,1,0:T(8,128)(2,1)S(1)}, u32[]{:S(2)}, u32[]{:S(2)}) %collective-permute-start.1) | collective-permute-done | bytes 32800 | tf_op jit(solution)/shard_map/ppermute | solution.py:534
  10.2 3.5 %shard_map.86 = f32[32,4,128]{2,1,0:T(4,128)S(1)} custom-call(f32[2,8]{1,0:T(2,128)S(1)} %bitcast.11, bf16[4,5,16,128]{3,2,1,0:T(8,128)(2,1)S(1)} %copy.11.first_ref, bf16[2,4,16,128]{3,2,1,0:T(8,128)(2,1)S(1)} %collective-permute-done.1.second_ref, bf16[896,128]{1,0:T(8,128)(2,1)S(1)} %get-tuple-element.20.own_feat, ...), custom_call_target="tpu_custom_call" | custom-call | flops 1000000000 | bytes 4194304 | tf_op jit(solution)/shard_map/pallas_call | solution.py:502
  13.7 9.9 %all_to_all.10.in_ref = f32[32,4,128]{2,1,0:T(4,128)S(1)} all-to-all(f32[32,4,128]{2,1,0:T(4,128)S(1)} %shard_map.86), channel_id=1, replica_groups=mesh['grp'=1,'gx'=32,'gy'=1] {'gx'}, dimensions={0} | all-to-all | bytes 131072 | tf_op jit(solution)/shard_map/all_to_all | solution.py:588
  23.6 0.5 %shard_map.87 = f32[32,4,128]{2,1,0:T(4,128)S(1)} custom-call(f32[32,4,128]{2,1,0:T(4,128)S(1)} %all_to_all.10.in_ref, bf16[512,768]{1,0:T(8,128)(2,1)S(1)} %shard_map.85.green_ref), custom_call_target="tpu_custom_call" | custom-call | flops 100000000 | bytes 4194304 | tf_op jit(solution)/shard_map/pallas_call | solution.py:502
  24.2 9.1 %all_to_all.11.in_ref = f32[32,4,128]{2,1,0:T(4,128)S(1)} all-to-all(f32[32,4,128]{2,1,0:T(4,128)S(1)} %shard_map.87), channel_id=1, replica_groups=mesh['grp'=1,'gx'=32,'gy'=1] {'gx'}, dimensions={0} | all-to-all | bytes 131072 | tf_op jit(solution)/shard_map/all_to_all | solution.py:595
  33.3 1.0 %shard_map.88 = f32[2,16,4,128]{3,2,1,0:T(4,128)} custom-call(f32[32,4,128]{2,1,0:T(4,128)S(1)} %all_to_all.11.in_ref, bf16[384,256]{1,0:T(8,128)(2,1)S(1)} %get-tuple-element.32.back_ref, f32[4,16,4,128]{3,2,1,0:T(4,128)S(1)} %get-tuple-element.33.own_ref.inc_ref), custom_call_target="tpu_custom_call" | custom-call | flops 100000000 | bytes 4194304 | tf_op jit(solution)/shard_map/pallas_call | solution.py:502
  (8 shorter events, 0.1 us)
Async XLA Ops:
  1.0 3.8 %copy-start = (f32[8,2]{0,1:T(2,128)S(1)}, f32[8,2]{0,1:T(2,128)}, u32[]{:S(2)}) copy-start(f32[8,2]{0,1:T(2,128)} %param.10) | copy-start | bytes 196
  1.0 3.8 %copy-start.1 = (bf16[32,32,3,3,3]{1,0,4,3,2:T(8,128)(2,1)S(1)}, bf16[32,32,3,3,3]{1,0,4,3,2:T(8,128)(2,1)}, u32[]{:S(2)}) copy-start(bf16[32,32,3,3,3]{1,0,4,3,2:T(8,128)(2,1)} %param.12) | copy-start | bytes 165892
  1.0 3.8 %copy-start.2 = (bf16[32,4,3,3,3]{0,1,4,3,2:T(4,128)(2,1)S(1)}, bf16[32,4,3,3,3]{0,1,4,3,2:T(4,128)(2,1)}, u32[]{:S(2)}) copy-start(bf16[32,4,3,3,3]{0,1,4,3,2:T(4,128)(2,1)} %param.11) | copy-start | bytes 20740
  1.1 3.8 %copy-start.3 = (f32[2,16,16]{2,1,0:T(8,128)S(1)}, f32[2,16,16]{2,1,0:T(8,128)}, u32[]{:S(2)}) copy-start(f32[2,16,16]{2,1,0:T(8,128)} %zk_ref.1) | copy-start | bytes 6148
  1.1 3.8 %copy-start.4 = (bf16[2,32,3,3,3]{1,0,4,3,2:T(2,128)(2,1)S(1)}, bf16[2,32,3,3,3]{1,0,4,3,2:T(2,128)(2,1)}, u32[]{:S(2)}) copy-start(bf16[2,32,3,3,3]{1,0,4,3,2:T(2,128)(2,1)} %param.13) | copy-start | bytes 10372
  1.1 3.8 %copy-start.5 = (f32[2,4,128]{2,1,0:T(4,128)S(1)}, f32[2,4,128]{2,1,0:T(4,128)}, u32[]{:S(2)}) copy-start(f32[2,4,128]{2,1,0:T(4,128)} %sp_ref.1) | copy-start | bytes 12292
  1.1 8.6 %collective-permute-start = (bf16[4,5,16,128]{3,0,2,1:T(4,128)(2,1)S(1)}, bf16[4,5,16,128]{3,0,2,1:T(4,128)(2,1)S(1)}, u32[]{:S(2)}, u32[]{:S(2)}) collective-permute-start(bf16[4,5,16,128]{3,0,2,1:T(4,128)(2,1)S(1)} %fusion), channel_id=1, source_target_pairs={{0,1},{1,2},{2,3},{3,4},{4,5},{5,6},{6,7},{7,8},{8,9},{9,10},{10,1... | collective-permute-start | bytes 245768 | tf_op jit(solution)/shard_map/ppermute | solution.py:530
  1.7 8.4 %collective-permute-start.1 = (bf16[2,4,16,128]{3,2,1,0:T(8,128)(2,1)S(1)}, bf16[2,4,16,128]{3,2,1,0:T(8,128)(2,1)S(1)}, u32[]{:S(2)}, u32[]{:S(2)}) collective-permute-start(bf16[2,4,16,128]{3,2,1,0:T(8,128)(2,1)S(1)} %shard_map.82), channel_id=1, source_target_pairs={{0,2},{1,3},{2,4},{3,5},{4,6},{5,7},{6,8},{7,9},{8,10},{9,11},{10,... | collective-permute-start | bytes 98312 | tf_op jit(solution)/shard_map/ppermute | solution.py:534
